TPU v7x, 128 devices: a whole 4x4x4 slice. The times are simulated.
128 devices in a mesh: row: 8 (over y_lo, z), col: 16 (over x, y_hi, core).
Axes of the slice: x: 4, y: 4 (y_hi: 2, y_lo: 2; y = y_hi * 2 + y_lo), z: 4, core: 2. Of those that a mesh axis runs over, the one named last changes fastest.
Arguments:
- carried_sum: float32 [7680, 28672], P('row', 'col'), may hold values from -6 to 6
- x_panels: bfloat16 [7680, 4096], P('row', 'col'), may hold values from -6 to 6
- w_panels: bfloat16 [4096, 28672], P('row', 'col'), may hold values from -0.0625 to 0.0625
- cotangent: bfloat16 [7680, 28672], P('row', 'col'), may hold values from -6 to 6
Outputs:
- activated: bfloat16 [7680, 28672], P('row', 'col')
- input_grad: bfloat16 [7680, 4096], P('row', 'col')
All inputs are finite; a program needn't handle non-finite values.
Results may differ from a plain program's by a relative error of at most 0.017.
Values may be sent and summed in bfloat16 or wider, within the bound.
No kernel may reach another device: no remote copies, remote signals or barrier semaphores. Data moves between devices by JAX's collectives and lax.ppermute only.
A program may use at most 128 MiB of HBM per device.

v0:
```python
import jax
import jax.numpy as jnp
from jax import lax
from jax.sharding import PartitionSpec as P

inv_root_two = 0.7071067811865476
inv_root_tau = 0.3989422804014327


def body(carried_sum, x_panels, w_panels, cotangent):
    x_whole = lax.all_gather(x_panels, "col", axis=1, tiled=True)
    preact = carried_sum + jnp.dot(
        x_whole,
        lax.all_gather(w_panels, "row", axis=0, tiled=True),
        preferred_element_type=jnp.float32,
    )
    normal_cdf = 0.5 * (1.0 + jax.scipy.special.erf(preact * inv_root_two))
    normal_pdf = jnp.exp(-0.5 * preact * preact) * inv_root_tau
    activated = (preact * normal_cdf).astype(jnp.bfloat16)
    slope_grad = (cotangent.astype(jnp.float32) * (normal_cdf + preact * normal_pdf)).astype(
        jnp.bfloat16
    )
    partial_grad = lax.dot_general(
        slope_grad,
        lax.all_gather(w_panels, "row", axis=0, tiled=True),
        (((1,), (1,)), ((), ())),
        preferred_element_type=jnp.float32,
    )
    input_grad = lax.psum_scatter(
        partial_grad.astype(jnp.bfloat16), "col", scatter_dimension=1, tiled=True
    )
    return (activated, input_grad)


def solution(mesh):
    return jax.shard_map(
        body,
        mesh=mesh,
        in_specs=(P("row", "col"), P("row", "col"), P("row", "col"), P("row", "col")),
        out_specs=(P("row", "col"), P("row", "col")),
        check_vma=False,
    )
```

profile of v0, /device:TPU:1, one launch (start us, length us, event | category | flops | bytes accessed | tf_op | source)
XLA Modules:
  0.0 389.6 jit_solution(9525455329591428692)
XLA Ops:
  7.2 0.0 all-gather.3.cloned.1.call-start
  7.2 0.7 all-gather.3.cloned.1.call-update
  7.9 0.0 all-gather.5.cloned.1.call-start
  7.9 0.7 all-gather.5.cloned.1.call-update
  8.6 0.0 copy-start
  8.7 0.0 reduce-scatter.2.cloned.1.call-start
  8.7 82.6 %all-gather.3.cloned.1.call-done = bf16[960,4096]{1,0:T(8,128)(2,1)} async-done(((bf16[960,256]{1,0:T(8,128)(2,1)}), bf16[960,4096]{1,0:T(8,128)(2,1)}) %all-gather.3.cloned.1.call-update) | async-done | bytes 7864336 | tf_op jit(solution)/shard_map/all_gather | solution.py:11
  91.3 150.8 %all-gather.5.cloned.1.call-done = bf16[4096,1792]{1,0:T(8,128)(2,1)} async-done(((bf16[512,1792]{1,0:T(8,128)(2,1)}), bf16[4096,1792]{1,0:T(8,128)(2,1)}) %all-gather.5.cloned.1.call-update) | async-done | bytes 14680080 | tf_op jit(solution)/shard_map/all_gather | solution.py:14
  242.1 23.4 %multiply_convert_fusion = (bf16[960,1792]{1,0:T(8,128)(2,1)}, f32[960,1792]{1,0:T(8,128)}) fusion(f32[960,1792]{1,0:T(8,128)} %param.4, bf16[960,4096]{1,0:T(8,128)(2,1)} %all-gather.3.cloned.1.call-done, bf16[4096,1792]{1,0:T(8,128)(2,1)} %all-gather.5.cloned.1.call-done), kind=kOutput, calls=%fused_computation.8 | convolution fusion | flops 14103183360 | bytes 39747584 | tf_op jit(solution)/shard_map/dot_general | solution.py:12
  265.5 0.0 copy-done
  265.5 23.4 %convolution_convert_fusion = bf16[960,4096]{1,0:T(8,128)(2,1)} fusion(bf16[4096,1792]{1,0:T(8,128)(2,1)} %all-gather.5.cloned.1.call-done, f32[960,1792]{1,0:T(8,128)} %get-tuple-element.3, bf16[960,1792]{1,0:T(8,128)(2,1)S(1)} %copy-done), kind=kOutput, calls=%fused_computation.1 | convolution fusion | flops 14115717120 | bytes 32866304 | tf_op jit(solution)/shard_map/dot_general | solution.py:23
  288.9 0.0 reduce-scatter.2.cloned.1.call-update
  289.0 94.1 %reduce-scatter.2.cloned.1.call-done = bf16[960,256]{1,0:T(8,128)(2,1)} async-done(((bf16[960,4096]{1,0:T(8,128)(2,1)}), bf16[960,256]{1,0:T(8,128)(2,1)}) %reduce-scatter.2.cloned.1.call-update) | async-done | bytes 491536 | tf_op jit(solution)/shard_map/reduce_scatter | solution.py:29
Async XLA Ops:
  7.2 84.1 %all-gather.3.cloned.1.call-start = ((), (), s32[]{:S(2)}) async-start(), calls=%async_computation.1 | async-start | bytes 8355840 | tf_op jit(solution)/shard_map/all_gather | solution.py:11
  7.9 234.2 %all-gather.5.cloned.1.call-start = ((), (), s32[]{:S(2)}) async-start(), calls=%async_computation.2 | async-start | bytes 16515072 | tf_op jit(solution)/shard_map/all_gather | solution.py:14
  8.6 256.9 %copy-start = (bf16[960,1792]{1,0:T(8,128)(2,1)S(1)}, bf16[960,1792]{1,0:T(8,128)(2,1)}, u32[]{:S(2)}) copy-start(bf16[960,1792]{1,0:T(8,128)(2,1)} %param.7) | copy-start | bytes 10321924
  8.7 374.4 %reduce-scatter.2.cloned.1.call-start = ((), (), s32[]{:S(2)}) async-start(), calls=%async_computation.3 | async-start | bytes 8355840 | tf_op jit(solution)/shard_map/reduce_scatter | solution.py:29
Sparse Core Ops, SparseCore 0:
  10.3 80.9 all-gather.2
  92.9 149.1 all-gather.4
  289.1 93.9 reduce-scatter.1
where the time goes:
time: 390 us
  waiting for transfers between devices  329 us (84%)
  matrix products  46.8 us (12%)
  between operations  13.7 us (4%)
    all_gather x1, waiting for transfers between devices, body(): lax.all_gather(w_panels, 'row', axis=0, tiled=True)  151 us
    reduce_scatter x1, waiting for transfers between devices, body(): lax.psum_scatter(partial_grad.astype(jnp.bfloat16), 'col', scatter_dimens...  94.1 us
    all_gather x1, waiting for transfers between devices, body(): x_whole = lax.all_gather(x_panels, 'col', axis=1, tiled=True)  82.6 us
    dot_general x1, matrix products, body(): lax.dot_general(slope_grad, lax.all_gather(w_panels, 'row', axis=0, tiled...  23.4 us
    dot_general x1, matrix products, body(): jnp.dot(x_whole, lax.all_gather(w_panels, 'row', axis=0, tiled=True), pre...  23.4 us
  transfers between devices with their start and end apart: 3, of which 3 were waited for; matrix products, arithmetic and copies ran while one was open for 0% of the time, Pallas kernels for 0%

commit v1 on v0

v1 whole, which is shorter than its diff:
```python
import jax
import jax.numpy as jnp
from jax import lax
from jax.experimental import pallas as pl
from jax.experimental.pallas import tpu as pltpu
from jax.sharding import Mesh, PartitionSpec as P

inv_root_two = 0.7071067811865476
inv_root_tau = 0.3989422804014327

NZ, NX = 4, 4
WIDTHS = (1280, 512)
ROWS_AXES = ("y_lo", "z")
COLS_AXES = ("x", "y_hi", "core")
F32, BF16 = jnp.float32, jnp.bfloat16


def shift(value, axis, by, size):
    return lax.ppermute(value, axis, [(i, (i + by) % size) for i in range(size)])


def gather_w(own):
    half = own.shape[0] // 2
    z_minus = shift(own, "z", 1, NZ)
    z_plus = shift(own, "z", -1, NZ)
    other = shift(own, "y_lo", 1, 2)
    far_a = shift(z_minus[:half], "z", 1, NZ)
    far_b = shift(z_plus[half:], "z", -1, NZ)
    other_minus = shift(other, "z", 1, NZ)
    other_plus = shift(other, "z", -1, NZ)
    far = jnp.concatenate([far_a, far_b])
    other_far = shift(far, "y_lo", 1, 2)
    return jnp.stack([own, z_plus, far, z_minus, other, other_plus, other_far, other_minus])


def gather_x(own):
    pair = jnp.stack([own, shift(own, "y_hi", 1, 2)])
    x_minus = shift(pair, "x", 1, NX)
    x_plus = shift(pair, "x", -1, NX)
    far = jnp.stack([shift(x_minus[0], "x", 1, NX), shift(x_plus[1], "x", -1, NX)])
    mine = jnp.concatenate([pair, x_plus, far, x_minus])
    theirs = shift(mine, "core", 1, 2)
    return mine, theirs


def grad_kernel(pick_ref, core_ref, s_ref, w_ref, base_ref, mine_ref, theirs_ref):
    core = core_ref[0]
    rows = w_ref.shape[1] // 2
    for half, out in ((core, mine_ref), (1 - core, theirs_ref)):
        part = w_ref[0, pl.ds(pl.multiple_of(half * rows, rows), rows), :]
        out[0] = lax.dot_general(
            s_ref[...], part, (((1,), (1,)), ((), ())), preferred_element_type=F32
        ).astype(out.dtype)


def grad_blocks(s, w, picks, core, out_dtype):
    tokens, width = s.shape
    n = picks.shape[0]
    rows = w.shape[1]
    return pl.pallas_call(
        lambda p, c, a, b, m, t: grad_kernel(p, c, a, b, None, m, t),
        grid_spec=pltpu.PrefetchScalarGridSpec(
            num_scalar_prefetch=2,
            grid=(n,),
            in_specs=[
                pl.BlockSpec((tokens, width), lambda i, p, c: (0, 0)),
                pl.BlockSpec((1, rows, width), lambda i, p, c: (p[i], 0, 0)),
            ],
            out_specs=[
                pl.BlockSpec((1, tokens, rows // 2), lambda i, p, c: (i, 0, 0)),
                pl.BlockSpec((1, tokens, rows // 2), lambda i, p, c: (i, 0, 0)),
            ],
        ),
        out_shape=[jax.ShapeDtypeStruct((n, tokens, rows // 2), out_dtype)] * 2,
        compiler_params=pltpu.CompilerParams(vmem_limit_bytes=40 * 2**20),
        cost_estimate=pl.CostEstimate(flops=1000, bytes_accessed=1000, transcendentals=0),
    )(picks, core, s, w)


def body(carried_sum, x_panels, w_panels, cotangent):
    y_lo, z = lax.axis_index("y_lo"), lax.axis_index("z")
    x, y_hi, core = lax.axis_index("x"), lax.axis_index("y_hi"), lax.axis_index("core")
    core_of = core.reshape(1).astype(jnp.int32)

    which = []
    for dy in range(2):
        for dz in range(NZ):
            r = ((y_lo + dy) % 2) * NZ + (z + dz) % NZ
            which.append(((r // 2 - x) % NX) * 2 + (r % 2 - y_hi) % 2)

    def block_for(dx, dyh):
        r = ((x + dx) % NX) * 2 + (y_hi + dyh) % 2
        return ((r // NZ - y_lo) % 2) * NZ + (r % NZ - z) % NZ

    order = ((2, 0), (2, 1), (1, 1), (3, 1), (1, 0), (3, 0), (0, 1), (0, 0))
    picks = jnp.stack([block_for(*d) for d in order]).astype(jnp.int32)

    mine, theirs = gather_x(x_panels)
    first = jnp.where(core == 0, mine, theirs)
    second = jnp.where(core == 0, theirs, mine)
    x_cols = []
    for at in which:
        x_cols.append(lax.dynamic_index_in_dim(first, at, 0, keepdims=False))
        x_cols.append(lax.dynamic_index_in_dim(second, at, 0, keepdims=False))
    x_whole = jnp.concatenate(x_cols, axis=1)

    activated, grads = [], []
    start = 0
    w_chunks, s_chunks = [], []
    for width in WIDTHS:
        cols = slice(start, start + width)
        start += width
        w_all = gather_w(w_panels[:, cols])
        preact = carried_sum[:, cols] + jnp.dot(
            x_whole, w_all.reshape(-1, width), preferred_element_type=F32
        )
        normal_cdf = 0.5 * (1.0 + jax.scipy.special.erf(preact * inv_root_two))
        normal_pdf = jnp.exp(-0.5 * preact * preact) * inv_root_tau
        activated.append((preact * normal_cdf).astype(BF16))
        s_chunks.append(
            (cotangent[:, cols].astype(F32) * (normal_cdf + preact * normal_pdf)).astype(BF16)
        )
        w_chunks.append(w_all)

    base_mine, base_theirs = grad_blocks(s_chunks[0], w_chunks[0], picks, core_of, F32)

    def blocks(lo, hi):
        m, t = grad_blocks(s_chunks[1], w_chunks[1], picks[lo:hi], core_of, F32)
        m = m + base_mine[lo:hi]
        t = (t + base_theirs[lo:hi]).astype(BF16)
        return m + shift(t, "core", 1, 2).astype(F32)

    half = carried_sum.shape[0] // 2
    b2 = blocks(0, 2).astype(BF16)
    via_minus = shift(b2[:, :half], "x", 1, NX)
    via_plus = shift(b2[:, half:], "x", -1, NX)
    got = []
    for pair in (1, 0):
        b13 = blocks(2, 4) if pair == 1 else blocks(4, 6)
        up = jnp.concatenate([b13[0, :half] + via_minus[pair].astype(F32), b13[0, half:]])
        down = jnp.concatenate([b13[1, :half], b13[1, half:] + via_plus[pair].astype(F32)])
        got.append(
            (shift(up.astype(BF16), "x", 1, NX), shift(down.astype(BF16), "x", -1, NX))
        )
    b0 = blocks(6, 8)
    to_other = b0[0] + got[0][0].astype(F32) + got[0][1].astype(F32)
    from_other = shift(to_other.astype(BF16), "y_hi", 1, 2)
    input_grad = (
        b0[1] + got[1][0].astype(F32) + got[1][1].astype(F32) + from_other.astype(F32)
    ).astype(BF16)
    return jnp.concatenate(activated, axis=1), input_grad


def solution(mesh):
    fine = Mesh(mesh.devices.reshape(2, 4, 4, 2, 2), ROWS_AXES + COLS_AXES)
    spec = P(ROWS_AXES, COLS_AXES)
    return jax.shard_map(
        body,
        mesh=fine,
        in_specs=(spec, spec, spec, spec),
        out_specs=(spec, spec),
        check_vma=False,
    )
```

time: 390 us -> 292 us (0.75); the launches traced: 390 us -> 288 us
  waiting for transfers between devices: 329 us -> 134 us
  starting transfers between devices: 0.11 us -> 42.7 us
  local copies, waits for them, and re-layouts: 0.01 us -> 35 us
  Pallas kernels: 0 us -> 24.1 us
  other arithmetic: 0 us -> 22.1 us
  matrix products: 46.8 us -> 27.8 us
  between operations: 13.7 us -> 1.83 us
    all_gather x2 -> x0, waiting for transfers between devices: 233 us -> none  [the longest x1 151 us: body(): lax.all_gather(w_panels, 'row', axis=0, tiled=True)]
    ppermute x0 -> x33, waiting for transfers between devices: none -> 134 us  [shift(): lax.ppermute(value, axis, [(i, (i + by) % size) for i in range(size)])]
    reduce_scatter x1 -> x0, waiting for transfers between devices: 94.1 us -> none  [body(): lax.psum_scatter(partial_grad.astype(jnp.bfloat16), 'col', scatter_dimens...]
    ppermute x0 -> x33, starting transfers between devices: none -> 42.7 us  [shift(): lax.ppermute(value, axis, [(i, (i + by) % size) for i in range(size)])]
    unnamed x2 -> x80, local copies, waits for them, and re-layouts: 0.01 us -> 27.7 us
    pallas_call x0 -> x5, Pallas kernels: none -> 24.1 us  [grad_blocks(): pl.pallas_call(lambda p, c, a, b, m, t: grad_kernel(p, c, a, b, None, m,...]
    dot_general x2, matrix products: 46.8 us -> 27.8 us  [body(): jnp.dot(x_whole, w_all.reshape(-1, width), preferred_element_type=F32)]
    another operation x0 -> x4, other arithmetic: none -> 9.85 us
  transfers between devices with their start and end apart: 3 -> 33, of which waited for: 3 -> 18; matrix products, arithmetic and copies ran while one was open for 0% -> 8% of each run, Pallas kernels for 0% -> 0%
where the time goes in v1:
time: 292 us; the launch traced here: 288 us
  waiting for transfers between devices  134 us (46%)
  starting transfers between devices  42.7 us (15%)
  local copies, waits for them, and re-layouts  35 us (12%)
  matrix products  27.8 us (10%)
  Pallas kernels  24.1 us (8%)
  other arithmetic  22.1 us (8%)
    ppermute x33, waiting for transfers between devices, shift(): lax.ppermute(value, axis, [(i, (i + by) % size) for i in range(size)])  134 us
    ppermute x33, starting transfers between devices, shift(): lax.ppermute(value, axis, [(i, (i + by) % size) for i in range(size)])  42.7 us
    dot_general x2, matrix products, body(): jnp.dot(x_whole, w_all.reshape(-1, width), preferred_element_type=F32)  27.8 us
    unnamed x80, local copies, waits for them, and re-layouts  27.7 us
    pallas_call x5, Pallas kernels, grad_blocks(): pl.pallas_call(lambda p, c, a, b, m, t: grad_kernel(p, c, a, b, None, m,...  24.1 us
    another operation x1, other arithmetic  9.6 us
    convert_element_type x1, other arithmetic, blocks(): t = (t + base_theirs[lo:hi]).astype(BF16)  6.5 us
  transfers between devices with their start and end apart: 33, of which 18 were waited for; matrix products, arithmetic and copies ran while one was open for 8% of the time, Pallas kernels for 0%

profile of v1, /device:TPU:1, one launch (start us, length us, event | category | flops | bytes accessed | tf_op | source)
XLA Modules:
  0.0 287.7 jit_solution(3294487749053257295)
XLA Ops:
  0.7 2.0 slice.127
  2.7 4.6 %collective-permute-start.14 = (bf16[512,512]{1,0:T(8,128)(2,1)}, bf16[512,512]{1,0:T(8,128)(2,1)S(1)}, u32[]{:S(2)}, u32[]{:S(2)}) collective-permute-start(bf16[512,512]{1,0:T(8,128)(2,1)} %slice.127), channel_id=1, source_target_pairs={{0,48},{16,0},{32,16},{48,32},{1,49},{17,1},{33,17},{49,33},{2,50}... | collective-permute-start | bytes 1572872 | tf_op jit(solution)/shard_map/ppermute | solution.py:19
  7.3 1.3 collective-permute-start.18
  8.6 2.6 collective-permute-start
  11.2 2.5 slice.123
  13.6 2.7 collective-permute-start.6
  20.0 12.9 %collective-permute-done = bf16[960,256]{1,0:T(8,128)(2,1)S(1)} collective-permute-done((bf16[960,256]{1,0:T(8,128)(2,1)}, bf16[960,256]{1,0:T(8,128)(2,1)S(1)}, u32[]{:S(2)}, u32[]{:S(2)}) %collective-permute-start) | collective-permute-done | bytes 491552 | tf_op jit(solution)/shard_map/ppermute | solution.py:19
  34.7 2.1 collective-permute-start.17
  37.6 30.8 %collective-permute-done.16 = bf16[256,512]{1,0:T(8,128)(2,1)S(1)} collective-permute-done((bf16[256,512]{1,0:T(8,128)(2,1)S(1)}, bf16[256,512]{1,0:T(8,128)(2,1)S(1)}, u32[]{:S(2)}, u32[]{:S(2)}) %collective-permute-start.16) | collective-permute-done | bytes 262176 | tf_op jit(solution)/shard_map/ppermute | solution.py:19
  72.3 1.9 bitcast_dynamic-update-slice_fusion.11
  74.2 6.0 %collective-permute-done.19 = bf16[512,512]{1,0:T(8,128)(2,1)S(1)} collective-permute-done((bf16[512,512]{1,0:T(8,128)(2,1)}, bf16[512,512]{1,0:T(8,128)(2,1)S(1)}, u32[]{:S(2)}, u32[]{:S(2)}) %collective-permute-start.19) | collective-permute-done | bytes 524320 | tf_op jit(solution)/shard_map/ppermute | solution.py:19
  80.1 1.5 collective-permute-start.1
  82.4 1.3 collective-permute-start.20
  85.0 5.1 %collective-permute-done.2 = bf16[2,960,256]{2,1,0:T(8,128)(2,1)S(1)} collective-permute-done((bf16[2,960,256]{2,1,0:T(8,128)(2,1)S(1)}, bf16[2,960,256]{2,1,0:T(8,128)(2,1)S(1)}, u32[]{:S(2)}, u32[]{:S(2)}) %collective-permute-start.2) | collective-permute-done | bytes 983072 | tf_op jit(solution)/shard_map/ppermute | solution.py:19
  90.1 9.2 %collective-permute-done.1 = bf16[2,960,256]{2,1,0:T(8,128)(2,1)S(1)} collective-permute-done((bf16[2,960,256]{2,1,0:T(8,128)(2,1)S(1)}, bf16[2,960,256]{2,1,0:T(8,128)(2,1)S(1)}, u32[]{:S(2)}, u32[]{:S(2)}) %collective-permute-start.1) | collective-permute-done | bytes 983072 | tf_op jit(solution)/shard_map/ppermute | solution.py:19
  100.5 6.8 %collective-permute-done.20 = bf16[512,512]{1,0:T(8,128)(2,1)S(1)} collective-permute-done((bf16[512,512]{1,0:T(8,128)(2,1)S(1)}, bf16[512,512]{1,0:T(8,128)(2,1)S(1)}, u32[]{:S(2)}, u32[]{:S(2)}) %collective-permute-start.20) | collective-permute-done | bytes 524320 | tf_op jit(solution)/shard_map/ppermute | solution.py:19
  107.3 2.5 collective-permute-start.4
  110.8 5.8 %collective-permute-done.4 = bf16[960,256]{1,0:T(8,128)(2,1)S(1)} collective-permute-done((bf16[960,256]{1,0:T(8,128)(2,1)S(1)}, bf16[960,256]{1,0:T(8,128)(2,1)S(1)}, u32[]{:S(2)}, u32[]{:S(2)}) %collective-permute-start.4) | collective-permute-done | bytes 491552 | tf_op jit(solution)/shard_map/ppermute | solution.py:19
  116.7 4.7 %collective-permute-start.5 = (bf16[8,960,256]{2,1,0:T(8,128)(2,1)S(1)}, bf16[8,960,256]{2,1,0:T(8,128)(2,1)S(1)}, u32[]{:S(2)}, u32[]{:S(2)}) collective-permute-start(bf16[8,960,256]{2,1,0:T(8,128)(2,1)S(1)} %constant_dynamic-update-slice_fusion), channel_id=1, source_target_pairs={{0,1},{1,0},{2,3},{3,2},{4,5},{5,4},{6,7},{7,6},{8,9},{9,8},{10,11... | collective-permute-start | bytes 11796488 | tf_op jit(solution)/shard_map/ppermute | solution.py:19
  126.4 24.0 %collective-permute-done.11 = bf16[512,1280]{1,0:T(8,128)(2,1)S(1)} collective-permute-done((bf16[512,1280]{1,0:T(8,128)(2,1)S(1)}, bf16[512,1280]{1,0:T(8,128)(2,1)S(1)}, u32[]{:S(2)}, u32[]{:S(2)}) %collective-permute-start.11) | collective-permute-done | bytes 1310752 | tf_op jit(solution)/shard_map/ppermute | solution.py:19
  155.6 8.7 %fusion.11 = (bf16[960,512]{1,0:T(8,128)(2,1)S(1)}, bf16[960,512]{1,0:T(8,128)(2,1)}) fusion(bf16[960,1792]{1,0:T(8,128)(2,1)} %param.7, bf16[960,4096]{1,0:T(8,128)(2,1)S(1)} %bitcast_dynamic-update-slice_fusion.16, bf16[4096,512]{1,0:T(8,128)(2,1)S(1)} %bitcast.125, f32[960,1792]{1,0:T(8,128)} %param.4), kind=kOutput, calls=%fused_computation.19 | convolution fusion | flops 4033413120 | bytes 16973824 | tf_op jit(solution)/shard_map/dot_general | solution.py:114
  164.4 19.1 %fusion.5 = (bf16[960,1280]{1,0:T(8,128)(2,1)S(1)}, bf16[960,1280]{1,0:T(8,128)(2,1)}) fusion(bf16[960,1792]{1,0:T(8,128)(2,1)S(1)} %copy-done.21, bf16[960,4096]{1,0:T(8,128)(2,1)} %copy-done.20, bf16[4096,1280]{1,0:T(8,128)(2,1)} %bitcast.126, f32[960,1792]{1,0:T(8,128)} %param.4), kind=kOutput, calls=%fused_computation.6 | convolution fusion | flops 10083532800 | bytes 30638080 | tf_op jit(solution)/shard_map/dot_general | solution.py:114
  183.4 2.0 shard_map.61
  185.4 1.3 copy-done.5
  186.7 2.0 shard_map.63
  191.3 2.0 shard_map.62
  193.3 1.3 copy-done.3
  194.6 1.3 copy-done.7
  195.9 2.0 shard_map.59
  197.9 16.2 %shard_map.60 = (f32[8,960,256]{2,1,0:T(8,128)S(1)}, f32[8,960,256]{2,1,0:T(8,128)}) custom-call(s32[8]{0:T(128)S(1)} %stack.136.p, s32[1]{0:T(128)} %bitcast.42.c, bf16[960,1280]{1,0:T(8,128)(2,1)S(1)} %get-tuple-element.36.a, bf16[8,512,1280]{2,1,0:T(8,128)(2,1)} %bitcast_dynamic-update-slice_fusion.b), custom_call_target="tpu_custom_call" | custom-call | flops 1000 | bytes 1000 | tf_op jit(solution)/shard_map/pallas_call | solution.py:60
  214.1 3.1 %copy-done.1 = f32[8,960,256]{2,1,0:T(8,128)} copy-done((f32[8,960,256]{2,1,0:T(8,128)}, f32[8,960,256]{2,1,0:T(8,128)S(1)}, u32[]{:S(2)}) %copy-start.1) | copy-done | bytes 7864344
  217.2 6.5 %add_convert_fusion.3 = (bf16[2,960,256]{2,1,0:T(8,128)(2,1)S(1)}, bf16[2,960,256]{2,1,0:T(8,128)(2,1)S(1)}, bf16[2,960,256]{2,1,0:T(8,128)(2,1)S(1)}, bf16[2,960,256]{2,1,0:T(8,128)(2,1)S(1)}) fusion(f32[2,960,256]{2,1,0:T(8,128)} %copy-done.5, f32[8,960,256]{2,1,0:T(8,128)} %get-tuple-element.15, f32[2,960,256]{2,1,0:T(8,128)} %copy-done.6, ...), kind=kLoop, calls=%fused_computation.25 | loop fusion | flops 3932160 | bytes 19660800 | tf_op jit(solution)/shard_map/convert_element_type | solution.py:130
  223.7 5.0 %collective-permute-start.23 = (bf16[2,960,256]{2,1,0:T(8,128)(2,1)S(1)}, bf16[2,960,256]{2,1,0:T(8,128)(2,1)S(1)}, u32[]{:S(2)}, u32[]{:S(2)}) collective-permute-start(bf16[2,960,256]{2,1,0:T(8,128)(2,1)S(1)} %get-tuple-element.30), channel_id=1, source_target_pairs={{0,1},{1,0},{2,3},{3,2},{4,5},{5,4},{6,7},{7,6},{8,9},{9,8},{10,11... | collective-permute-start | bytes 2949128 | tf_op jit(solution)/shard_map/ppermute | solution.py:19
  229.3 1.6 collective-permute-done.23
  230.9 1.4 collective-permute-done.29
  232.3 1.4 collective-permute-done.24
  233.7 1.4 collective-permute-done.22
  236.1 9.6 %fusion.27 = (bf16[2,960,256]{2,1,0:T(8,128)(2,1)}, f32[2,960,256]{2,1,0:T(8,128)}, bf16[2,960,256]{2,1,0:T(8,128)(2,1)}, f32[2,960,256]{2,1,0:T(8,128)}, bf16[2...) fusion(bf16[2,960,256]{2,1,0:T(8,128)(2,1)} %copy-done.15, f32[2,960,256]{2,1,0:T(8,128)S(1)} %get-tuple-element.16, ...), kind=kLoop, calls=%fused_computation.109 | loop fusion | flops 7372800 | bytes 28508160 | tf_op jit(solution)/shard_map/convert.18
  245.9 2.7 collective-permute-start.27
  249.7 9.9 %collective-permute-done.25 = bf16[2,480,256]{2,1,0:T(8,128)(2,1)S(1)} collective-permute-done((bf16[2,480,256]{2,1,0:T(8,128)(2,1)S(1)}, bf16[2,480,256]{2,1,0:T(8,128)(2,1)S(1)}, u32[]{:S(2)}, u32[]{:S(2)}) %collective-permute-start.25) | collective-permute-done | bytes 491552 | tf_op jit(solution)/shard_map/ppermute | solution.py:19
  259.5 1.9 fusion.25
  261.5 2.4 collective-permute-start.31
  264.1 2.7 collective-permute-start.28
  267.0 6.1 %collective-permute-done.31 = bf16[960,256]{1,0:T(8,128)(2,1)S(1)} collective-permute-done((bf16[960,256]{1,0:T(8,128)(2,1)S(1)}, bf16[960,256]{1,0:T(8,128)(2,1)S(1)}, u32[]{:S(2)}, u32[]{:S(2)}) %collective-permute-start.31) | collective-permute-done | bytes 491552 | tf_op jit(solution)/shard_map/ppermute | solution.py:19
  273.1 3.1 %collective-permute-done.30 = bf16[960,256]{1,0:T(8,128)(2,1)S(1)} collective-permute-done((bf16[960,256]{1,0:T(8,128)(2,1)S(1)}, bf16[960,256]{1,0:T(8,128)(2,1)S(1)}, u32[]{:S(2)}, u32[]{:S(2)}) %collective-permute-start.30) | collective-permute-done | bytes 491552 | tf_op jit(solution)/shard_map/ppermute | solution.py:19
  276.8 2.0 pad_maximum_fusion
  278.8 4.8 %collective-permute-done.28 = bf16[960,256]{1,0:T(8,128)(2,1)S(1)} collective-permute-done((bf16[960,256]{1,0:T(8,128)(2,1)S(1)}, bf16[960,256]{1,0:T(8,128)(2,1)S(1)}, u32[]{:S(2)}, u32[]{:S(2)}) %collective-permute-start.28) | collective-permute-done | bytes 491552 | tf_op jit(solution)/shard_map/ppermute | solution.py:19
  283.6 3.1 %collective-permute-done.26 = bf16[960,256]{1,0:T(8,128)(2,1)S(1)} collective-permute-done((bf16[960,256]{1,0:T(8,128)(2,1)S(1)}, bf16[960,256]{1,0:T(8,128)(2,1)S(1)}, u32[]{:S(2)}, u32[]{:S(2)}) %collective-permute-start.26) | collective-permute-done | bytes 491552 | tf_op jit(solution)/shard_map/ppermute | solution.py:19
  (137 shorter events, 31.2 us)
Async XLA Ops:
  0.6 15.7 %copy-start.10 = (bf16[512,1792]{1,0:T(8,128)(2,1)S(1)}, bf16[512,1792]{1,0:T(8,128)(2,1)}, u32[]{:S(2)}) copy-start(bf16[512,1792]{1,0:T(8,128)(2,1)} %param.6) | copy-start | bytes 5505028
  0.6 17.7 %copy-start.14 = (bf16[960,256]{1,0:T(8,128)(2,1)S(1)}, bf16[960,256]{1,0:T(8,128)(2,1)}, u32[]{:S(2)}) copy-start(bf16[960,256]{1,0:T(8,128)(2,1)} %param.5) | copy-start | bytes 1474564
  2.7 32.0 %collective-permute-start.14 = (bf16[512,512]{1,0:T(8,128)(2,1)}, bf16[512,512]{1,0:T(8,128)(2,1)S(1)}, u32[]{:S(2)}, u32[]{:S(2)}) collective-permute-start(bf16[512,512]{1,0:T(8,128)(2,1)} %slice.127), channel_id=1, source_target_pairs={{0,48},{16,0},{32,16},{48,32},{1,49},{17,1},{33,17},{49,33},{2,50}... | collective-permute-start | bytes 1572872 | tf_op jit(solution)/shard_map/ppermute | solution.py:19
  7.3 26.5 %collective-permute-start.15 = (bf16[512,512]{1,0:T(8,128)(2,1)}, bf16[512,512]{1,0:T(8,128)(2,1)S(1)}, u32[]{:S(2)}, u32[]{:S(2)}) collective-permute-start(bf16[512,512]{1,0:T(8,128)(2,1)} %slice.127), channel_id=1, source_target_pairs={{0,16},{16,32},{32,48},{48,0},{1,17},{17,33},{33,49},{49,1},{2,18}... | collective-permute-start | bytes 1572872 | tf_op jit(solution)/shard_map/ppermute | solution.py:19
  7.3 61.1 %collective-permute-start.18 = (bf16[512,512]{1,0:T(8,128)(2,1)}, bf16[512,512]{1,0:T(8,128)(2,1)}, u32[]{:S(2)}, u32[]{:S(2)}) collective-permute-start(bf16[512,512]{1,0:T(8,128)(2,1)} %slice.127), channel_id=1, source_target_pairs={{0,64},{64,0},{1,65},{65,1},{2,66},{66,2},{3,67},{67,3},{4,68},{68... | collective-permute-start | bytes 1572872 | tf_op jit(solution)/shard_map/ppermute | solution.py:19
  8.6 24.4 %collective-permute-start = (bf16[960,256]{1,0:T(8,128)(2,1)}, bf16[960,256]{1,0:T(8,128)(2,1)S(1)}, u32[]{:S(2)}, u32[]{:S(2)}) collective-permute-start(bf16[960,256]{1,0:T(8,128)(2,1)} %param.5), channel_id=1, source_target_pairs={{0,2},{2,0},{1,3},{3,1},{4,6},{6,4},{5,7},{7,5},{8,10},{10,8},{9,1... | collective-permute-start | bytes 1474568 | tf_op jit(solution)/shard_map/ppermute | solution.py:19
  13.6 68.8 %collective-permute-start.6 = (bf16[512,1280]{1,0:T(8,128)(2,1)}, bf16[512,1280]{1,0:T(8,128)(2,1)S(1)}, u32[]{:S(2)}, u32[]{:S(2)}) collective-permute-start(bf16[512,1280]{1,0:T(8,128)(2,1)} %slice.123), channel_id=1, source_target_pairs={{0,48},{16,0},{32,16},{48,32},{1,49},{17,1},{33,17},{49,33},{2,50}... | collective-permute-start | bytes 3932168 | tf_op jit(solution)/shard_map/ppermute | solution.py:19
  32.9 52.0 %collective-permute-start.7 = (bf16[512,1280]{1,0:T(8,128)(2,1)}, bf16[512,1280]{1,0:T(8,128)(2,1)S(1)}, u32[]{:S(2)}, u32[]{:S(2)}) collective-permute-start(bf16[512,1280]{1,0:T(8,128)(2,1)} %slice.123), channel_id=1, source_target_pairs={{0,16},{16,32},{32,48},{48,0},{1,17},{17,33},{33,49},{49,1},{2,18}... | collective-permute-start | bytes 3932168 | tf_op jit(solution)/shard_map/ppermute | solution.py:19
  33.8 34.6 %collective-permute-start.16 = (bf16[256,512]{1,0:T(8,128)(2,1)S(1)}, bf16[256,512]{1,0:T(8,128)(2,1)S(1)}, u32[]{:S(2)}, u32[]{:S(2)}) collective-permute-start(bf16[256,512]{1,0:T(8,128)(2,1)S(1)} %slice.160), channel_id=1, source_target_pairs={{0,16},{16,32},{32,48},{48,0},{1,17},{17,33},{33,49},{49,1},{2,18}... | collective-permute-start | bytes 786440 | tf_op jit(solution)/shard_map/ppermute | solution.py:19
  34.7 35.0 %collective-permute-start.17 = (bf16[256,512]{1,0:T(8,128)(2,1)S(1)}, bf16[256,512]{1,0:T(8,128)(2,1)S(1)}, u32[]{:S(2)}, u32[]{:S(2)}) collective-permute-start(bf16[256,512]{1,0:T(8,128)(2,1)S(1)} %slice.161), channel_id=1, source_target_pairs={{0,48},{16,0},{32,16},{48,32},{1,49},{17,1},{33,17},{49,33},{2,50}... | collective-permute-start | bytes 786440 | tf_op jit(solution)/shard_map/ppermute | solution.py:19
  68.4 41.6 %collective-permute-start.10 = (bf16[512,1280]{1,0:T(8,128)(2,1)}, bf16[512,1280]{1,0:T(8,128)(2,1)S(1)}, u32[]{:S(2)}, u32[]{:S(2)}) collective-permute-start(bf16[512,1280]{1,0:T(8,128)(2,1)} %slice.123), channel_id=1, source_target_pairs={{0,64},{64,0},{1,65},{65,1},{2,66},{66,2},{3,67},{67,3},{4,68},{68... | collective-permute-start | bytes 3932168 | tf_op jit(solution)/shard_map/ppermute | solution.py:19
  68.4 21.6 %collective-permute-start.2 = (bf16[2,960,256]{2,1,0:T(8,128)(2,1)S(1)}, bf16[2,960,256]{2,1,0:T(8,128)(2,1)S(1)}, u32[]{:S(2)}, u32[]{:S(2)}) collective-permute-start(bf16[2,960,256]{2,1,0:T(8,128)(2,1)S(1)} %pad_maximum_fusion.1), channel_id=1, source_target_pairs={{0,4},{4,8},{8,12},{12,0},{1,5},{5,9},{9,13},{13,1},{2,6},{6,10},{... | collective-permute-start | bytes 2949128 | tf_op jit(solution)/shard_map/ppermute | solution.py:19
  69.7 10.4 %collective-permute-start.19 = (bf16[512,512]{1,0:T(8,128)(2,1)}, bf16[512,512]{1,0:T(8,128)(2,1)S(1)}, u32[]{:S(2)}, u32[]{:S(2)}) collective-permute-start(bf16[512,512]{1,0:T(8,128)(2,1)} %collective-permute-done.18), channel_id=1, source_target_pairs={{0,48},{16,0},{32,16},{48,32},{1,49},{17,1},{33,17},{49,33},{2,50}... | collective-permute-start | bytes 1572872 | tf_op jit(solution)/shard_map/ppermute | solution.py:19
  80.1 19.1 %collective-permute-start.1 = (bf16[2,960,256]{2,1,0:T(8,128)(2,1)S(1)}, bf16[2,960,256]{2,1,0:T(8,128)(2,1)S(1)}, u32[]{:S(2)}, u32[]{:S(2)}) collective-permute-start(bf16[2,960,256]{2,1,0:T(8,128)(2,1)S(1)} %pad_maximum_fusion.1), channel_id=1, source_target_pairs={{0,12},{4,0},{8,4},{12,8},{1,13},{5,1},{9,5},{13,9},{2,14},{6,2},{... | collective-permute-start | bytes 2949128 | tf_op jit(solution)/shard_map/ppermute | solution.py:19
  82.4 27.4 %copy-start = (bf16[8,512,512]{2,1,0:T(8,128)(2,1)S(1)}, bf16[8,512,512]{2,1,0:T(8,128)(2,1)}, u32[]{:S(2)}) copy-start(bf16[8,512,512]{2,1,0:T(8,128)(2,1)} %bitcast_dynamic-update-slice_fusion.10) | copy-start | bytes 12582916
  82.4 27.5 %copy-start.11 = (bf16[8,960,256]{2,1,0:T(8,128)(2,1)S(1)}, bf16[8,960,256]{2,1,0:T(8,128)(2,1)}, u32[]{:S(2)}) copy-start(bf16[8,960,256]{2,1,0:T(8,128)(2,1)} %constant_dynamic-update-slice_fusion.2) | copy-start | bytes 11796484
  82.4 24.9 %collective-permute-start.20 = (bf16[512,512]{1,0:T(8,128)(2,1)S(1)}, bf16[512,512]{1,0:T(8,128)(2,1)S(1)}, u32[]{:S(2)}, u32[]{:S(2)}) collective-permute-start(bf16[512,512]{1,0:T(8,128)(2,1)S(1)} %constant_dynamic-update-slice_fusion.6), channel_id=1, source_target_pairs={{0,64},{64,0},{1,65},{65,1},{2,66},{66,2},{3,67},{67,3},{4,68},{68... | collective-permute-start | bytes 1572872 | tf_op jit(solution)/shard_map/ppermute | solution.py:19
  84.9 31.8 %collective-permute-start.21 = (bf16[512,512]{1,0:T(8,128)(2,1)}, bf16[512,512]{1,0:T(8,128)(2,1)S(1)}, u32[]{:S(2)}, u32[]{:S(2)}) collective-permute-start(bf16[512,512]{1,0:T(8,128)(2,1)} %collective-permute-done.18), channel_id=1, source_target_pairs={{0,16},{16,32},{32,48},{48,0},{1,17},{17,33},{33,49},{49,1},{2,18}... | collective-permute-start | bytes 1572872 | tf_op jit(solution)/shard_map/ppermute | solution.py:19
  90.0 31.4 %collective-permute-start.8 = (bf16[256,1280]{1,0:T(8,128)(2,1)S(1)}, bf16[256,1280]{1,0:T(8,128)(2,1)S(1)}, u32[]{:S(2)}, u32[]{:S(2)}) collective-permute-start(bf16[256,1280]{1,0:T(8,128)(2,1)S(1)} %slice.158), channel_id=1, source_target_pairs={{0,16},{16,32},{32,48},{48,0},{1,17},{17,33},{33,49},{49,1},{2,18}... | collective-permute-start | bytes 1966088 | tf_op jit(solution)/shard_map/ppermute | solution.py:19
  99.3 11.4 %collective-permute-start.3 = (bf16[960,256]{1,0:T(8,128)(2,1)S(1)}, bf16[960,256]{1,0:T(8,128)(2,1)S(1)}, u32[]{:S(2)}, u32[]{:S(2)}) collective-permute-start(bf16[960,256]{1,0:T(8,128)(2,1)S(1)} %slice_bitcast_fusion.3), channel_id=1, source_target_pairs={{0,4},{4,8},{8,12},{12,0},{1,5},{5,9},{9,13},{13,1},{2,6},{6,10},{... | collective-permute-start | bytes 1474568 | tf_op jit(solution)/shard_map/ppermute | solution.py:19
  107.3 9.3 %collective-permute-start.4 = (bf16[960,256]{1,0:T(8,128)(2,1)S(1)}, bf16[960,256]{1,0:T(8,128)(2,1)S(1)}, u32[]{:S(2)}, u32[]{:S(2)}) collective-permute-start(bf16[960,256]{1,0:T(8,128)(2,1)S(1)} %slice_bitcast_fusion.2), channel_id=1, source_target_pairs={{0,12},{4,0},{8,4},{12,8},{1,13},{5,1},{9,5},{13,9},{2,14},{6,2},{... | collective-permute-start | bytes 1474568 | tf_op jit(solution)/shard_map/ppermute | solution.py:19
  110.0 12.3 %collective-permute-start.9 = (bf16[256,1280]{1,0:T(8,128)(2,1)S(1)}, bf16[256,1280]{1,0:T(8,128)(2,1)S(1)}, u32[]{:S(2)}, u32[]{:S(2)}) collective-permute-start(bf16[256,1280]{1,0:T(8,128)(2,1)S(1)} %slice.159), channel_id=1, source_target_pairs={{0,48},{16,0},{32,16},{48,32},{1,49},{17,1},{33,17},{49,33},{2,50}... | collective-permute-start | bytes 1966088 | tf_op jit(solution)/shard_map/ppermute | solution.py:19
  110.6 39.7 %collective-permute-start.11 = (bf16[512,1280]{1,0:T(8,128)(2,1)S(1)}, bf16[512,1280]{1,0:T(8,128)(2,1)S(1)}, u32[]{:S(2)}, u32[]{:S(2)}) collective-permute-start(bf16[512,1280]{1,0:T(8,128)(2,1)S(1)} %collective-permute-done.10), channel_id=1, source_target_pairs={{0,48},{16,0},{32,16},{48,32},{1,49},{17,1},{33,17},{49,33},{2,50}... | collective-permute-start | bytes 3932168 | tf_op jit(solution)/shard_map/ppermute | solution.py:19
  116.6 36.2 %collective-permute-start.13 = (bf16[512,1280]{1,0:T(8,128)(2,1)S(1)}, bf16[512,1280]{1,0:T(8,128)(2,1)S(1)}, u32[]{:S(2)}, u32[]{:S(2)}) collective-permute-start(bf16[512,1280]{1,0:T(8,128)(2,1)S(1)} %collective-permute-done.10), channel_id=1, source_target_pairs={{0,16},{16,32},{32,48},{48,0},{1,17},{17,33},{33,49},{49,1},{2,18}... | collective-permute-start | bytes 3932168 | tf_op jit(solution)/shard_map/ppermute | solution.py:19
  116.7 37.2 %collective-permute-start.5 = (bf16[8,960,256]{2,1,0:T(8,128)(2,1)S(1)}, bf16[8,960,256]{2,1,0:T(8,128)(2,1)S(1)}, u32[]{:S(2)}, u32[]{:S(2)}) collective-permute-start(bf16[8,960,256]{2,1,0:T(8,128)(2,1)S(1)} %constant_dynamic-update-slice_fusion), channel_id=1, source_target_pairs={{0,1},{1,0},{2,3},{3,2},{4,5},{5,4},{6,7},{7,6},{8,9},{9,8},{10,11... | collective-permute-start | bytes 11796488 | tf_op jit(solution)/shard_map/ppermute | solution.py:19
  122.3 29.3 %collective-permute-start.12 = (bf16[512,1280]{1,0:T(8,128)(2,1)S(1)}, bf16[512,1280]{1,0:T(8,128)(2,1)S(1)}, u32[]{:S(2)}, u32[]{:S(2)}) collective-permute-start(bf16[512,1280]{1,0:T(8,128)(2,1)S(1)} %constant_dynamic-update-slice_fusion.4), channel_id=1, source_target_pairs={{0,64},{64,0},{1,65},{65,1},{2,66},{66,2},{3,67},{67,3},{4,68},{68... | collective-permute-start | bytes 3932168 | tf_op jit(solution)/shard_map/ppermute | solution.py:19
  155.6 8.7 %copy-start.20 = (bf16[960,4096]{1,0:T(8,128)(2,1)}, bf16[960,4096]{1,0:T(8,128)(2,1)S(1)}, u32[]{:S(2)}) copy-start(bf16[960,4096]{1,0:T(8,128)(2,1)S(1)} %bitcast_dynamic-update-slice_fusion.16) | copy-start | bytes 23592964
  155.6 8.7 %copy-start.21 = (bf16[960,1792]{1,0:T(8,128)(2,1)S(1)}, bf16[960,1792]{1,0:T(8,128)(2,1)}, u32[]{:S(2)}) copy-start(bf16[960,1792]{1,0:T(8,128)(2,1)} %param.7) | copy-start | bytes 10321924
  197.9 16.2 %copy-start.4 = (f32[2,960,256]{2,1,0:T(8,128)}, f32[2,960,256]{2,1,0:T(8,128)S(1)}, u32[]{:S(2)}) copy-start(f32[2,960,256]{2,1,0:T(8,128)S(1)} %get-tuple-element.12) | copy-start | bytes 5898244
  197.9 16.2 %copy-start.8 = (f32[2,960,256]{2,1,0:T(8,128)}, f32[2,960,256]{2,1,0:T(8,128)S(1)}, u32[]{:S(2)}) copy-start(f32[2,960,256]{2,1,0:T(8,128)S(1)} %get-tuple-element.14) | copy-start | bytes 5898244
  214.1 3.1 %copy-start.1 = (f32[8,960,256]{2,1,0:T(8,128)}, f32[8,960,256]{2,1,0:T(8,128)S(1)}, u32[]{:S(2)}) copy-start(f32[8,960,256]{2,1,0:T(8,128)S(1)} %get-tuple-element.13) | copy-start | bytes 23592964
  223.7 7.2 %collective-permute-start.23 = (bf16[2,960,256]{2,1,0:T(8,128)(2,1)S(1)}, bf16[2,960,256]{2,1,0:T(8,128)(2,1)S(1)}, u32[]{:S(2)}, u32[]{:S(2)}) collective-permute-start(bf16[2,960,256]{2,1,0:T(8,128)(2,1)S(1)} %get-tuple-element.30), channel_id=1, source_target_pairs={{0,1},{1,0},{2,3},{3,2},{4,5},{5,4},{6,7},{7,6},{8,9},{9,8},{10,11... | collective-permute-start | bytes 2949128 | tf_op jit(solution)/shard_map/ppermute | solution.py:19
  228.7 3.6 %collective-permute-start.29 = (bf16[2,960,256]{2,1,0:T(8,128)(2,1)S(1)}, bf16[2,960,256]{2,1,0:T(8,128)(2,1)S(1)}, u32[]{:S(2)}, u32[]{:S(2)}) collective-permute-start(bf16[2,960,256]{2,1,0:T(8,128)(2,1)S(1)} %get-tuple-element.31), channel_id=1, source_target_pairs={{0,1},{1,0},{2,3},{3,2},{4,5},{5,4},{6,7},{7,6},{8,9},{9,8},{10,11... | collective-permute-start | bytes 2949128 | tf_op jit(solution)/shard_map/ppermute | solution.py:19
  228.8 4.9 %collective-permute-start.24 = (bf16[2,960,256]{2,1,0:T(8,128)(2,1)S(1)}, bf16[2,960,256]{2,1,0:T(8,128)(2,1)S(1)}, u32[]{:S(2)}, u32[]{:S(2)}) collective-permute-start(bf16[2,960,256]{2,1,0:T(8,128)(2,1)S(1)} %get-tuple-element.32), channel_id=1, source_target_pairs={{0,1},{1,0},{2,3},{3,2},{4,5},{5,4},{6,7},{7,6},{8,9},{9,8},{10,11... | collective-permute-start | bytes 2949128 | tf_op jit(solution)/shard_map/ppermute | solution.py:19
  229.2 5.9 %collective-permute-start.22 = (bf16[2,960,256]{2,1,0:T(8,128)(2,1)S(1)}, bf16[2,960,256]{2,1,0:T(8,128)(2,1)S(1)}, u32[]{:S(2)}, u32[]{:S(2)}) collective-permute-start(bf16[2,960,256]{2,1,0:T(8,128)(2,1)S(1)} %get-tuple-element.33), channel_id=1, source_target_pairs={{0,1},{1,0},{2,3},{3,2},{4,5},{5,4},{6,7},{7,6},{8,9},{9,8},{10,11... | collective-permute-start | bytes 2949128 | tf_op jit(solution)/shard_map/ppermute | solution.py:19
  230.9 4.2 %copy-start.15 = (bf16[2,960,256]{2,1,0:T(8,128)(2,1)}, bf16[2,960,256]{2,1,0:T(8,128)(2,1)S(1)}, u32[]{:S(2)}) copy-start(bf16[2,960,256]{2,1,0:T(8,128)(2,1)S(1)} %collective-permute-done.23) | copy-start | bytes 2949124
  232.3 2.8 copy-start.16
  245.8 18.2 %copy-start.13 = (bf16[2,960,256]{2,1,0:T(8,128)(2,1)S(1)}, bf16[2,960,256]{2,1,0:T(8,128)(2,1)}, u32[]{:S(2)}) copy-start(bf16[2,960,256]{2,1,0:T(8,128)(2,1)} %get-tuple-element.22) | copy-start | bytes 2949124
  245.8 13.7 %collective-permute-start.25 = (bf16[2,480,256]{2,1,0:T(8,128)(2,1)S(1)}, bf16[2,480,256]{2,1,0:T(8,128)(2,1)S(1)}, u32[]{:S(2)}, u32[]{:S(2)}) collective-permute-start(bf16[2,480,256]{2,1,0:T(8,128)(2,1)S(1)} %get-tuple-element.48), channel_id=1, source_target_pairs={{0,4},{4,8},{8,12},{12,0},{1,5},{5,9},{9,13},{13,1},{2,6},{6,10},{... | collective-permute-start | bytes 1474568 | tf_op jit(solution)/shard_map/ppermute | solution.py:19
  245.9 13.6 %collective-permute-start.27 = (bf16[2,480,256]{2,1,0:T(8,128)(2,1)S(1)}, bf16[2,480,256]{2,1,0:T(8,128)(2,1)S(1)}, u32[]{:S(2)}, u32[]{:S(2)}) collective-permute-start(bf16[2,480,256]{2,1,0:T(8,128)(2,1)S(1)} %get-tuple-element.49), channel_id=1, source_target_pairs={{0,12},{4,0},{8,4},{12,8},{1,13},{5,1},{9,5},{13,9},{2,14},{6,2},{... | collective-permute-start | bytes 1474568 | tf_op jit(solution)/shard_map/ppermute | solution.py:19
  259.5 16.6 %copy-start.9 = (f32[2,960,256]{2,1,0:T(8,128)S(1)}, f32[2,960,256]{2,1,0:T(8,128)}, u32[]{:S(2)}) copy-start(f32[2,960,256]{2,1,0:T(8,128)} %get-tuple-element.29) | copy-start | bytes 5898244
  261.4 15.3 %copy-start.12 = (bf16[960,1280]{1,0:T(8,128)(2,1)S(1)}, bf16[960,1280]{1,0:T(8,128)(2,1)}, u32[]{:S(2)}) copy-start(bf16[960,1280]{1,0:T(8,128)(2,1)} %get-tuple-element.37) | copy-start | bytes 7372804
  261.4 15.3 %copy-start.19 = (bf16[960,512]{1,0:T(8,128)(2,1)S(1)}, bf16[960,512]{1,0:T(8,128)(2,1)}, u32[]{:S(2)}) copy-start(bf16[960,512]{1,0:T(8,128)(2,1)} %get-tuple-element.43) | copy-start | bytes 2949124
  261.5 11.6 %collective-permute-start.31 = (bf16[960,256]{1,0:T(8,128)(2,1)S(1)}, bf16[960,256]{1,0:T(8,128)(2,1)S(1)}, u32[]{:S(2)}, u32[]{:S(2)}) collective-permute-start(bf16[960,256]{1,0:T(8,128)(2,1)S(1)} %pad_maximum_fusion.5), channel_id=1, source_target_pairs={{0,12},{4,0},{8,4},{12,8},{1,13},{5,1},{9,5},{13,9},{2,14},{6,2},{... | collective-permute-start | bytes 1474568 | tf_op jit(solution)/shard_map/ppermute | solution.py:19
  264.0 12.2 %collective-permute-start.30 = (bf16[960,256]{1,0:T(8,128)(2,1)S(1)}, bf16[960,256]{1,0:T(8,128)(2,1)S(1)}, u32[]{:S(2)}, u32[]{:S(2)}) collective-permute-start(bf16[960,256]{1,0:T(8,128)(2,1)S(1)} %pad_maximum_fusion.4), channel_id=1, source_target_pairs={{0,4},{4,8},{8,12},{12,0},{1,5},{5,9},{9,13},{13,1},{2,6},{6,10},{... | collective-permute-start | bytes 1474568 | tf_op jit(solution)/shard_map/ppermute | solution.py:19
  264.1 19.5 %collective-permute-start.28 = (bf16[960,256]{1,0:T(8,128)(2,1)S(1)}, bf16[960,256]{1,0:T(8,128)(2,1)S(1)}, u32[]{:S(2)}, u32[]{:S(2)}) collective-permute-start(bf16[960,256]{1,0:T(8,128)(2,1)S(1)} %pad_maximum_fusion.3), channel_id=1, source_target_pairs={{0,12},{4,0},{8,4},{12,8},{1,13},{5,1},{9,5},{13,9},{2,14},{6,2},{... | collective-permute-start | bytes 1474568 | tf_op jit(solution)/shard_map/ppermute | solution.py:19
  266.9 19.8 %collective-permute-start.26 = (bf16[960,256]{1,0:T(8,128)(2,1)S(1)}, bf16[960,256]{1,0:T(8,128)(2,1)S(1)}, u32[]{:S(2)}, u32[]{:S(2)}) collective-permute-start(bf16[960,256]{1,0:T(8,128)(2,1)S(1)} %pad_maximum_fusion.2), channel_id=1, source_target_pairs={{0,4},{4,8},{8,12},{12,0},{1,5},{5,9},{9,13},{13,1},{2,6},{6,10},{... | collective-permute-start | bytes 1474568 | tf_op jit(solution)/shard_map/ppermute | solution.py:19
  276.4 10.3 %collective-permute-start.32 = (bf16[960,256]{1,0:T(8,128)(2,1)S(1)}, bf16[960,256]{1,0:T(8,128)(2,1)S(1)}, u32[]{:S(2)}, u32[]{:S(2)}) collective-permute-start(bf16[960,256]{1,0:T(8,128)(2,1)S(1)} %fusion.14), channel_id=1, source_target_pairs={{0,2},{2,0},{1,3},{3,1},{4,6},{6,4},{5,7},{7,5},{8,10},{10,8},{9,1... | collective-permute-start | bytes 1474568 | tf_op jit(solution)/shard_map/ppermute | solution.py:19
  (7 other events, 8.9 us)

commit v2 on v0

v2 whole, which is shorter than its diff:
```python
import jax
import jax.numpy as jnp
from jax import lax
from jax.experimental import pallas as pl
from jax.experimental.pallas import tpu as pltpu
from jax.sharding import Mesh, PartitionSpec as P

inv_root_two = 0.7071067811865476
inv_root_tau = 0.3989422804014327

NZ, NX = 4, 4
LANES = 256
WIDTH_A = 1280
ROWS_AXES = ("y_lo", "z")
COLS_AXES = ("x", "y_hi", "core")
F32, BF16 = jnp.float32, jnp.bfloat16
VMEM_LIMIT = 62 * 2**20
PARTS = 2


CHEAP = pl.CostEstimate(flops=1000, bytes_accessed=1000, transcendentals=0)


def flops(n):
    return pl.CostEstimate(flops=n, bytes_accessed=1000, transcendentals=0)


DEAR = flops(4 * 10**10)


def shift(value, axis, by, size):
    pairs = [(i, (i + by) % size) for i in range(size)]
    return lax.ppermute(value, axis, pairs)


def after(value, *deps):
    return lax.optimization_barrier((value, *deps))[0]


def forward_early(places, late, core, mine, theirs, start, shards):
    tokens, width = start.shape
    panels = sum(p.shape[0] for p in mine)
    n, n_p, n_late = len(shards), len(mine), late.shape[0]
    rows = shards[0][0].shape[0]
    pieces = [a for shard in shards for a in shard]

    def kernel(places_ref, late_ref, core_ref, *refs):
        parts, (start_ref, *refs) = refs[: 2 * n_p], refs[2 * n_p :]
        w_refs = refs[: len(pieces)]
        total_ref, late_x_ref, mine_ref, theirs_ref, sems, late_sems = refs[len(pieces) :]
        i = pl.program_id(0)
        own = core_ref[0]
        out_copies = []
        for j in range(n_late):
            for k, buf in enumerate((mine_ref, theirs_ref)):
                column = pl.multiple_of((2 * j + jnp.where(own == k, 0, 1)) * LANES, LANES)
                out_copies.append(
                    pltpu.make_async_copy(
                        buf.at[late_ref[j]],
                        late_x_ref.at[:, pl.ds(column, LANES)],
                        late_sems.at[2 * j + k],
                    )
                )

        @pl.when(i == 0)
        def _():
            copies = []
            for k, buf in enumerate((mine_ref, theirs_ref)):
                to = 0
                for part in parts[k * n_p : (k + 1) * n_p]:
                    held = buf.at[pl.ds(to, part.shape[0])]
                    copies.append(pltpu.make_async_copy(part, held, sems.at[len(copies)]))
                    to += part.shape[0]
            for c in copies:
                c.start()
            for c in copies:
                c.wait()
            for c in out_copies:
                c.start()

        lo = pl.multiple_of(own * LANES, LANES)
        hi = pl.multiple_of((1 - own) * LANES, LANES)
        lhs = jnp.concatenate(
            [r[places_ref[j]] for j in range(n) for r in (mine_ref, theirs_ref)], axis=1
        )
        rhs, at = [], 0
        for shard in shards:
            held = w_refs[at : at + len(shard)]
            for o in (lo, hi):
                block = held[0][pl.ds(o, LANES), :]
                if len(shard) == 2:
                    edge = shard[0].shape[1] // LANES
                    block = jnp.where(i < edge, block, held[1][pl.ds(o, LANES), :])
                rhs.append(block)
            at += len(shard)
        rhs = jnp.concatenate(rhs, axis=0)
        total_ref[...] = start_ref[...] + jnp.dot(lhs, rhs, preferred_element_type=F32)

        @pl.when(i == pl.num_programs(0) - 1)
        def _():
            for c in out_copies:
                c.wait()

    def piece_specs(shard):
        if len(shard) == 1:
            return [pl.BlockSpec((rows, LANES), lambda i, *_: (0, i))]
        edge = shard[0].shape[1] // LANES
        return [
            pl.BlockSpec((rows, LANES), lambda i, *_: (0, jnp.minimum(i, edge - 1))),
            pl.BlockSpec((rows, LANES), lambda i, *_: (0, jnp.maximum(i - edge, 0))),
        ]

    tile = pl.BlockSpec((tokens, LANES), lambda i, *_: (0, i))
    hbm = pl.BlockSpec(memory_space=pl.ANY)
    return pl.pallas_call(
        kernel,
        grid_spec=pltpu.PrefetchScalarGridSpec(
            num_scalar_prefetch=3,
            grid=(width // LANES,),
            in_specs=[hbm] * (2 * n_p) + [tile] + [p for shard in shards for p in piece_specs(shard)],
            out_specs=[tile, hbm],
            scratch_shapes=[pltpu.VMEM((panels, tokens, LANES), BF16)] * 2
            + [pltpu.SemaphoreType.DMA((2 * n_p,)), pltpu.SemaphoreType.DMA((2 * n_late,))],
        ),
        out_shape=[
            jax.ShapeDtypeStruct((tokens, width), F32),
            jax.ShapeDtypeStruct((tokens, 2 * n_late * LANES), BF16),
        ],
        compiler_params=pltpu.CompilerParams(vmem_limit_bytes=VMEM_LIMIT),
        cost_estimate=CHEAP,
        name="early",
    )(places, late, core, *mine, *theirs, start, *pieces)


def forward_late(late_x, total, cotangent, shards, offset, dest, name):
    tokens, width = total.shape
    rows, cols = shards[0].shape
    n = len(shards)
    depth = late_x.shape[1]
    t = tokens // PARTS

    def kernel(x_ref, start_ref, cot_ref, *refs):
        w_refs, (act_ref, slope_ref) = refs[:n], refs[-2:]
        rhs = jnp.concatenate([w[...] for w in w_refs], axis=0)
        for p in range(PARTS):
            at = pl.ds(p * t, t)
            preact = start_ref[at, :] + jnp.dot(x_ref[at, :], rhs, preferred_element_type=F32)
            normal_cdf = 0.5 * (1.0 + lax.erf(preact * inv_root_two))
            normal_pdf = jnp.exp(-0.5 * preact * preact) * inv_root_tau
            act_ref[at, :] = (preact * normal_cdf).astype(BF16)
            slope = cot_ref[at, :].astype(F32) * (normal_cdf + preact * normal_pdf)
            slope_ref[at, :] = slope.astype(BF16)

    first = offset // LANES
    tile = pl.BlockSpec((tokens, LANES), lambda i: (0, i + first))
    return pl.pallas_call(
        kernel,
        grid=(cols // LANES,),
        in_specs=[pl.BlockSpec((tokens, depth), lambda i: (0, 0)), tile, tile]
        + [pl.BlockSpec((rows, LANES), lambda i: (0, i))] * n
        + [pl.BlockSpec(memory_space=pl.ANY)] * len(dest),
        out_specs=[tile, tile],
        out_shape=[jax.ShapeDtypeStruct((tokens, width), BF16)] * 2,
        input_output_aliases={3 + n + k: k for k in range(len(dest))},
        compiler_params=pltpu.CompilerParams(vmem_limit_bytes=VMEM_LIMIT),
        cost_estimate=CHEAP,
        name=name,
    )(late_x, total, cotangent, *shards, *dest)


def gradient(picks, core, slope, blocks, name):
    tokens, width = slope.shape
    rows = 2 * LANES
    n = picks.shape[0]
    arrays = [a for shard in blocks for a in shard]

    def kernel(picks_ref, core_ref, s_ref, *refs):
        a_refs, (mine_ref, theirs_ref, w_buf, sem) = refs[: len(arrays)], refs[len(arrays) :]
        i = pl.program_id(0)

        def fetch(step, slot):
            wanted = picks_ref[step]
            at = 0
            for j, shard in enumerate(blocks):
                held = a_refs[at : at + len(shard)]
                at += len(shard)

                @pl.when(wanted == j)
                def _():
                    to = 0
                    for ref in held:
                        w = ref.shape[1]
                        pltpu.make_async_copy(
                            ref, w_buf.at[slot, :, pl.ds(to, w)], sem.at[slot]
                        ).start()
                        to += w

        @pl.when(i == 0)
        def _():
            fetch(0, 0)

        @pl.when(i + 1 < n)
        def _():
            fetch(i + 1, (i + 1) % 2)

        slot = i % 2
        pltpu.make_async_copy(a_refs[0], w_buf.at[slot], sem.at[slot]).wait()
        own = core_ref[0]
        for half, out in ((own, mine_ref), (1 - own, theirs_ref)):
            part = w_buf[slot, pl.ds(pl.multiple_of(half * LANES, LANES), LANES), :]
            out[0] = lax.dot_general(
                s_ref[...], part, (((1,), (1,)), ((), ())), preferred_element_type=F32
            ).astype(BF16)

    out_block = pl.BlockSpec((1, tokens, LANES), lambda i, *_: (i, 0, 0))
    return pl.pallas_call(
        kernel,
        grid_spec=pltpu.PrefetchScalarGridSpec(
            num_scalar_prefetch=2,
            grid=(n,),
            in_specs=[pl.BlockSpec((tokens, width), lambda i, *_: (0, 0))]
            + [pl.BlockSpec(memory_space=pl.ANY)] * len(arrays),
            out_specs=[out_block, out_block],
            scratch_shapes=[pltpu.VMEM((2, rows, width), BF16), pltpu.SemaphoreType.DMA((2,))],
        ),
        out_shape=[jax.ShapeDtypeStruct((n, tokens, LANES), BF16)] * 2,
        compiler_params=pltpu.CompilerParams(vmem_limit_bytes=VMEM_LIMIT),
        cost_estimate=CHEAP,
        name=name,
    )(picks, core, slope, *arrays)


def cut_first(z_minus, z_plus):
    rows, width = z_minus.shape
    steps = 4

    def kernel(minus_ref, plus_ref, up_ref, down_ref):
        up_ref[...] = minus_ref[...]
        down_ref[...] = plus_ref[...]

    def block(at=0):
        return pl.BlockSpec((rows // 2 // steps, width), lambda i: (i + at, 0))

    return pl.pallas_call(
        kernel,
        grid=(steps,),
        in_specs=[block(), block(steps)],
        out_specs=[block()] * 2,
        out_shape=[jax.ShapeDtypeStruct((rows // 2, width), BF16)] * 2,
        cost_estimate=DEAR,
        name="cut_first",
    )(z_minus, z_plus)


def cut_far(far_a, far_b, width_a):
    half, width = far_a.shape

    def kernel(top_ref, low_ref, a_ref, b_ref):
        for k, ref in enumerate((top_ref, low_ref)):
            at = pl.ds(k * half, half)
            a_ref[at, :] = ref[:, :width_a]
            b_ref[at, :] = ref[:, width_a:]

    return pl.pallas_call(
        kernel,
        out_shape=[jax.ShapeDtypeStruct((2 * half, w), BF16) for w in (width_a, width - width_a)],
        cost_estimate=CHEAP,
        name="cut_far",
    )(far_a, far_b)


def mark(cost, *arrays):
    n = len(arrays)
    any_space = [pl.BlockSpec(memory_space=pl.ANY)] * n
    return pl.pallas_call(
        lambda *refs: None,
        in_specs=any_space,
        out_specs=any_space,
        out_shape=[jax.ShapeDtypeStruct(a.shape, a.dtype) for a in arrays],
        input_output_aliases={i: i for i in range(n)},
        cost_estimate=cost,
        name="mark",
    )(*arrays)


def add_up(mine, back, via_minus, via_plus, dyh, name):
    tokens, lanes = mine.shape[1:]
    steps = 2
    t = tokens // steps

    def kernel(mine_ref, back_ref, minus_ref, plus_ref, up_ref, down_ref, own_ref):
        first = pl.program_id(0) < steps // 2
        total = mine_ref[...].astype(F32) + back_ref[...].astype(F32)
        minus, plus = minus_ref[0].astype(F32), plus_ref[0].astype(F32)
        up_ref[...] = (total[0] + jnp.where(first, minus, 0.0)).astype(BF16)
        down_ref[...] = (total[1] + jnp.where(first, 0.0, plus)).astype(BF16)
        own_ref[...] = total[2]

    tile = pl.BlockSpec((t, lanes), lambda i: (i, 0))
    three = pl.BlockSpec((3, t, lanes), lambda i: (0, i, 0))
    last = steps // 2 - 1
    return pl.pallas_call(
        kernel,
        grid=(steps,),
        in_specs=[
            three,
            three,
            pl.BlockSpec((1, t, lanes), lambda i: (dyh, jnp.minimum(i, last), 0)),
            pl.BlockSpec((1, t, lanes), lambda i: (dyh, jnp.maximum(i - last - 1, 0), 0)),
        ],
        out_specs=[tile] * 3,
        out_shape=[jax.ShapeDtypeStruct((tokens, lanes), d) for d in (BF16, BF16, F32)],
        cost_estimate=CHEAP,
        name=name,
    )(mine, back, via_minus, via_plus)


def body(carried_sum, x_panels, w_panels, cotangent):
    y_lo, z = lax.axis_index("y_lo"), lax.axis_index("z")
    x, y_hi, core = lax.axis_index("x"), lax.axis_index("y_hi"), lax.axis_index("core")
    core_of = core.reshape(1).astype(jnp.int32)
    tokens, width = carried_sum.shape
    width_a, width_b = WIDTH_A, width - WIDTH_A
    rows = w_panels.shape[0]

    def panels_for(dy, dz):
        r = ((y_lo + dy) % 2) * NZ + (z + dz) % NZ
        dx = (r // 2 - x) % NX
        return (dx ^ (dx >> 1)) * 2 + (r % 2 - y_hi) % 2

    def places(*ds):
        return jnp.stack([panels_for(*d) for d in ds]).astype(jnp.int32)

    def block_for(dx, dyh):
        r = ((x + dx) % NX) * 2 + (y_hi + dyh) % 2
        return ((r // NZ - y_lo) % 2) * NZ + (r % NZ - z) % NZ

    def picks(*ds):
        return jnp.stack([block_for(*d) for d in ds]).astype(jnp.int32)

    w_a, w_b = w_panels[:, :width_a], w_panels[:, width_a:]
    z_minus = shift(w_panels, "z", 1, NZ)
    z_plus = shift(w_panels, "z", -1, NZ)
    other_a = shift(w_a, "y_lo", 1, 2)
    pair = mark(flops(38 * 10**9), jnp.stack([x_panels, shift(x_panels, "y_hi", 1, 2)]))[0]
    x_minus = shift(pair, "x", 1, NX)
    x_plus = shift(pair, "x", -1, NX)
    up, down = cut_first(z_minus, z_plus)
    other_a = mark(DEAR, other_a)[0]
    up, down, w_b, other_a, x_minus, x_plus = lax.optimization_barrier(
        (up, down, w_b, other_a, x_minus, x_plus)
    )
    far_top = shift(up, "z", 1, NZ)
    far_low = shift(down, "z", -1, NZ)
    near = jnp.concatenate([pair, x_plus, x_minus])
    near_theirs = shift(near, "core", 1, 2)
    other_b = shift(after(w_b, near_theirs), "y_lo", 1, 2)
    x_far = [shift(x_minus[0], "x", 1, NX), shift(x_plus[1], "x", -1, NX)]
    x_far = jnp.stack(x_far)
    mine = [near, x_far]
    theirs = [near_theirs, shift(x_far, "core", 1, 2)]
    far_a, far_b = cut_far(far_top, far_low, width_a)
    send_a = after(other_a, far_a, other_b)
    other_minus_a = shift(send_a, "z", 1, NZ)
    other_plus_a = shift(send_a, "z", -1, NZ)
    other_far_a = shift(far_a, "y_lo", 1, 2)
    total, late_x = forward_early(
        places((0, 0), (0, 1), (0, 3), (1, 0)),
        places((0, 2), (1, 1), (1, 3), (1, 2)),
        core_of, mine, theirs, carried_sum,
        [(w_panels,), (z_plus,), (z_minus,), (other_a, other_b)],
    )
    send_b, send_far_b = lax.optimization_barrier(
        (other_b, far_b, other_minus_a, other_plus_a, other_far_a, total)
    )[:2]
    other_minus_b = shift(send_b, "z", 1, NZ)
    other_plus_b = shift(send_b, "z", -1, NZ)
    other_far_b = shift(send_far_b, "y_lo", 1, 2)
    done = forward_late(
        late_x, total, cotangent, [far_a, other_plus_a, other_minus_a, other_far_a], 0, [], "gelu_a"
    )
    activated, slope = forward_late(
        late_x, total, cotangent, [far_b, other_plus_b, other_minus_b, other_far_b], width_a, done, "gelu_b"
    )
    blocks = [(w_panels,), (z_plus,), (far_a, far_b), (z_minus,), (other_a, other_b)]
    blocks += [(other_plus_a, other_plus_b), (other_far_a, other_far_b), (other_minus_a, other_minus_b)]

    half = tokens // 2
    m, t = gradient(picks((2, 0), (2, 1)), core_of, slope, blocks, "grad_far")
    far_sum = (m.astype(F32) + shift(t, "core", 1, 2).astype(F32)).astype(BF16)
    up, down = lax.optimization_barrier((far_sum[:, :half], far_sum[:, half:]))
    via_minus = shift(up, "x", 1, NX)
    via_plus = shift(down, "x", -1, NX)

    slope = after(slope, up, down)
    m, t = gradient(picks((1, 1), (3, 1), (0, 1)), core_of, slope, blocks, "grad_1")
    via_minus, via_plus = mark(DEAR, via_minus, via_plus)
    up, down, own_1 = add_up(m, shift(t, "core", 1, 2), via_minus, via_plus, 1, "add_1")
    got_1 = shift(up, "x", 1, NX), shift(down, "x", -1, NX)

    slope = after(slope, up, down)
    m, t = gradient(picks((1, 0), (3, 0), (0, 0)), core_of, slope, blocks, "grad_0")
    got_1 = mark(DEAR, *got_1)
    m, via_minus, *got_1 = lax.optimization_barrier((m, via_minus, *got_1))
    up, down, own_0 = add_up(m, shift(t, "core", 1, 2), via_minus, via_plus, 0, "add_0")
    got_0 = shift(up, "x", 1, NX), shift(down, "x", -1, NX)
    to_other = own_1 + got_1[0].astype(F32) + got_1[1].astype(F32)
    from_other = shift(to_other.astype(BF16), "y_hi", 1, 2)
    input_grad = own_0 + got_0[0].astype(F32) + got_0[1].astype(F32) + from_other.astype(F32)
    return activated, input_grad.astype(BF16)


def solution(mesh):
    fine = Mesh(mesh.devices.reshape(2, 4, 4, 2, 2), ROWS_AXES + COLS_AXES)
    spec = P(ROWS_AXES, COLS_AXES)
    return jax.shard_map(
        body,
        mesh=fine,
        in_specs=(spec, spec, spec, spec),
        out_specs=(spec, spec),
        check_vma=False,
    )
```

time: 390 us -> 225 us (0.58)
  waiting for transfers between devices: 329 us -> 69 us
  Pallas kernels: 0 us -> 83.3 us
  matrix products: 46.8 us -> 0 us
  starting transfers between devices: 0.11 us -> 39.9 us
  local copies, waits for them, and re-layouts: 0.01 us -> 19.4 us
  between operations: 13.7 us -> 0.83 us
  other arithmetic: 0 us -> 11.7 us
    all_gather x2 -> x0, waiting for transfers between devices: 233 us -> none  [the longest x1 151 us: body(): lax.all_gather(w_panels, 'row', axis=0, tiled=True)]
    reduce_scatter x1 -> x0, waiting for transfers between devices: 94.1 us -> none  [body(): lax.psum_scatter(partial_grad.astype(jnp.bfloat16), 'col', scatter_dimens...]
    pallas_call x0 -> x14, Pallas kernels: none -> 83.3 us  [the longest x3 31.4 us: gradient(): pl.pallas_call(kernel, grid_spec=pltpu.PrefetchScalarGridSpec(num_scalar_...]
    ppermute x0 -> x29, waiting for transfers between devices: none -> 69 us  [shift(): return lax.ppermute(value, axis, pairs)]
    dot_general x2 -> x0, matrix products: 46.8 us -> none  [the longest x1 23.4 us: body(): lax.dot_general(slope_grad, lax.all_gather(w_panels, 'row', axis=0, tiled...]
    ppermute x0 -> x29, starting transfers between devices: none -> 39.9 us  [shift(): return lax.ppermute(value, axis, pairs)]
    unnamed x2 -> x40, local copies, waits for them, and re-layouts: 0.01 us -> 12.3 us
    convert_element_type x0 -> x3, other arithmetic: none -> 5.03 us  [the longest x1 2.25 us: body(): return (activated, input_grad.astype(BF16))]
  transfers between devices with their start and end apart: 3 -> 29, of which waited for: 3 -> 14; matrix products, arithmetic and copies ran while one was open for 0% -> 6% of each run, Pallas kernels for 0% -> 28%
where the time goes in v2:
time: 225 us; the launch traced here: 224 us
  Pallas kernels  83.3 us (37%)
  waiting for transfers between devices  69 us (31%)
  starting transfers between devices  39.9 us (18%)
  local copies, waits for them, and re-layouts  19.4 us (9%)
  other arithmetic  11.7 us (5%)
    ppermute x29, waiting for transfers between devices, shift(): return lax.ppermute(value, axis, pairs)  69 us
    ppermute x29, starting transfers between devices, shift(): return lax.ppermute(value, axis, pairs)  39.9 us
    pallas_call x3, Pallas kernels, gradient(): pl.pallas_call(kernel, grid_spec=pltpu.PrefetchScalarGridSpec(num_scalar_...  31.4 us
    pallas_call x2, Pallas kernels, forward_late(): pl.pallas_call(kernel, grid=(cols // LANES,), in_specs=[pl.BlockSpec((tok...  20.9 us
    pallas_call x1, Pallas kernels, forward_early(): pl.pallas_call(kernel, grid_spec=pltpu.PrefetchScalarGridSpec(num_scalar_...  18.4 us
    unnamed x40, local copies, waits for them, and re-layouts  12.3 us
    pallas_call x2, Pallas kernels, add_up(): pl.pallas_call(kernel, grid=(steps,), in_specs=[three, three, pl.BlockSpe...  6.05 us
  transfers between devices with their start and end apart: 29, of which 14 were waited for; matrix products, arithmetic and copies ran while one was open for 6% of the time, Pallas kernels for 28%

profile of v2, /device:TPU:1, one launch (start us, length us, event | category | flops | bytes accessed | tf_op | source)
XLA Modules:
  0.0 224.1 jit_solution(11593139763619749845)
XLA Ops:
  0.6 3.8 %collective-permute-start = (bf16[960,256]{1,0:T(8,128)(2,1)}, bf16[960,256]{1,0:T(8,128)(2,1)S(1)}, u32[]{:S(2)}, u32[]{:S(2)}) collective-permute-start(bf16[960,256]{1,0:T(8,128)(2,1)} %param.5), channel_id=1, source_target_pairs={{0,2},{2,0},{1,3},{3,1},{4,6},{6,4},{5,7},{7,5},{8,10},{10,8},{9,1... | collective-permute-start | bytes 1474568 | tf_op jit(solution)/shard_map/ppermute | solution.py:33
  4.5 3.8 %collective-permute-start.2 = (bf16[512,1792]{1,0:T(8,128)(2,1)}, bf16[512,1792]{1,0:T(8,128)(2,1)S(1)}, u32[]{:S(2)}, u32[]{:S(2)}) collective-permute-start(bf16[512,1792]{1,0:T(8,128)(2,1)} %refs_0_.5), channel_id=1, source_target_pairs={{0,48},{16,0},{32,16},{48,32},{1,49},{17,1},{33,17},{49,33},{2,50}... | collective-permute-start | bytes 5505032 | tf_op jit(solution)/shard_map/ppermute | solution.py:33
  8.2 1.5 slice.19
  10.2 1.9 slice.18
  12.1 3.2 %collective-permute-done = bf16[960,256]{1,0:T(8,128)(2,1)S(1)} collective-permute-done((bf16[960,256]{1,0:T(8,128)(2,1)}, bf16[960,256]{1,0:T(8,128)(2,1)S(1)}, u32[]{:S(2)}, u32[]{:S(2)}) %collective-permute-start) | collective-permute-done | bytes 491552 | tf_op jit(solution)/shard_map/ppermute | solution.py:33
  16.4 2.5 %collective-permute-start.5 = (bf16[2,960,256]{2,1,0:T(8,128)(2,1)}, bf16[2,960,256]{2,1,0:T(8,128)(2,1)}, u32[]{:S(2)}, u32[]{:S(2)}) collective-permute-start(bf16[2,960,256]{2,1,0:T(8,128)(2,1)} %mark.4), channel_id=1, source_target_pairs={{0,12},{4,0},{8,4},{12,8},{1,13},{5,1},{9,5},{13,9},{2,14},{6,2},{... | collective-permute-start | bytes 2949128 | tf_op jit(solution)/shard_map/ppermute | solution.py:33
  18.9 25.0 %collective-permute-done.3.refs_0_ = bf16[512,1280]{1,0:T(8,128)(2,1)} collective-permute-done((bf16[512,1280]{1,0:T(8,128)(2,1)S(1)}, bf16[512,1280]{1,0:T(8,128)(2,1)}, u32[]{:S(2)}, u32[]{:S(2)}) %collective-permute-start.3) | collective-permute-done | bytes 1310752 | tf_op jit(solution)/shard_map/ppermute | solution.py:33
  43.9 3.0 %collective-permute-done.2.plus_ref.refs_6_.refs_1_ = bf16[512,1792]{1,0:T(8,128)(2,1)S(1)} collective-permute-done((bf16[512,1792]{1,0:T(8,128)(2,1)}, bf16[512,1792]{1,0:T(8,128)(2,1)S(1)}, u32[]{:S(2)}, u32[]{:S(2)}) %collective-permute-start.2) | collective-permute-done | bytes 1835040 | tf_op jit(solution)/shard_map/ppermute | solution.py:33
  46.9 3.1 %collective-permute-done.1.minus_ref.refs_7_.refs_4_ = bf16[512,1792]{1,0:T(8,128)(2,1)} collective-permute-done((bf16[512,1792]{1,0:T(8,128)(2,1)}, bf16[512,1792]{1,0:T(8,128)(2,1)}, u32[]{:S(2)}, u32[]{:S(2)}) %collective-permute-start.1) | collective-permute-done | bytes 1835040 | tf_op jit(solution)/shard_map/ppermute | solution.py:33
  50.0 3.8 %cut_first.1 = (bf16[256,1792]{1,0:T(8,128)(2,1)}, bf16[256,1792]{1,0:T(8,128)(2,1)}) custom-call(bf16[512,1792]{1,0:T(8,128)(2,1)} %collective-permute-done.1.minus_ref.refs_7_.refs_4_, bf16[512,1792]{1,0:T(8,128)(2,1)} %copy-done), custom_call_target="tpu_custom_call" | custom-call | flops 40000000000 | bytes 1000 | tf_op jit(solution)/shard_map/cut_first/pallas_call | solution.py:244
  53.8 1.9 pad_maximum_fusion.refs_0_
  55.8 1.6 copy-done.2
  57.4 2.2 collective-permute-start.8
  59.6 2.7 %collective-permute-start.12 = (bf16[256,1792]{1,0:T(8,128)(2,1)S(1)}, bf16[256,1792]{1,0:T(8,128)(2,1)S(1)}, u32[]{:S(2)}, u32[]{:S(2)}) collective-permute-start(bf16[256,1792]{1,0:T(8,128)(2,1)S(1)} %copy-done.18), channel_id=1, source_target_pairs={{0,48},{16,0},{32,16},{48,32},{1,49},{17,1},{33,17},{49,33},{2,50}... | collective-permute-start | bytes 2752520 | tf_op jit(solution)/shard_map/ppermute | solution.py:33
  62.2 1.8 slice_bitcast_fusion
  64.5 1.7 copy-done.7
  66.6 1.9 slice_bitcast_fusion.1
  68.5 1.2 collective-permute-start.6
  69.7 1.5 collective-permute-start.7
  71.1 11.7 %collective-permute-done.11.top_ref = bf16[256,1792]{1,0:T(8,128)(2,1)S(1)} collective-permute-done((bf16[256,1792]{1,0:T(8,128)(2,1)S(1)}, bf16[256,1792]{1,0:T(8,128)(2,1)S(1)}, u32[]{:S(2)}, u32[]{:S(2)}) %collective-permute-start.11) | collective-permute-done | bytes 917536 | tf_op jit(solution)/shard_map/ppermute | solution.py:33
  84.7 2.8 %cut_far.1 = (bf16[512,1280]{1,0:T(8,128)(2,1)}, bf16[512,512]{1,0:T(8,128)(2,1)}) custom-call(bf16[256,1792]{1,0:T(8,128)(2,1)} %copy-done.13, bf16[256,1792]{1,0:T(8,128)(2,1)} %copy-done.14), custom_call_target="tpu_custom_call" | custom-call | flops 1000 | bytes 1000 | tf_op jit(solution)/shard_map/cut_far/pallas_call | solution.py:264
  88.0 1.3 collective-permute-start.14
  89.4 1.3 pad_maximum_fusion.2.refs_1_
  91.7 1.5 collective-permute-start.9
  93.9 1.6 collective-permute-done.9.refs_3_
  95.5 18.4 %early.1 = (f32[960,1792]{1,0:T(8,128)}, bf16[960,2048]{1,0:T(8,128)(2,1)}) custom-call(s32[4]{0:T(128)} %get-tuple-element.92.places_ref, s32[4]{0:T(128)} %get-tuple-element.93.late_ref, s32[1]{0:T(128)} %bitcast.8.core_ref, bf16[6,960,256]{2,1,0:T(8,128)(2,1)} %copy-done.2, bf16[2,960,256]{2,1,0:T(8,128)(2,1)} %copy-done.5, ...), custom_call_target="tpu_custom_call" | custom-call | flops 1000 | bytes 1000 | tf_op jit(solution)/shard_map/early/pallas_call | solution.py:115
  113.9 3.6 %collective-permute-done.15.refs_3_.refs_9_ = bf16[512,1280]{1,0:T(8,128)(2,1)S(1)} collective-permute-done((bf16[512,1280]{1,0:T(8,128)(2,1)}, bf16[512,1280]{1,0:T(8,128)(2,1)S(1)}, u32[]{:S(2)}, u32[]{:S(2)}) %collective-permute-start.15) | collective-permute-done | bytes 1310752 | tf_op jit(solution)/shard_map/ppermute | solution.py:33
  117.6 1.8 collective-permute-done.13.refs_2_.refs_11_
  120.5 2.7 %collective-permute-start.16 = (bf16[512,512]{1,0:T(8,128)(2,1)}, bf16[512,512]{1,0:T(8,128)(2,1)}, u32[]{:S(2)}, u32[]{:S(2)}) collective-permute-start(bf16[512,512]{1,0:T(8,128)(2,1)} %copy-done.3), channel_id=1, source_target_pairs={{0,48},{16,0},{32,16},{48,32},{1,49},{17,1},{33,17},{49,33},{2,50}... | collective-permute-start | bytes 1572872 | tf_op jit(solution)/shard_map/ppermute | solution.py:33
  123.7 13.3 %gelu_a.1 = (bf16[960,1792]{1,0:T(8,128)(2,1)}, bf16[960,1792]{1,0:T(8,128)(2,1)}) custom-call(bf16[960,2048]{1,0:T(8,128)(2,1)} %get-tuple-element.53.x_ref, f32[960,1792]{1,0:T(8,128)} %get-tuple-element.54.start_ref, bf16[960,1792]{1,0:T(8,128)(2,1)} %cot_ref.3, bf16[512,1280]{1,0:T(8,128)(2,1)} %get-tuple-element.58.refs_0_.refs_2_, ...), custom_call_target="tpu_custom_call" | custom-call | flops 1000 | bytes 1000 | tf_op jit(solution)/shard_map/gelu_a/pallas_call | solution.py:156
  137.9 7.6 %gelu_b.1 = (bf16[960,1792]{1,0:T(8,128)(2,1)}, bf16[960,1792]{1,0:T(8,128)(2,1)}) custom-call(bf16[960,2048]{1,0:T(8,128)(2,1)} %get-tuple-element.53.x_ref, f32[960,1792]{1,0:T(8,128)} %get-tuple-element.54.start_ref, bf16[960,1792]{1,0:T(8,128)(2,1)} %cot_ref.3, ...), custom_call_target="tpu_custom_call", output_to_operand_aliasing={{0}: (7, {}), {1}: (8, {})} | custom-call | flops 1000 | bytes 1000 | tf_op jit(solution)/shard_map/gelu_b/pallas_call | solution.py:156
  145.5 9.1 %grad_far.1 = (bf16[2,960,256]{2,1,0:T(8,128)(2,1)}, bf16[2,960,256]{2,1,0:T(8,128)(2,1)}) custom-call(s32[2]{0:T(128)} %pad_add_fusion.3.picks_ref, s32[1]{0:T(128)} %bitcast.8.core_ref, bf16[960,1792]{1,0:T(8,128)(2,1)} %get-tuple-element.77.s_ref, bf16[512,1792]{1,0:T(8,128)(2,1)} %refs_0_.5, bf16[512,1792]{1,0:T(8,128)(2,1)} %copy-done, ...), custom_call_target="tpu_custom_call" | custom-call | flops 1000 | bytes 1000 | tf_op jit(solution)/shard_map/grad_far/pallas_call | solution.py:216
  154.5 3.5 %collective-permute-start.19 = (bf16[2,960,256]{2,1,0:T(8,128)(2,1)}, bf16[2,960,256]{2,1,0:T(8,128)(2,1)S(1)}, u32[]{:S(2)}, u32[]{:S(2)}) collective-permute-start(bf16[2,960,256]{2,1,0:T(8,128)(2,1)} %get-tuple-element.67), channel_id=1, source_target_pairs={{0,1},{1,0},{2,3},{3,2},{4,5},{5,4},{6,7},{7,6},{8,9},{9,8},{10,11... | collective-permute-start | bytes 2949128 | tf_op jit(solution)/shard_map/ppermute | solution.py:33
  158.0 2.4 %collective-permute-done.19 = bf16[2,960,256]{2,1,0:T(8,128)(2,1)S(1)} collective-permute-done((bf16[2,960,256]{2,1,0:T(8,128)(2,1)}, bf16[2,960,256]{2,1,0:T(8,128)(2,1)S(1)}, u32[]{:S(2)}, u32[]{:S(2)}) %collective-permute-start.19) | collective-permute-done | bytes 983072 | tf_op jit(solution)/shard_map/ppermute | solution.py:33
  160.4 1.5 add_convert_fusion
  162.0 1.3 collective-permute-start.21
  163.3 1.5 collective-permute-start.22
  165.3 11.2 %grad_1.1 = (bf16[3,960,256]{2,1,0:T(8,128)(2,1)}, bf16[3,960,256]{2,1,0:T(8,128)(2,1)}) custom-call(s32[3]{0:T(128)} %pad_add_fusion.4.picks_ref, s32[1]{0:T(128)} %bitcast.8.core_ref, bf16[960,1792]{1,0:T(8,128)(2,1)} %get-tuple-element.77.s_ref, bf16[512,1792]{1,0:T(8,128)(2,1)} %refs_0_.5, bf16[512,1792]{1,0:T(8,128)(2,1)} %copy-done, ...), custom_call_target="tpu_custom_call" | custom-call | flops 1000 | bytes 1000 | tf_op jit(solution)/shard_map/grad_1/pallas_call | solution.py:216
  179.1 1.5 collective-permute-done.20.back_ref
  181.7 3.0 %add_1.1 = (bf16[960,256]{1,0:T(8,128)(2,1)}, bf16[960,256]{1,0:T(8,128)(2,1)}, f32[960,256]{1,0:T(8,128)}) custom-call(bf16[3,960,256]{2,1,0:T(8,128)(2,1)} %get-tuple-element.71.mine_ref, bf16[3,960,256]{2,1,0:T(8,128)(2,1)} %copy-done.11, bf16[2,480,256]{2,1,0:T(8,128)(2,1)} %get-tuple-element.83.minus_ref, bf16[2,480,256]{2,1,0:T(8,128)(2,1)} %get-tuple-element.74.plus_ref), custom_call_target="tpu_custom_call" | custom-call | flops 1000 | bytes 1000 | tf_op jit(solution)/shard_map/add_1/pallas_call | solution.py:302
  184.8 2.7 %collective-permute-start.24 = (bf16[960,256]{1,0:T(8,128)(2,1)}, bf16[960,256]{1,0:T(8,128)(2,1)S(1)}, u32[]{:S(2)}, u32[]{:S(2)}) collective-permute-start(bf16[960,256]{1,0:T(8,128)(2,1)} %get-tuple-element.76), channel_id=1, source_target_pairs={{0,12},{4,0},{8,4},{12,8},{1,13},{5,1},{9,5},{13,9},{2,14},{6,2},{... | collective-permute-start | bytes 1474568 | tf_op jit(solution)/shard_map/ppermute | solution.py:33
  188.0 11.1 %grad_0.1 = (bf16[3,960,256]{2,1,0:T(8,128)(2,1)}, bf16[3,960,256]{2,1,0:T(8,128)(2,1)}) custom-call(s32[3]{0:T(128)} %pad_add_fusion.2.picks_ref, s32[1]{0:T(128)} %bitcast.8.core_ref, bf16[960,1792]{1,0:T(8,128)(2,1)} %get-tuple-element.77.s_ref, bf16[512,1792]{1,0:T(8,128)(2,1)} %refs_0_.5, bf16[512,1792]{1,0:T(8,128)(2,1)} %copy-done, ...), custom_call_target="tpu_custom_call" | custom-call | flops 1000 | bytes 1000 | tf_op jit(solution)/shard_map/grad_0/pallas_call | solution.py:216
  201.8 1.3 add_convert_fusion.2
  204.9 3.0 %add_0.1 = (bf16[960,256]{1,0:T(8,128)(2,1)}, bf16[960,256]{1,0:T(8,128)(2,1)}, f32[960,256]{1,0:T(8,128)}) custom-call(bf16[3,960,256]{2,1,0:T(8,128)(2,1)} %get-tuple-element.81.mine_ref, bf16[3,960,256]{2,1,0:T(8,128)(2,1)} %copy-done.10, bf16[2,480,256]{2,1,0:T(8,128)(2,1)} %get-tuple-element.83.minus_ref, bf16[2,480,256]{2,1,0:T(8,128)(2,1)} %get-tuple-element.74.plus_ref), custom_call_target="tpu_custom_call" | custom-call | flops 1000 | bytes 1000 | tf_op jit(solution)/shard_map/add_0/pallas_call | solution.py:302
  207.9 2.7 %collective-permute-start.27 = (bf16[960,256]{1,0:T(8,128)(2,1)}, bf16[960,256]{1,0:T(8,128)(2,1)S(1)}, u32[]{:S(2)}, u32[]{:S(2)}) collective-permute-start(bf16[960,256]{1,0:T(8,128)(2,1)} %get-tuple-element.86), channel_id=1, source_target_pairs={{0,12},{4,0},{8,4},{12,8},{1,13},{5,1},{9,5},{13,9},{2,14},{6,2},{... | collective-permute-start | bytes 1474568 | tf_op jit(solution)/shard_map/ppermute | solution.py:33
  210.6 6.9 %collective-permute-done.28 = bf16[960,256]{1,0:T(8,128)(2,1)S(1)} collective-permute-done((bf16[960,256]{1,0:T(8,128)(2,1)S(1)}, bf16[960,256]{1,0:T(8,128)(2,1)S(1)}, u32[]{:S(2)}, u32[]{:S(2)}) %collective-permute-start.28) | collective-permute-done | bytes 491552 | tf_op jit(solution)/shard_map/ppermute | solution.py:33
  217.5 4.3 %collective-permute-done.26 = bf16[960,256]{1,0:T(8,128)(2,1)S(1)} collective-permute-done((bf16[960,256]{1,0:T(8,128)(2,1)}, bf16[960,256]{1,0:T(8,128)(2,1)S(1)}, u32[]{:S(2)}, u32[]{:S(2)}) %collective-permute-start.26) | collective-permute-done | bytes 491552 | tf_op jit(solution)/shard_map/ppermute | solution.py:33
  221.9 2.2 %add_convert_fusion.1 = bf16[960,256]{1,0:T(8,128)(2,1)} fusion(bf16[960,256]{1,0:T(8,128)(2,1)S(1)} %collective-permute-done.28, bf16[960,256]{1,0:T(8,128)(2,1)S(1)} %collective-permute-done.27, f32[960,256]{1,0:T(8,128)} %get-tuple-element.84, bf16[960,256]{1,0:T(8,128)(2,1)S(1)} %collective-permute-done.26), kind=kLoop, calls=%fused_computation.4 | loop fusion | flops 1720320 | bytes 2949120 | tf_op jit(solution)/shard_map/convert_element_type | solution.py:410
  (79 shorter events, 18.3 us)
Async XLA Ops:
  0.6 14.7 %copy-start.17 = (bf16[960,256]{1,0:T(8,128)(2,1)S(1)}, bf16[960,256]{1,0:T(8,128)(2,1)}, u32[]{:S(2)}) copy-start(bf16[960,256]{1,0:T(8,128)(2,1)} %param.5) | copy-start | bytes 1474564
  0.6 14.7 %collective-permute-start = (bf16[960,256]{1,0:T(8,128)(2,1)}, bf16[960,256]{1,0:T(8,128)(2,1)S(1)}, u32[]{:S(2)}, u32[]{:S(2)}) collective-permute-start(bf16[960,256]{1,0:T(8,128)(2,1)} %param.5), channel_id=1, source_target_pairs={{0,2},{2,0},{1,3},{3,1},{4,6},{6,4},{5,7},{7,5},{8,10},{10,8},{9,1... | collective-permute-start | bytes 1474568 | tf_op jit(solution)/shard_map/ppermute | solution.py:33
  4.5 42.4 %collective-permute-start.2 = (bf16[512,1792]{1,0:T(8,128)(2,1)}, bf16[512,1792]{1,0:T(8,128)(2,1)S(1)}, u32[]{:S(2)}, u32[]{:S(2)}) collective-permute-start(bf16[512,1792]{1,0:T(8,128)(2,1)} %refs_0_.5), channel_id=1, source_target_pairs={{0,48},{16,0},{32,16},{48,32},{1,49},{17,1},{33,17},{49,33},{2,50}... | collective-permute-start | bytes 5505032 | tf_op jit(solution)/shard_map/ppermute | solution.py:33
  8.2 41.8 %collective-permute-start.1 = (bf16[512,1792]{1,0:T(8,128)(2,1)}, bf16[512,1792]{1,0:T(8,128)(2,1)}, u32[]{:S(2)}, u32[]{:S(2)}) collective-permute-start(bf16[512,1792]{1,0:T(8,128)(2,1)} %refs_0_.5), channel_id=1, source_target_pairs={{0,16},{16,32},{32,48},{48,0},{1,17},{17,33},{33,49},{49,1},{2,18}... | collective-permute-start | bytes 5505032 | tf_op jit(solution)/shard_map/ppermute | solution.py:33
  9.7 34.2 %collective-permute-start.3 = (bf16[512,1280]{1,0:T(8,128)(2,1)S(1)}, bf16[512,1280]{1,0:T(8,128)(2,1)}, u32[]{:S(2)}, u32[]{:S(2)}) collective-permute-start(bf16[512,1280]{1,0:T(8,128)(2,1)S(1)} %slice.19), channel_id=1, source_target_pairs={{0,64},{64,0},{1,65},{65,1},{2,66},{66,2},{3,67},{67,3},{4,68},{68... | collective-permute-start | bytes 3932168 | tf_op jit(solution)/shard_map/ppermute | solution.py:33
  16.4 37.4 %collective-permute-start.5 = (bf16[2,960,256]{2,1,0:T(8,128)(2,1)}, bf16[2,960,256]{2,1,0:T(8,128)(2,1)}, u32[]{:S(2)}, u32[]{:S(2)}) collective-permute-start(bf16[2,960,256]{2,1,0:T(8,128)(2,1)} %mark.4), channel_id=1, source_target_pairs={{0,12},{4,0},{8,4},{12,8},{1,13},{5,1},{9,5},{13,9},{2,14},{6,2},{... | collective-permute-start | bytes 2949128 | tf_op jit(solution)/shard_map/ppermute | solution.py:33
  18.9 34.9 %collective-permute-start.4 = (bf16[2,960,256]{2,1,0:T(8,128)(2,1)}, bf16[2,960,256]{2,1,0:T(8,128)(2,1)}, u32[]{:S(2)}, u32[]{:S(2)}) collective-permute-start(bf16[2,960,256]{2,1,0:T(8,128)(2,1)} %mark.4), channel_id=1, source_target_pairs={{0,4},{4,8},{8,12},{12,0},{1,5},{5,9},{9,13},{13,1},{2,6},{6,10},{... | collective-permute-start | bytes 2949128 | tf_op jit(solution)/shard_map/ppermute | solution.py:33
  43.9 9.9 %copy-start.6 = (bf16[2,960,256]{2,1,0:T(8,128)(2,1)S(1)}, bf16[2,960,256]{2,1,0:T(8,128)(2,1)}, u32[]{:S(2)}) copy-start(bf16[2,960,256]{2,1,0:T(8,128)(2,1)} %mark.4) | copy-start | bytes 2949124
  46.9 3.1 %copy-start = (bf16[512,1792]{1,0:T(8,128)(2,1)}, bf16[512,1792]{1,0:T(8,128)(2,1)S(1)}, u32[]{:S(2)}) copy-start(bf16[512,1792]{1,0:T(8,128)(2,1)S(1)} %collective-permute-done.2.plus_ref.refs_6_.refs_1_) | copy-start | bytes 5505028
  53.8 5.7 %copy-start.19 = (bf16[256,1792]{1,0:T(8,128)(2,1)S(1)}, bf16[256,1792]{1,0:T(8,128)(2,1)}, u32[]{:S(2)}) copy-start(bf16[256,1792]{1,0:T(8,128)(2,1)} %get-tuple-element.55) | copy-start | bytes 2752516
  53.8 5.7 %copy-start.18 = (bf16[256,1792]{1,0:T(8,128)(2,1)S(1)}, bf16[256,1792]{1,0:T(8,128)(2,1)}, u32[]{:S(2)}) copy-start(bf16[256,1792]{1,0:T(8,128)(2,1)} %get-tuple-element.56) | copy-start | bytes 2752516
  55.8 1.6 copy-start.2
  57.4 7.2 %collective-permute-start.8 = (bf16[6,960,256]{2,1,0:T(8,128)(2,1)S(1)}, bf16[6,960,256]{2,1,0:T(8,128)(2,1)S(1)}, u32[]{:S(2)}, u32[]{:S(2)}) collective-permute-start(bf16[6,960,256]{2,1,0:T(8,128)(2,1)S(1)} %pad_maximum_fusion.refs_0_), channel_id=1, source_target_pairs={{0,1},{1,0},{2,3},{3,2},{4,5},{5,4},{6,7},{7,6},{8,9},{9,8},{10,11... | collective-permute-start | bytes 8847368 | tf_op jit(solution)/shard_map/ppermute | solution.py:33
  59.5 23.3 %collective-permute-start.11 = (bf16[256,1792]{1,0:T(8,128)(2,1)S(1)}, bf16[256,1792]{1,0:T(8,128)(2,1)S(1)}, u32[]{:S(2)}, u32[]{:S(2)}) collective-permute-start(bf16[256,1792]{1,0:T(8,128)(2,1)S(1)} %copy-done.19), channel_id=1, source_target_pairs={{0,16},{16,32},{32,48},{48,0},{1,17},{17,33},{33,49},{49,1},{2,18}... | collective-permute-start | bytes 2752520 | tf_op jit(solution)/shard_map/ppermute | solution.py:33
  59.6 23.3 %collective-permute-start.12 = (bf16[256,1792]{1,0:T(8,128)(2,1)S(1)}, bf16[256,1792]{1,0:T(8,128)(2,1)S(1)}, u32[]{:S(2)}, u32[]{:S(2)}) collective-permute-start(bf16[256,1792]{1,0:T(8,128)(2,1)S(1)} %copy-done.18), channel_id=1, source_target_pairs={{0,48},{16,0},{32,16},{48,32},{1,49},{17,1},{33,17},{49,33},{2,50}... | collective-permute-start | bytes 2752520 | tf_op jit(solution)/shard_map/ppermute | solution.py:33
  64.5 1.7 copy-start.7
  66.2 21.7 %collective-permute-start.10 = (bf16[512,512]{1,0:T(8,128)(2,1)}, bf16[512,512]{1,0:T(8,128)(2,1)S(1)}, u32[]{:S(2)}, u32[]{:S(2)}) collective-permute-start(bf16[512,512]{1,0:T(8,128)(2,1)} %slice.18), channel_id=1, source_target_pairs={{0,64},{64,0},{1,65},{65,1},{2,66},{66,2},{3,67},{67,3},{4,68},{68... | collective-permute-start | bytes 1572872 | tf_op jit(solution)/shard_map/ppermute | solution.py:33
  68.5 21.0 %collective-permute-start.6 = (bf16[960,256]{1,0:T(8,128)(2,1)}, bf16[960,256]{1,0:T(8,128)(2,1)}, u32[]{:S(2)}, u32[]{:S(2)}) collective-permute-start(bf16[960,256]{1,0:T(8,128)(2,1)} %slice_bitcast_fusion.1), channel_id=1, source_target_pairs={{0,4},{4,8},{8,12},{12,0},{1,5},{5,9},{9,13},{13,1},{2,6},{6,10},{... | collective-permute-start | bytes 1474568 | tf_op jit(solution)/shard_map/ppermute | solution.py:33
  69.7 19.8 %collective-permute-start.7 = (bf16[960,256]{1,0:T(8,128)(2,1)}, bf16[960,256]{1,0:T(8,128)(2,1)}, u32[]{:S(2)}, u32[]{:S(2)}) collective-permute-start(bf16[960,256]{1,0:T(8,128)(2,1)} %slice_bitcast_fusion), channel_id=1, source_target_pairs={{0,12},{4,0},{8,4},{12,8},{1,13},{5,1},{9,5},{13,9},{2,14},{6,2},{... | collective-permute-start | bytes 1474568 | tf_op jit(solution)/shard_map/ppermute | solution.py:33
  82.8 1.0 copy-start.13
  83.8 0.9 copy-start.14
  87.6 30.0 %collective-permute-start.15 = (bf16[512,1280]{1,0:T(8,128)(2,1)}, bf16[512,1280]{1,0:T(8,128)(2,1)S(1)}, u32[]{:S(2)}, u32[]{:S(2)}) collective-permute-start(bf16[512,1280]{1,0:T(8,128)(2,1)} %get-tuple-element.58.refs_0_.refs_2_), channel_id=1, source_target_pairs={{0,64},{64,0},{1,65},{65,1},{2,66},{66,2},{3,67},{67,3},{4,68},{68... | collective-permute-start | bytes 3932168 | tf_op jit(solution)/shard_map/ppermute | solution.py:33
  88.0 7.5 %copy-start.3 = (bf16[512,512]{1,0:T(8,128)(2,1)}, bf16[512,512]{1,0:T(8,128)(2,1)S(1)}, u32[]{:S(2)}) copy-start(bf16[512,512]{1,0:T(8,128)(2,1)S(1)} %collective-permute-done.10.refs_9_.refs_6_) | copy-start | bytes 1572868
  88.0 29.6 %collective-permute-start.14 = (bf16[512,1280]{1,0:T(8,128)(2,1)}, bf16[512,1280]{1,0:T(8,128)(2,1)}, u32[]{:S(2)}, u32[]{:S(2)}) collective-permute-start(bf16[512,1280]{1,0:T(8,128)(2,1)} %mark.5.refs_8_.refs_5_), channel_id=1, source_target_pairs={{0,48},{16,0},{32,16},{48,32},{1,49},{17,1},{33,17},{49,33},{2,50}... | collective-permute-start | bytes 3932168 | tf_op jit(solution)/shard_map/ppermute | solution.py:33
  89.3 30.1 %collective-permute-start.13 = (bf16[512,1280]{1,0:T(8,128)(2,1)}, bf16[512,1280]{1,0:T(8,128)(2,1)}, u32[]{:S(2)}, u32[]{:S(2)}) collective-permute-start(bf16[512,1280]{1,0:T(8,128)(2,1)} %mark.5.refs_8_.refs_5_), channel_id=1, source_target_pairs={{0,16},{16,32},{32,48},{48,0},{1,17},{17,33},{33,49},{49,1},{2,18}... | collective-permute-start | bytes 3932168 | tf_op jit(solution)/shard_map/ppermute | solution.py:33
  90.7 1.0 copy-start.5
  91.7 3.8 %collective-permute-start.9 = (bf16[2,960,256]{2,1,0:T(8,128)(2,1)S(1)}, bf16[2,960,256]{2,1,0:T(8,128)(2,1)}, u32[]{:S(2)}, u32[]{:S(2)}) collective-permute-start(bf16[2,960,256]{2,1,0:T(8,128)(2,1)S(1)} %pad_maximum_fusion.2.refs_1_), channel_id=1, source_target_pairs={{0,1},{1,0},{2,3},{3,2},{4,5},{5,4},{6,7},{7,6},{8,9},{9,8},{10,11... | collective-permute-start | bytes 2949128 | tf_op jit(solution)/shard_map/ppermute | solution.py:33
  117.5 6.2 %copy-start.1 = (bf16[512,1280]{1,0:T(8,128)(2,1)}, bf16[512,1280]{1,0:T(8,128)(2,1)S(1)}, u32[]{:S(2)}) copy-start(bf16[512,1280]{1,0:T(8,128)(2,1)S(1)} %collective-permute-done.15.refs_3_.refs_9_) | copy-start | bytes 3932164
  119.4 17.7 %collective-permute-start.18 = (bf16[512,512]{1,0:T(8,128)(2,1)}, bf16[512,512]{1,0:T(8,128)(2,1)S(1)}, u32[]{:S(2)}, u32[]{:S(2)}) collective-permute-start(bf16[512,512]{1,0:T(8,128)(2,1)} %get-tuple-element.61.refs_0_.refs_3_), channel_id=1, source_target_pairs={{0,64},{64,0},{1,65},{65,1},{2,66},{66,2},{3,67},{67,3},{4,68},{68... | collective-permute-start | bytes 1572872 | tf_op jit(solution)/shard_map/ppermute | solution.py:33
  120.5 16.6 %collective-permute-start.17 = (bf16[512,512]{1,0:T(8,128)(2,1)}, bf16[512,512]{1,0:T(8,128)(2,1)}, u32[]{:S(2)}, u32[]{:S(2)}) collective-permute-start(bf16[512,512]{1,0:T(8,128)(2,1)} %copy-done.3), channel_id=1, source_target_pairs={{0,16},{16,32},{32,48},{48,0},{1,17},{17,33},{33,49},{49,1},{2,18}... | collective-permute-start | bytes 1572872 | tf_op jit(solution)/shard_map/ppermute | solution.py:33
  120.5 16.6 %collective-permute-start.16 = (bf16[512,512]{1,0:T(8,128)(2,1)}, bf16[512,512]{1,0:T(8,128)(2,1)}, u32[]{:S(2)}, u32[]{:S(2)}) collective-permute-start(bf16[512,512]{1,0:T(8,128)(2,1)} %copy-done.3), channel_id=1, source_target_pairs={{0,48},{16,0},{32,16},{48,32},{1,49},{17,1},{33,17},{49,33},{2,50}... | collective-permute-start | bytes 1572872 | tf_op jit(solution)/shard_map/ppermute | solution.py:33
  137.1 0.8 copy-start.4
  154.5 5.9 %collective-permute-start.19 = (bf16[2,960,256]{2,1,0:T(8,128)(2,1)}, bf16[2,960,256]{2,1,0:T(8,128)(2,1)S(1)}, u32[]{:S(2)}, u32[]{:S(2)}) collective-permute-start(bf16[2,960,256]{2,1,0:T(8,128)(2,1)} %get-tuple-element.67), channel_id=1, source_target_pairs={{0,1},{1,0},{2,3},{3,2},{4,5},{5,4},{6,7},{7,6},{8,9},{9,8},{10,11... | collective-permute-start | bytes 2949128 | tf_op jit(solution)/shard_map/ppermute | solution.py:33
  162.0 15.5 %collective-permute-start.21 = (bf16[2,480,256]{2,1,0:T(8,128)(2,1)S(1)}, bf16[2,480,256]{2,1,0:T(8,128)(2,1)S(1)}, u32[]{:S(2)}, u32[]{:S(2)}) collective-permute-start(bf16[2,480,256]{2,1,0:T(8,128)(2,1)S(1)} %get-tuple-element.68), channel_id=1, source_target_pairs={{0,4},{4,8},{8,12},{12,0},{1,5},{5,9},{9,13},{13,1},{2,6},{6,10},{... | collective-permute-start | bytes 1474568 | tf_op jit(solution)/shard_map/ppermute | solution.py:33
  163.3 14.3 %collective-permute-start.22 = (bf16[2,480,256]{2,1,0:T(8,128)(2,1)S(1)}, bf16[2,480,256]{2,1,0:T(8,128)(2,1)S(1)}, u32[]{:S(2)}, u32[]{:S(2)}) collective-permute-start(bf16[2,480,256]{2,1,0:T(8,128)(2,1)S(1)} %get-tuple-element.69), channel_id=1, source_target_pairs={{0,12},{4,0},{8,4},{12,8},{1,13},{5,1},{9,5},{13,9},{2,14},{6,2},{... | collective-permute-start | bytes 1474568 | tf_op jit(solution)/shard_map/ppermute | solution.py:33
  176.5 4.1 %collective-permute-start.20 = (bf16[3,960,256]{2,1,0:T(8,128)(2,1)}, bf16[3,960,256]{2,1,0:T(8,128)(2,1)S(1)}, u32[]{:S(2)}, u32[]{:S(2)}) collective-permute-start(bf16[3,960,256]{2,1,0:T(8,128)(2,1)} %get-tuple-element.72), channel_id=1, source_target_pairs={{0,1},{1,0},{2,3},{3,2},{4,5},{5,4},{6,7},{7,6},{8,9},{9,8},{10,11... | collective-permute-start | bytes 4423688 | tf_op jit(solution)/shard_map/ppermute | solution.py:33
  177.5 0.8 copy-start.8
  180.6 1.1 copy-start.11
  184.8 15.4 %collective-permute-start.23 = (bf16[960,256]{1,0:T(8,128)(2,1)}, bf16[960,256]{1,0:T(8,128)(2,1)S(1)}, u32[]{:S(2)}, u32[]{:S(2)}) collective-permute-start(bf16[960,256]{1,0:T(8,128)(2,1)} %get-tuple-element.75), channel_id=1, source_target_pairs={{0,4},{4,8},{8,12},{12,0},{1,5},{5,9},{9,13},{13,1},{2,6},{6,10},{... | collective-permute-start | bytes 1474568 | tf_op jit(solution)/shard_map/ppermute | solution.py:33
  184.8 15.4 %collective-permute-start.24 = (bf16[960,256]{1,0:T(8,128)(2,1)}, bf16[960,256]{1,0:T(8,128)(2,1)S(1)}, u32[]{:S(2)}, u32[]{:S(2)}) collective-permute-start(bf16[960,256]{1,0:T(8,128)(2,1)} %get-tuple-element.76), channel_id=1, source_target_pairs={{0,12},{4,0},{8,4},{12,8},{1,13},{5,1},{9,5},{13,9},{2,14},{6,2},{... | collective-permute-start | bytes 1474568 | tf_op jit(solution)/shard_map/ppermute | solution.py:33
  199.2 2.6 %copy-start.12 = (f32[960,256]{1,0:T(8,128)S(1)}, f32[960,256]{1,0:T(8,128)}, u32[]{:S(2)}) copy-start(f32[960,256]{1,0:T(8,128)} %get-tuple-element.87) | copy-start | bytes 2949124
  199.2 4.6 %collective-permute-start.25 = (bf16[3,960,256]{2,1,0:T(8,128)(2,1)}, bf16[3,960,256]{2,1,0:T(8,128)(2,1)S(1)}, u32[]{:S(2)}, u32[]{:S(2)}) collective-permute-start(bf16[3,960,256]{2,1,0:T(8,128)(2,1)} %get-tuple-element.82), channel_id=1, source_target_pairs={{0,1},{1,0},{2,3},{3,2},{4,5},{5,4},{6,7},{7,6},{8,9},{9,8},{10,11... | collective-permute-start | bytes 4423688 | tf_op jit(solution)/shard_map/ppermute | solution.py:33
  200.2 0.8 copy-start.15
  201.0 0.8 copy-start.16
  203.1 14.4 %collective-permute-start.28 = (bf16[960,256]{1,0:T(8,128)(2,1)S(1)}, bf16[960,256]{1,0:T(8,128)(2,1)S(1)}, u32[]{:S(2)}, u32[]{:S(2)}) collective-permute-start(bf16[960,256]{1,0:T(8,128)(2,1)S(1)} %add_convert_fusion.2), channel_id=1, source_target_pairs={{0,2},{2,0},{1,3},{3,1},{4,6},{6,4},{5,7},{7,5},{8,10},{10,8},{9,1... | collective-permute-start | bytes 1474568 | tf_op jit(solution)/shard_map/ppermute | solution.py:33
  203.8 1.1 copy-start.10
  207.9 13.9 %collective-permute-start.26 = (bf16[960,256]{1,0:T(8,128)(2,1)}, bf16[960,256]{1,0:T(8,128)(2,1)S(1)}, u32[]{:S(2)}, u32[]{:S(2)}) collective-permute-start(bf16[960,256]{1,0:T(8,128)(2,1)} %get-tuple-element.85), channel_id=1, source_target_pairs={{0,4},{4,8},{8,12},{12,0},{1,5},{5,9},{9,13},{13,1},{2,6},{6,10},{... | collective-permute-start | bytes 1474568 | tf_op jit(solution)/shard_map/ppermute | solution.py:33
  207.9 13.9 %collective-permute-start.27 = (bf16[960,256]{1,0:T(8,128)(2,1)}, bf16[960,256]{1,0:T(8,128)(2,1)S(1)}, u32[]{:S(2)}, u32[]{:S(2)}) collective-permute-start(bf16[960,256]{1,0:T(8,128)(2,1)} %get-tuple-element.86), channel_id=1, source_target_pairs={{0,12},{4,0},{8,4},{12,8},{1,13},{5,1},{9,5},{13,9},{2,14},{6,2},{... | collective-permute-start | bytes 1474568 | tf_op jit(solution)/shard_map/ppermute | solution.py:33
  (1 other events, 0.8 us)

commit v3 on v2

--- a/solution.py
+++ b/solution.py
@@ -15,7 +15,9 @@
 COLS_AXES = ("x", "y_hi", "core")
 F32, BF16 = jnp.float32, jnp.bfloat16
 VMEM_LIMIT = 62 * 2**20
+SMALL_LIMIT = 16 * 2**20
 PARTS = 2
+CHUNKS = 2
 
 
 CHEAP = pl.CostEstimate(flops=1000, bytes_accessed=1000, transcendentals=0)
@@ -37,26 +39,38 @@
     return lax.optimization_barrier((value, *deps))[0]
 
 
-def forward_early(places, late, core, mine, theirs, start, shards):
+def panel_place(dy, dz):
+    r = ((lax.axis_index("y_lo") + dy) & 1) * NZ + ((lax.axis_index("z") + dz) & (NZ - 1))
+    dx = ((r >> 1) - lax.axis_index("x")) & (NX - 1)
+    return (dx ^ (dx >> 1)) * 2 + ((r ^ lax.axis_index("y_hi")) & 1)
+
+
+def block_place(dx, dyh):
+    r = ((lax.axis_index("x") + dx) & (NX - 1)) * 2 + ((lax.axis_index("y_hi") + dyh) & 1)
+    return (((r >> 2) ^ lax.axis_index("y_lo")) & 1) * NZ + ((r - lax.axis_index("z")) & (NZ - 1))
+
+
+def forward_early(early, late, mine, theirs, start, shards):
     tokens, width = start.shape
     panels = sum(p.shape[0] for p in mine)
-    n, n_p, n_late = len(shards), len(mine), late.shape[0]
+    n, n_p, n_late = len(shards), len(mine) + len(theirs), len(late)
     rows = shards[0][0].shape[0]
     pieces = [a for shard in shards for a in shard]
 
-    def kernel(places_ref, late_ref, core_ref, *refs):
-        parts, (start_ref, *refs) = refs[: 2 * n_p], refs[2 * n_p :]
+    def kernel(*refs):
+        parts, (start_ref, *refs) = refs[:n_p], refs[n_p:]
         w_refs = refs[: len(pieces)]
         total_ref, late_x_ref, mine_ref, theirs_ref, sems, late_sems = refs[len(pieces) :]
         i = pl.program_id(0)
-        own = core_ref[0]
+        own = lax.axis_index("core")
         out_copies = []
-        for j in range(n_late):
+        for j, spot in enumerate(late):
+            place = panel_place(*spot)
             for k, buf in enumerate((mine_ref, theirs_ref)):
                 column = pl.multiple_of((2 * j + jnp.where(own == k, 0, 1)) * LANES, LANES)
                 out_copies.append(
                     pltpu.make_async_copy(
-                        buf.at[late_ref[j]],
+                        buf.at[place],
                         late_x_ref.at[:, pl.ds(column, LANES)],
                         late_sems.at[2 * j + k],
                     )
@@ -65,9 +79,9 @@
         @pl.when(i == 0)
         def _():
             copies = []
-            for k, buf in enumerate((mine_ref, theirs_ref)):
+            for buf, own_parts in ((mine_ref, parts[: len(mine)]), (theirs_ref, parts[len(mine) :])):
                 to = 0
-                for part in parts[k * n_p : (k + 1) * n_p]:
+                for part in own_parts:
                     held = buf.at[pl.ds(to, part.shape[0])]
                     copies.append(pltpu.make_async_copy(part, held, sems.at[len(copies)]))
                     to += part.shape[0]
@@ -81,7 +95,7 @@
         lo = pl.multiple_of(own * LANES, LANES)
         hi = pl.multiple_of((1 - own) * LANES, LANES)
         lhs = jnp.concatenate(
-            [r[places_ref[j]] for j in range(n) for r in (mine_ref, theirs_ref)], axis=1
+            [r[panel_place(*spot)] for spot in early for r in (mine_ref, theirs_ref)], axis=1
         )
         rhs, at = [], 0
         for shard in shards:
@@ -114,14 +128,11 @@
     hbm = pl.BlockSpec(memory_space=pl.ANY)
     return pl.pallas_call(
         kernel,
-        grid_spec=pltpu.PrefetchScalarGridSpec(
-            num_scalar_prefetch=3,
-            grid=(width // LANES,),
-            in_specs=[hbm] * (2 * n_p) + [tile] + [p for shard in shards for p in piece_specs(shard)],
-            out_specs=[tile, hbm],
-            scratch_shapes=[pltpu.VMEM((panels, tokens, LANES), BF16)] * 2
-            + [pltpu.SemaphoreType.DMA((2 * n_p,)), pltpu.SemaphoreType.DMA((2 * n_late,))],
-        ),
+        grid=(width // LANES,),
+        in_specs=[hbm] * n_p + [tile] + [p for shard in shards for p in piece_specs(shard)],
+        out_specs=[tile, hbm],
+        scratch_shapes=[pltpu.VMEM((panels, tokens, LANES), BF16)] * 2
+        + [pltpu.SemaphoreType.DMA((n_p,)), pltpu.SemaphoreType.DMA((2 * n_late,))],
         out_shape=[
             jax.ShapeDtypeStruct((tokens, width), F32),
             jax.ShapeDtypeStruct((tokens, 2 * n_late * LANES), BF16),
@@ -129,7 +140,7 @@
         compiler_params=pltpu.CompilerParams(vmem_limit_bytes=VMEM_LIMIT),
         cost_estimate=CHEAP,
         name="early",
-    )(places, late, core, *mine, *theirs, start, *pieces)
+    )(*mine, *theirs, start, *pieces)
 
 
 def forward_late(late_x, total, cotangent, shards, offset, dest, name):
@@ -168,18 +179,19 @@
     )(late_x, total, cotangent, *shards, *dest)
 
 
-def gradient(picks, core, slope, blocks, name):
+def gradient(places, slope, blocks, name):
     tokens, width = slope.shape
     rows = 2 * LANES
-    n = picks.shape[0]
+    n = len(places)
     arrays = [a for shard in blocks for a in shard]
-
-    def kernel(picks_ref, core_ref, s_ref, *refs):
-        a_refs, (mine_ref, theirs_ref, w_buf, sem) = refs[: len(arrays)], refs[len(arrays) :]
-        i = pl.program_id(0)
-
-        def fetch(step, slot):
-            wanted = picks_ref[step]
+    t = tokens // CHUNKS
+
+    def kernel(s_hbm, *refs):
+        a_refs, refs = refs[: len(arrays)], refs[len(arrays) :]
+        mine_hbm, theirs_hbm, s_buf, w_buf, out_buf, s_sem, w_sem, out_sem = refs
+
+        def fetch(k):
+            wanted = block_place(*places[k])
             at = 0
             for j, shard in enumerate(blocks):
                 held = a_refs[at : at + len(shard)]
@@ -190,83 +202,56 @@
                     to = 0
                     for ref in held:
                         w = ref.shape[1]
-                        pltpu.make_async_copy(
-                            ref, w_buf.at[slot, :, pl.ds(to, w)], sem.at[slot]
-                        ).start()
+                        pltpu.make_async_copy(ref, w_buf.at[k, :, pl.ds(to, w)], w_sem.at[k]).start()
                         to += w
 
-        @pl.when(i == 0)
-        def _():
-            fetch(0, 0)
-
-        @pl.when(i + 1 < n)
-        def _():
-            fetch(i + 1, (i + 1) % 2)
-
-        slot = i % 2
-        pltpu.make_async_copy(a_refs[0], w_buf.at[slot], sem.at[slot]).wait()
-        own = core_ref[0]
-        for half, out in ((own, mine_ref), (1 - own, theirs_ref)):
-            part = w_buf[slot, pl.ds(pl.multiple_of(half * LANES, LANES), LANES), :]
-            out[0] = lax.dot_general(
-                s_ref[...], part, (((1,), (1,)), ((), ())), preferred_element_type=F32
-            ).astype(BF16)
-
-    out_block = pl.BlockSpec((1, tokens, LANES), lambda i, *_: (i, 0, 0))
+        chunks = [pl.ds(c * t, t) for c in range(CHUNKS)]
+        loads = [
+            pltpu.make_async_copy(s_hbm.at[at], s_buf.at[at], s_sem.at[c]) for c, at in enumerate(chunks)
+        ]
+        fetch(0)
+        for load in loads:
+            load.start()
+        own = lax.axis_index("core")
+        stores = []
+        for k in range(n):
+            if k + 1 < n:
+                fetch(k + 1)
+            pltpu.make_async_copy(a_refs[0], w_buf.at[k], w_sem.at[k]).wait()
+            for c, at in enumerate(chunks):
+                if k == 0:
+                    loads[c].wait()
+                for h, (half, out) in enumerate(((1 - own, theirs_hbm), (own, mine_hbm))):
+                    part = w_buf[k, pl.ds(pl.multiple_of(half * LANES, LANES), LANES), :]
+                    out_buf[k, h, at, :] = lax.dot_general(
+                        s_buf[at, :], part, (((1,), (1,)), ((), ())), preferred_element_type=F32
+                    ).astype(BF16)
+                    store = pltpu.make_async_copy(
+                        out_buf.at[k, h, at], out.at[k, at], out_sem.at[k, h, c]
+                    )
+                    store.start()
+                    stores.append(store)
+        for store in stores:
+            store.wait()
+
+    hbm = pl.BlockSpec(memory_space=pl.ANY)
     return pl.pallas_call(
         kernel,
-        grid_spec=pltpu.PrefetchScalarGridSpec(
-            num_scalar_prefetch=2,
-            grid=(n,),
-            in_specs=[pl.BlockSpec((tokens, width), lambda i, *_: (0, 0))]
-            + [pl.BlockSpec(memory_space=pl.ANY)] * len(arrays),
-            out_specs=[out_block, out_block],
-            scratch_shapes=[pltpu.VMEM((2, rows, width), BF16), pltpu.SemaphoreType.DMA((2,))],
-        ),
+        in_specs=[hbm] * (1 + len(arrays)),
+        out_specs=[hbm] * 2,
+        scratch_shapes=[
+            pltpu.VMEM((tokens, width), BF16),
+            pltpu.VMEM((n, rows, width), BF16),
+            pltpu.VMEM((n, 2, tokens, LANES), BF16),
+            pltpu.SemaphoreType.DMA((CHUNKS,)),
+            pltpu.SemaphoreType.DMA((n,)),
+            pltpu.SemaphoreType.DMA((n, 2, CHUNKS)),
+        ],
         out_shape=[jax.ShapeDtypeStruct((n, tokens, LANES), BF16)] * 2,
         compiler_params=pltpu.CompilerParams(vmem_limit_bytes=VMEM_LIMIT),
         cost_estimate=CHEAP,
         name=name,
-    )(picks, core, slope, *arrays)
-
-
-def cut_first(z_minus, z_plus):
-    rows, width = z_minus.shape
-    steps = 4
-
-    def kernel(minus_ref, plus_ref, up_ref, down_ref):
-        up_ref[...] = minus_ref[...]
-        down_ref[...] = plus_ref[...]
-
-    def block(at=0):
-        return pl.BlockSpec((rows // 2 // steps, width), lambda i: (i + at, 0))
-
-    return pl.pallas_call(
-        kernel,
-        grid=(steps,),
-        in_specs=[block(), block(steps)],
-        out_specs=[block()] * 2,
-        out_shape=[jax.ShapeDtypeStruct((rows // 2, width), BF16)] * 2,
-        cost_estimate=DEAR,
-        name="cut_first",
-    )(z_minus, z_plus)
-
-
-def cut_far(far_a, far_b, width_a):
-    half, width = far_a.shape
-
-    def kernel(top_ref, low_ref, a_ref, b_ref):
-        for k, ref in enumerate((top_ref, low_ref)):
-            at = pl.ds(k * half, half)
-            a_ref[at, :] = ref[:, :width_a]
-            b_ref[at, :] = ref[:, width_a:]
-
-    return pl.pallas_call(
-        kernel,
-        out_shape=[jax.ShapeDtypeStruct((2 * half, w), BF16) for w in (width_a, width - width_a)],
-        cost_estimate=CHEAP,
-        name="cut_far",
-    )(far_a, far_b)
+    )(slope, *arrays)
 
 
 def mark(cost, *arrays):
@@ -278,6 +263,7 @@
         out_specs=any_space,
         out_shape=[jax.ShapeDtypeStruct(a.shape, a.dtype) for a in arrays],
         input_output_aliases={i: i for i in range(n)},
+        compiler_params=pltpu.CompilerParams(vmem_limit_bytes=SMALL_LIMIT),
         cost_estimate=cost,
         name="mark",
     )(*arrays)
@@ -310,33 +296,16 @@
         ],
         out_specs=[tile] * 3,
         out_shape=[jax.ShapeDtypeStruct((tokens, lanes), d) for d in (BF16, BF16, F32)],
+        compiler_params=pltpu.CompilerParams(vmem_limit_bytes=SMALL_LIMIT),
         cost_estimate=CHEAP,
         name=name,
     )(mine, back, via_minus, via_plus)
 
 
 def body(carried_sum, x_panels, w_panels, cotangent):
-    y_lo, z = lax.axis_index("y_lo"), lax.axis_index("z")
-    x, y_hi, core = lax.axis_index("x"), lax.axis_index("y_hi"), lax.axis_index("core")
-    core_of = core.reshape(1).astype(jnp.int32)
     tokens, width = carried_sum.shape
-    width_a, width_b = WIDTH_A, width - WIDTH_A
+    width_a = WIDTH_A
     rows = w_panels.shape[0]
-
-    def panels_for(dy, dz):
-        r = ((y_lo + dy) % 2) * NZ + (z + dz) % NZ
-        dx = (r // 2 - x) % NX
-        return (dx ^ (dx >> 1)) * 2 + (r % 2 - y_hi) % 2
-
-    def places(*ds):
-        return jnp.stack([panels_for(*d) for d in ds]).astype(jnp.int32)
-
-    def block_for(dx, dyh):
-        r = ((x + dx) % NX) * 2 + (y_hi + dyh) % 2
-        return ((r // NZ - y_lo) % 2) * NZ + (r % NZ - z) % NZ
-
-    def picks(*ds):
-        return jnp.stack([block_for(*d) for d in ds]).astype(jnp.int32)
 
     w_a, w_b = w_panels[:, :width_a], w_panels[:, width_a:]
     z_minus = shift(w_panels, "z", 1, NZ)
@@ -345,29 +314,29 @@
     pair = mark(flops(38 * 10**9), jnp.stack([x_panels, shift(x_panels, "y_hi", 1, 2)]))[0]
     x_minus = shift(pair, "x", 1, NX)
     x_plus = shift(pair, "x", -1, NX)
-    up, down = cut_first(z_minus, z_plus)
-    other_a = mark(DEAR, other_a)[0]
+    z_minus, z_plus, other_a = mark(DEAR, z_minus, z_plus, other_a)
+    up, down = z_minus[: rows // 2], z_plus[rows // 2 :]
     up, down, w_b, other_a, x_minus, x_plus = lax.optimization_barrier(
         (up, down, w_b, other_a, x_minus, x_plus)
     )
     far_top = shift(up, "z", 1, NZ)
     far_low = shift(down, "z", -1, NZ)
-    near = jnp.concatenate([pair, x_plus, x_minus])
-    near_theirs = shift(near, "core", 1, 2)
-    other_b = shift(after(w_b, near_theirs), "y_lo", 1, 2)
+    other_b = shift(w_b, "y_lo", 1, 2)
     x_far = [shift(x_minus[0], "x", 1, NX), shift(x_plus[1], "x", -1, NX)]
     x_far = jnp.stack(x_far)
-    mine = [near, x_far]
-    theirs = [near_theirs, shift(x_far, "core", 1, 2)]
-    far_a, far_b = cut_far(far_top, far_low, width_a)
-    send_a = after(other_a, far_a, other_b)
+    near = jnp.concatenate([pair, x_plus, x_minus])
+    far_a = jnp.concatenate([far_top[:, :width_a], far_low[:, :width_a]])
+    far_b = jnp.concatenate([far_top[:, width_a:], far_low[:, width_a:]])
+    send_a, near, x_far = lax.optimization_barrier(
+        (other_a, near, x_far, far_top, far_low, other_b)
+    )[:3]
+    mine = [pair, x_plus, x_minus, x_far]
+    theirs = [shift(near, "core", 1, 2), shift(x_far, "core", 1, 2)]
     other_minus_a = shift(send_a, "z", 1, NZ)
     other_plus_a = shift(send_a, "z", -1, NZ)
     other_far_a = shift(far_a, "y_lo", 1, 2)
     total, late_x = forward_early(
-        places((0, 0), (0, 1), (0, 3), (1, 0)),
-        places((0, 2), (1, 1), (1, 3), (1, 2)),
-        core_of, mine, theirs, carried_sum,
+        ((0, 0), (0, 1), (0, 3), (1, 0)), ((0, 2), (1, 1), (1, 3), (1, 2)), mine, theirs, carried_sum,
         [(w_panels,), (z_plus,), (z_minus,), (other_a, other_b)],
     )
     send_b, send_far_b = lax.optimization_barrier(
@@ -386,20 +355,20 @@
     blocks += [(other_plus_a, other_plus_b), (other_far_a, other_far_b), (other_minus_a, other_minus_b)]
 
     half = tokens // 2
-    m, t = gradient(picks((2, 0), (2, 1)), core_of, slope, blocks, "grad_far")
+    m, t = gradient(((2, 0), (2, 1)), slope, blocks, "grad_far")
     far_sum = (m.astype(F32) + shift(t, "core", 1, 2).astype(F32)).astype(BF16)
     up, down = lax.optimization_barrier((far_sum[:, :half], far_sum[:, half:]))
     via_minus = shift(up, "x", 1, NX)
     via_plus = shift(down, "x", -1, NX)
 
     slope = after(slope, up, down)
-    m, t = gradient(picks((1, 1), (3, 1), (0, 1)), core_of, slope, blocks, "grad_1")
+    m, t = gradient(((1, 1), (3, 1), (0, 1)), slope, blocks, "grad_1")
     via_minus, via_plus = mark(DEAR, via_minus, via_plus)
     up, down, own_1 = add_up(m, shift(t, "core", 1, 2), via_minus, via_plus, 1, "add_1")
     got_1 = shift(up, "x", 1, NX), shift(down, "x", -1, NX)
 
     slope = after(slope, up, down)
-    m, t = gradient(picks((1, 0), (3, 0), (0, 0)), core_of, slope, blocks, "grad_0")
+    m, t = gradient(((1, 0), (3, 0), (0, 0)), slope, blocks, "grad_0")
     got_1 = mark(DEAR, *got_1)
     m, via_minus, *got_1 = lax.optimization_barrier((m, via_minus, *got_1))
     up, down, own_0 = add_up(m, shift(t, "core", 1, 2), via_minus, via_plus, 0, "add_0")

time: 225 us -> 199 us (0.88)
  Pallas kernels: 83.3 us -> 67.6 us
  local copies, waits for them, and re-layouts: 19.4 us -> 4.89 us
  waiting for transfers between devices: 69 us -> 78.9 us
  other arithmetic: 11.7 us -> 4.55 us
    pallas_call x6 -> x4, Pallas kernels: 56.3 us -> 44.7 us  [the longest x3 27 us: gradient(): pl.pallas_call(kernel, in_specs=[hbm] * (1 + len(arrays)), out_specs=[hbm...]
    unnamed x40 -> x30, local copies, waits for them, and re-layouts: 12.3 us -> 1.97 us
    ppermute x29, waiting for transfers between devices: 69 us -> 78.9 us  [shift(): return lax.ppermute(value, axis, pairs)]
    pallas_call x2, Pallas kernels: 6.05 us -> 2.18 us  [add_up(): pl.pallas_call(kernel, grid=(steps,), in_specs=[three, three, pl.BlockSpe...]
    squeeze x2, local copies, waits for them, and re-layouts: 3.7 us -> 0.07 us  [body(): x_far = [shift(x_minus[0], 'x', 1, NX), shift(x_plus[1], 'x', -1, NX)]]
    another operation x4 -> x0, other arithmetic: 2.41 us -> none  [the longest x3 1.73 us: picks(): return jnp.stack([block_for(*d) for d in ds]).astype(jnp.int32)]
  transfers between devices with their start and end apart: 29 -> 29, of which waited for: 14 -> 18; matrix products, arithmetic and copies ran while one was open for 6% -> 2% of each run, Pallas kernels for 28% -> 26%
where the time goes in v3:
time: 199 us; the launch traced here: 197 us
  waiting for transfers between devices  78.9 us (40%)
  Pallas kernels  67.6 us (34%)
  starting transfers between devices  40.4 us (20%)
  local copies, waits for them, and re-layouts  4.89 us (2%)
  other arithmetic  4.55 us (2%)
    ppermute x29, waiting for transfers between devices, shift(): return lax.ppermute(value, axis, pairs)  78.9 us
    ppermute x29, starting transfers between devices, shift(): return lax.ppermute(value, axis, pairs)  40.4 us
    pallas_call x3, Pallas kernels, gradient(): pl.pallas_call(kernel, in_specs=[hbm] * (1 + len(arrays)), out_specs=[hbm...  27 us
    pallas_call x2, Pallas kernels, forward_late(): pl.pallas_call(kernel, grid=(cols // LANES,), in_specs=[pl.BlockSpec((tok...  20.7 us
    pallas_call x1, Pallas kernels, forward_early(): pl.pallas_call(kernel, grid=(width // LANES,), in_specs=[hbm] * n_p + [ti...  17.7 us
  transfers between devices with their start and end apart: 29, of which 18 were waited for; matrix products, arithmetic and copies ran while one was open for 2% of the time, Pallas kernels for 26%

profile of v3, /device:TPU:1, one launch (start us, length us, event | category | flops | bytes accessed | tf_op | source)
XLA Modules:
  0.0 197.2 jit_solution(18296706721321042932)
XLA Ops:
  0.6 3.8 %collective-permute-start = (bf16[960,256]{1,0:T(8,128)(2,1)}, bf16[960,256]{1,0:T(8,128)(2,1)S(1)}, u32[]{:S(2)}, u32[]{:S(2)}) collective-permute-start(bf16[960,256]{1,0:T(8,128)(2,1)} %param.5), channel_id=1, source_target_pairs={{0,2},{2,0},{1,3},{3,1},{4,6},{6,4},{5,7},{7,5},{8,10},{10,8},{9,1... | collective-permute-start | bytes 1474568 | tf_op jit(solution)/shard_map/ppermute | solution.py:35
  4.5 3.8 %collective-permute-start.2 = (bf16[512,1792]{1,0:T(8,128)(2,1)}, bf16[512,1792]{1,0:T(8,128)(2,1)S(1)}, u32[]{:S(2)}, u32[]{:S(2)}) collective-permute-start(bf16[512,1792]{1,0:T(8,128)(2,1)} %refs_0_.5), channel_id=1, source_target_pairs={{0,48},{16,0},{32,16},{48,32},{1,49},{17,1},{33,17},{49,33},{2,50}... | collective-permute-start | bytes 5505032 | tf_op jit(solution)/shard_map/ppermute | solution.py:35
  8.2 1.5 slice.36
  10.2 1.1 slice.39
  11.2 4.1 %collective-permute-done = bf16[960,256]{1,0:T(8,128)(2,1)S(1)} collective-permute-done((bf16[960,256]{1,0:T(8,128)(2,1)}, bf16[960,256]{1,0:T(8,128)(2,1)S(1)}, u32[]{:S(2)}, u32[]{:S(2)}) %collective-permute-start) | collective-permute-done | bytes 491552 | tf_op jit(solution)/shard_map/ppermute | solution.py:35
  15.5 2.6 %collective-permute-start.5 = (bf16[2,960,256]{2,1,0:T(8,128)(2,1)S(1)}, bf16[2,960,256]{2,1,0:T(8,128)(2,1)S(1)}, u32[]{:S(2)}, u32[]{:S(2)}) collective-permute-start(bf16[2,960,256]{2,1,0:T(8,128)(2,1)S(1)} %mark.4.refs_0_), channel_id=1, source_target_pairs={{0,12},{4,0},{8,4},{12,8},{1,13},{5,1},{9,5},{13,9},{2,14},{6,2},{... | collective-permute-start | bytes 2949128 | tf_op jit(solution)/shard_map/ppermute | solution.py:35
  18.0 25.9 %collective-permute-done.3.refs_2_ = bf16[512,1280]{1,0:T(8,128)(2,1)} collective-permute-done((bf16[512,1280]{1,0:T(8,128)(2,1)S(1)}, bf16[512,1280]{1,0:T(8,128)(2,1)}, u32[]{:S(2)}, u32[]{:S(2)}) %collective-permute-start.3) | collective-permute-done | bytes 1310752 | tf_op jit(solution)/shard_map/ppermute | solution.py:35
  43.9 3.0 %collective-permute-done.2.refs_1_ = bf16[512,1792]{1,0:T(8,128)(2,1)S(1)} collective-permute-done((bf16[512,1792]{1,0:T(8,128)(2,1)}, bf16[512,1792]{1,0:T(8,128)(2,1)S(1)}, u32[]{:S(2)}, u32[]{:S(2)}) %collective-permute-start.2) | collective-permute-done | bytes 1835040 | tf_op jit(solution)/shard_map/ppermute | solution.py:35
  46.9 3.0 %collective-permute-done.1.refs_0_ = bf16[512,1792]{1,0:T(8,128)(2,1)S(1)} collective-permute-done((bf16[512,1792]{1,0:T(8,128)(2,1)}, bf16[512,1792]{1,0:T(8,128)(2,1)S(1)}, u32[]{:S(2)}, u32[]{:S(2)}) %collective-permute-start.1) | collective-permute-done | bytes 1835040 | tf_op jit(solution)/shard_map/ppermute | solution.py:35
  50.2 2.7 %collective-permute-start.9 = (bf16[256,1792]{1,0:T(8,128)(2,1)S(1)}, bf16[256,1792]{1,0:T(8,128)(2,1)S(1)}, u32[]{:S(2)}, u32[]{:S(2)}) collective-permute-start(bf16[256,1792]{1,0:T(8,128)(2,1)S(1)} %slice.38), channel_id=1, source_target_pairs={{0,48},{16,0},{32,16},{48,32},{1,49},{17,1},{33,17},{49,33},{2,50}... | collective-permute-start | bytes 2752520 | tf_op jit(solution)/shard_map/ppermute | solution.py:35
  52.9 1.3 collective-permute-start.6
  54.2 1.5 collective-permute-start.7
  56.4 7.8 %collective-permute-done.6 = bf16[960,256]{1,0:T(8,128)(2,1)S(1)} collective-permute-done((bf16[960,256]{1,0:T(8,128)(2,1)S(1)}, bf16[960,256]{1,0:T(8,128)(2,1)S(1)}, u32[]{:S(2)}, u32[]{:S(2)}) %collective-permute-start.6) | collective-permute-done | bytes 491552 | tf_op jit(solution)/shard_map/ppermute | solution.py:35
  64.3 1.5 collective-permute-done.10.refs_11_.refs_6_
  65.8 5.2 %collective-permute-done.8 = bf16[256,1792]{1,0:T(8,128)(2,1)S(1)} collective-permute-done((bf16[256,1792]{1,0:T(8,128)(2,1)S(1)}, bf16[256,1792]{1,0:T(8,128)(2,1)S(1)}, u32[]{:S(2)}, u32[]{:S(2)}) %collective-permute-start.8) | collective-permute-done | bytes 917536 | tf_op jit(solution)/shard_map/ppermute | solution.py:35
  71.1 3.1 %collective-permute-start.11 = (bf16[6,960,256]{2,1,0:T(8,128)(2,1)S(1)}, bf16[6,960,256]{2,1,0:T(8,128)(2,1)}, u32[]{:S(2)}, u32[]{:S(2)}) collective-permute-start(bf16[6,960,256]{2,1,0:T(8,128)(2,1)S(1)} %pad_maximum_fusion), channel_id=1, source_target_pairs={{0,1},{1,0},{2,3},{3,2},{4,5},{5,4},{6,7},{7,6},{8,9},{9,8},{10,11... | collective-permute-start | bytes 8847368 | tf_op jit(solution)/shard_map/ppermute | solution.py:35
  74.8 2.7 %collective-permute-start.14 = (bf16[512,1280]{1,0:T(8,128)(2,1)}, bf16[512,1280]{1,0:T(8,128)(2,1)}, u32[]{:S(2)}, u32[]{:S(2)}) collective-permute-start(bf16[512,1280]{1,0:T(8,128)(2,1)} %get-tuple-element.59.refs_10_.refs_5_), channel_id=1, source_target_pairs={{0,48},{16,0},{32,16},{48,32},{1,49},{17,1},{33,17},{49,33},{2,50}... | collective-permute-start | bytes 3932168 | tf_op jit(solution)/shard_map/ppermute | solution.py:35
  78.2 2.4 %collective-permute-done.12.refs_5_ = bf16[2,960,256]{2,1,0:T(8,128)(2,1)S(1)} collective-permute-done((bf16[2,960,256]{2,1,0:T(8,128)(2,1)S(1)}, bf16[2,960,256]{2,1,0:T(8,128)(2,1)S(1)}, u32[]{:S(2)}, u32[]{:S(2)}) %collective-permute-start.12) | collective-permute-done | bytes 983072 | tf_op jit(solution)/shard_map/ppermute | solution.py:35
  80.6 1.0 copy-done.13
  81.5 17.7 %early.1 = (f32[960,1792]{1,0:T(8,128)}, bf16[960,2048]{1,0:T(8,128)(2,1)}) custom-call(bf16[2,960,256]{2,1,0:T(8,128)(2,1)} %copy-done.2, bf16[2,960,256]{2,1,0:T(8,128)(2,1)} %copy-done.10, bf16[2,960,256]{2,1,0:T(8,128)(2,1)} %copy-done.11, bf16[2,960,256]{2,1,0:T(8,128)(2,1)} %copy-done.12, bf16[6,960,256]{2,1,0:T(8,128)(2,1)} %collective-permute-done.11.refs_4_, ...), custom_call_target="tpu_custom_call" | custom-call | flops 1000 | bytes 1000 | tf_op jit(solution)/shard_map/early/pallas_call | solution.py:129
  99.2 5.7 %collective-permute-done.15.refs_3_.refs_9_ = bf16[512,1280]{1,0:T(8,128)(2,1)} collective-permute-done((bf16[512,1280]{1,0:T(8,128)(2,1)S(1)}, bf16[512,1280]{1,0:T(8,128)(2,1)}, u32[]{:S(2)}, u32[]{:S(2)}) %collective-permute-start.15) | collective-permute-done | bytes 1310752 | tf_op jit(solution)/shard_map/ppermute | solution.py:35
  104.9 0.8 collective-permute-done.14.refs_1_.refs_7_
  105.7 3.1 %collective-permute-done.13.refs_2_.refs_11_ = bf16[512,1280]{1,0:T(8,128)(2,1)} collective-permute-done((bf16[512,1280]{1,0:T(8,128)(2,1)}, bf16[512,1280]{1,0:T(8,128)(2,1)}, u32[]{:S(2)}, u32[]{:S(2)}) %collective-permute-start.13) | collective-permute-done | bytes 1310752 | tf_op jit(solution)/shard_map/ppermute | solution.py:35
  108.8 1.1 collective-permute-start.18
  109.9 2.7 %collective-permute-start.16 = (bf16[512,512]{1,0:T(8,128)(2,1)}, bf16[512,512]{1,0:T(8,128)(2,1)}, u32[]{:S(2)}, u32[]{:S(2)}) collective-permute-start(bf16[512,512]{1,0:T(8,128)(2,1)} %copy-done.7), channel_id=1, source_target_pairs={{0,48},{16,0},{32,16},{48,32},{1,49},{17,1},{33,17},{49,33},{2,50}... | collective-permute-start | bytes 1572872 | tf_op jit(solution)/shard_map/ppermute | solution.py:35
  112.5 13.3 %gelu_a.1 = (bf16[960,1792]{1,0:T(8,128)(2,1)}, bf16[960,1792]{1,0:T(8,128)(2,1)}) custom-call(bf16[960,2048]{1,0:T(8,128)(2,1)} %get-tuple-element.57.x_ref, f32[960,1792]{1,0:T(8,128)} %get-tuple-element.58.start_ref, bf16[960,1792]{1,0:T(8,128)(2,1)} %cot_ref.3, bf16[512,1280]{1,0:T(8,128)(2,1)} %copy-done.5, ...), custom_call_target="tpu_custom_call" | custom-call | flops 1000 | bytes 1000 | tf_op jit(solution)/shard_map/gelu_a/pallas_call | solution.py:167
  125.9 0.8 copy-done.8
  126.9 7.4 %gelu_b.1 = (bf16[960,1792]{1,0:T(8,128)(2,1)}, bf16[960,1792]{1,0:T(8,128)(2,1)}) custom-call(bf16[960,2048]{1,0:T(8,128)(2,1)} %get-tuple-element.57.x_ref, f32[960,1792]{1,0:T(8,128)} %get-tuple-element.58.start_ref, bf16[960,1792]{1,0:T(8,128)(2,1)} %cot_ref.3, bf16[512,512]{1,0:T(8,128)(2,1)} %copy-done.6, ...), custom_call_target="tpu_custom_call", output_to_operand_aliasing={{0}: (7, {}), {1}: (8, {})} | custom-call | flops 1000 | bytes 1000 | tf_op jit(solution)/shard_map/gelu_b/pallas_call | solution.py:167
  134.3 7.7 %grad_far.1 = (bf16[2,960,256]{2,1,0:T(8,128)(2,1)}, bf16[2,960,256]{2,1,0:T(8,128)(2,1)}) custom-call(bf16[960,1792]{1,0:T(8,128)(2,1)} %get-tuple-element.77.s_hbm, bf16[512,1792]{1,0:T(8,128)(2,1)} %refs_0_.5, bf16[512,1792]{1,0:T(8,128)(2,1)} %copy-done, bf16[512,1280]{1,0:T(8,128)(2,1)} %copy-done.5, bf16[512,512]{1,0:T(8,128)(2,1)} %copy-done.6, ...), custom_call_target="tpu_custom_call" | custom-call | flops 1000 | bytes 1000 | tf_op jit(solution)/shard_map/grad_far/pallas_call | solution.py:238
  141.9 2.3 %collective-permute-start.19 = (bf16[2,960,256]{2,1,0:T(8,128)(2,1)}, bf16[2,960,256]{2,1,0:T(8,128)(2,1)S(1)}, u32[]{:S(2)}, u32[]{:S(2)}) collective-permute-start(bf16[2,960,256]{2,1,0:T(8,128)(2,1)} %get-tuple-element.67), channel_id=1, source_target_pairs={{0,1},{1,0},{2,3},{3,2},{4,5},{5,4},{6,7},{7,6},{8,9},{9,8},{10,11... | collective-permute-start | bytes 2949128 | tf_op jit(solution)/shard_map/ppermute | solution.py:35
  144.3 2.4 %collective-permute-done.19 = bf16[2,960,256]{2,1,0:T(8,128)(2,1)S(1)} collective-permute-done((bf16[2,960,256]{2,1,0:T(8,128)(2,1)}, bf16[2,960,256]{2,1,0:T(8,128)(2,1)S(1)}, u32[]{:S(2)}, u32[]{:S(2)}) %collective-permute-start.19) | collective-permute-done | bytes 983072 | tf_op jit(solution)/shard_map/ppermute | solution.py:35
  146.7 1.5 add_convert_fusion
  148.2 0.7 collective-permute-start.21
  148.9 2.0 %collective-permute-start.22 = (bf16[2,480,256]{2,1,0:T(8,128)(2,1)S(1)}, bf16[2,480,256]{2,1,0:T(8,128)(2,1)S(1)}, u32[]{:S(2)}, u32[]{:S(2)}) collective-permute-start(bf16[2,480,256]{2,1,0:T(8,128)(2,1)S(1)} %get-tuple-element.69), channel_id=1, source_target_pairs={{0,12},{4,0},{8,4},{12,8},{1,13},{5,1},{9,5},{13,9},{2,14},{6,2},{... | collective-permute-start | bytes 1474568 | tf_op jit(solution)/shard_map/ppermute | solution.py:35
  151.0 9.6 %grad_1.1 = (bf16[3,960,256]{2,1,0:T(8,128)(2,1)}, bf16[3,960,256]{2,1,0:T(8,128)(2,1)}) custom-call(bf16[960,1792]{1,0:T(8,128)(2,1)} %get-tuple-element.77.s_hbm, bf16[512,1792]{1,0:T(8,128)(2,1)} %refs_0_.5, bf16[512,1792]{1,0:T(8,128)(2,1)} %copy-done, bf16[512,1280]{1,0:T(8,128)(2,1)} %copy-done.5, bf16[512,512]{1,0:T(8,128)(2,1)} %copy-done.6, ...), custom_call_target="tpu_custom_call" | custom-call | flops 1000 | bytes 1000 | tf_op jit(solution)/shard_map/grad_1/pallas_call | solution.py:238
  160.5 1.0 collective-permute-start.20
  161.9 2.7 %collective-permute-done.20.back_ref = bf16[3,960,256]{2,1,0:T(8,128)(2,1)S(1)} collective-permute-done((bf16[3,960,256]{2,1,0:T(8,128)(2,1)}, bf16[3,960,256]{2,1,0:T(8,128)(2,1)S(1)}, u32[]{:S(2)}, u32[]{:S(2)}) %collective-permute-start.20) | collective-permute-done | bytes 1474592 | tf_op jit(solution)/shard_map/ppermute | solution.py:35
  164.7 1.4 add_1.1
  166.1 2.7 %collective-permute-start.24 = (bf16[960,256]{1,0:T(8,128)(2,1)}, bf16[960,256]{1,0:T(8,128)(2,1)}, u32[]{:S(2)}, u32[]{:S(2)}) collective-permute-start(bf16[960,256]{1,0:T(8,128)(2,1)} %get-tuple-element.76), channel_id=1, source_target_pairs={{0,12},{4,0},{8,4},{12,8},{1,13},{5,1},{9,5},{13,9},{2,14},{6,2},{... | collective-permute-start | bytes 1474568 | tf_op jit(solution)/shard_map/ppermute | solution.py:35
  168.8 9.7 %grad_0.1 = (bf16[3,960,256]{2,1,0:T(8,128)(2,1)}, bf16[3,960,256]{2,1,0:T(8,128)(2,1)}) custom-call(bf16[960,1792]{1,0:T(8,128)(2,1)} %get-tuple-element.77.s_hbm, bf16[512,1792]{1,0:T(8,128)(2,1)} %refs_0_.5, bf16[512,1792]{1,0:T(8,128)(2,1)} %copy-done, bf16[512,1280]{1,0:T(8,128)(2,1)} %copy-done.5, bf16[512,512]{1,0:T(8,128)(2,1)} %copy-done.6, ...), custom_call_target="tpu_custom_call" | custom-call | flops 1000 | bytes 1000 | tf_op jit(solution)/shard_map/grad_0/pallas_call | solution.py:238
  178.5 1.0 collective-permute-start.25
  180.1 1.4 add_convert_fusion.2
  181.5 0.8 collective-permute-start.28
  182.6 0.8 add_0.1
  183.5 2.7 %collective-permute-start.27 = (bf16[960,256]{1,0:T(8,128)(2,1)S(1)}, bf16[960,256]{1,0:T(8,128)(2,1)S(1)}, u32[]{:S(2)}, u32[]{:S(2)}) collective-permute-start(bf16[960,256]{1,0:T(8,128)(2,1)S(1)} %get-tuple-element.86), channel_id=1, source_target_pairs={{0,12},{4,0},{8,4},{12,8},{1,13},{5,1},{9,5},{13,9},{2,14},{6,2},{... | collective-permute-start | bytes 1474568 | tf_op jit(solution)/shard_map/ppermute | solution.py:35
  186.1 8.4 %collective-permute-done.28 = bf16[960,256]{1,0:T(8,128)(2,1)S(1)} collective-permute-done((bf16[960,256]{1,0:T(8,128)(2,1)S(1)}, bf16[960,256]{1,0:T(8,128)(2,1)S(1)}, u32[]{:S(2)}, u32[]{:S(2)}) %collective-permute-start.28) | collective-permute-done | bytes 491552 | tf_op jit(solution)/shard_map/ppermute | solution.py:35
  194.6 1.6 collective-permute-done.26
  196.2 1.0 add_convert_fusion.1
  (71 shorter events, 4.6 us)
Async XLA Ops:
  0.6 14.7 %copy-start.14 = (bf16[960,256]{1,0:T(8,128)(2,1)S(1)}, bf16[960,256]{1,0:T(8,128)(2,1)}, u32[]{:S(2)}) copy-start(bf16[960,256]{1,0:T(8,128)(2,1)} %param.5) | copy-start | bytes 1474564
  0.6 14.7 %collective-permute-start = (bf16[960,256]{1,0:T(8,128)(2,1)}, bf16[960,256]{1,0:T(8,128)(2,1)S(1)}, u32[]{:S(2)}, u32[]{:S(2)}) collective-permute-start(bf16[960,256]{1,0:T(8,128)(2,1)} %param.5), channel_id=1, source_target_pairs={{0,2},{2,0},{1,3},{3,1},{4,6},{6,4},{5,7},{7,5},{8,10},{10,8},{9,1... | collective-permute-start | bytes 1474568 | tf_op jit(solution)/shard_map/ppermute | solution.py:35
  4.5 42.4 %collective-permute-start.2 = (bf16[512,1792]{1,0:T(8,128)(2,1)}, bf16[512,1792]{1,0:T(8,128)(2,1)S(1)}, u32[]{:S(2)}, u32[]{:S(2)}) collective-permute-start(bf16[512,1792]{1,0:T(8,128)(2,1)} %refs_0_.5), channel_id=1, source_target_pairs={{0,48},{16,0},{32,16},{48,32},{1,49},{17,1},{33,17},{49,33},{2,50}... | collective-permute-start | bytes 5505032 | tf_op jit(solution)/shard_map/ppermute | solution.py:35
  8.2 41.7 %collective-permute-start.1 = (bf16[512,1792]{1,0:T(8,128)(2,1)}, bf16[512,1792]{1,0:T(8,128)(2,1)S(1)}, u32[]{:S(2)}, u32[]{:S(2)}) collective-permute-start(bf16[512,1792]{1,0:T(8,128)(2,1)} %refs_0_.5), channel_id=1, source_target_pairs={{0,16},{16,32},{32,48},{48,0},{1,17},{17,33},{33,49},{49,1},{2,18}... | collective-permute-start | bytes 5505032 | tf_op jit(solution)/shard_map/ppermute | solution.py:35
  9.7 34.2 %collective-permute-start.3 = (bf16[512,1280]{1,0:T(8,128)(2,1)S(1)}, bf16[512,1280]{1,0:T(8,128)(2,1)}, u32[]{:S(2)}, u32[]{:S(2)}) collective-permute-start(bf16[512,1280]{1,0:T(8,128)(2,1)S(1)} %slice.36), channel_id=1, source_target_pairs={{0,64},{64,0},{1,65},{65,1},{2,66},{66,2},{3,67},{67,3},{4,68},{68... | collective-permute-start | bytes 3932168 | tf_op jit(solution)/shard_map/ppermute | solution.py:35
  15.4 40.6 %copy-start.2 = (bf16[2,960,256]{2,1,0:T(8,128)(2,1)}, bf16[2,960,256]{2,1,0:T(8,128)(2,1)S(1)}, u32[]{:S(2)}) copy-start(bf16[2,960,256]{2,1,0:T(8,128)(2,1)S(1)} %mark.4.refs_0_) | copy-start | bytes 2949124
  15.5 34.6 %collective-permute-start.5 = (bf16[2,960,256]{2,1,0:T(8,128)(2,1)S(1)}, bf16[2,960,256]{2,1,0:T(8,128)(2,1)S(1)}, u32[]{:S(2)}, u32[]{:S(2)}) collective-permute-start(bf16[2,960,256]{2,1,0:T(8,128)(2,1)S(1)} %mark.4.refs_0_), channel_id=1, source_target_pairs={{0,12},{4,0},{8,4},{12,8},{1,13},{5,1},{9,5},{13,9},{2,14},{6,2},{... | collective-permute-start | bytes 2949128 | tf_op jit(solution)/shard_map/ppermute | solution.py:35
  18.0 32.0 %collective-permute-start.4 = (bf16[2,960,256]{2,1,0:T(8,128)(2,1)S(1)}, bf16[2,960,256]{2,1,0:T(8,128)(2,1)S(1)}, u32[]{:S(2)}, u32[]{:S(2)}) collective-permute-start(bf16[2,960,256]{2,1,0:T(8,128)(2,1)S(1)} %mark.4.refs_0_), channel_id=1, source_target_pairs={{0,4},{4,8},{8,12},{12,0},{1,5},{5,9},{9,13},{13,1},{2,6},{6,10},{... | collective-permute-start | bytes 2949128 | tf_op jit(solution)/shard_map/ppermute | solution.py:35
  49.9 3.0 %copy-start = (bf16[512,1792]{1,0:T(8,128)(2,1)}, bf16[512,1792]{1,0:T(8,128)(2,1)S(1)}, u32[]{:S(2)}) copy-start(bf16[512,1792]{1,0:T(8,128)(2,1)S(1)} %get-tuple-element.47.refs_8_.refs_1_) | copy-start | bytes 5505028
  49.9 3.0 %copy-start.1 = (bf16[512,1792]{1,0:T(8,128)(2,1)}, bf16[512,1792]{1,0:T(8,128)(2,1)S(1)}, u32[]{:S(2)}) copy-start(bf16[512,1792]{1,0:T(8,128)(2,1)S(1)} %get-tuple-element.46.refs_9_.refs_4_) | copy-start | bytes 5505028
  50.1 6.3 %copy-start.10 = (bf16[2,960,256]{2,1,0:T(8,128)(2,1)}, bf16[2,960,256]{2,1,0:T(8,128)(2,1)S(1)}, u32[]{:S(2)}) copy-start(bf16[2,960,256]{2,1,0:T(8,128)(2,1)S(1)} %collective-permute-done.5.refs_1_) | copy-start | bytes 2949124
  50.1 6.3 %copy-start.11 = (bf16[2,960,256]{2,1,0:T(8,128)(2,1)}, bf16[2,960,256]{2,1,0:T(8,128)(2,1)S(1)}, u32[]{:S(2)}) copy-start(bf16[2,960,256]{2,1,0:T(8,128)(2,1)S(1)} %collective-permute-done.4.refs_2_) | copy-start | bytes 2949124
  50.1 21.0 %collective-permute-start.8 = (bf16[256,1792]{1,0:T(8,128)(2,1)S(1)}, bf16[256,1792]{1,0:T(8,128)(2,1)S(1)}, u32[]{:S(2)}, u32[]{:S(2)}) collective-permute-start(bf16[256,1792]{1,0:T(8,128)(2,1)S(1)} %slice.37), channel_id=1, source_target_pairs={{0,16},{16,32},{32,48},{48,0},{1,17},{17,33},{33,49},{49,1},{2,18}... | collective-permute-start | bytes 2752520 | tf_op jit(solution)/shard_map/ppermute | solution.py:35
  50.2 20.9 %collective-permute-start.9 = (bf16[256,1792]{1,0:T(8,128)(2,1)S(1)}, bf16[256,1792]{1,0:T(8,128)(2,1)S(1)}, u32[]{:S(2)}, u32[]{:S(2)}) collective-permute-start(bf16[256,1792]{1,0:T(8,128)(2,1)S(1)} %slice.38), channel_id=1, source_target_pairs={{0,48},{16,0},{32,16},{48,32},{1,49},{17,1},{33,17},{49,33},{2,50}... | collective-permute-start | bytes 2752520 | tf_op jit(solution)/shard_map/ppermute | solution.py:35
  52.9 11.3 %collective-permute-start.6 = (bf16[960,256]{1,0:T(8,128)(2,1)S(1)}, bf16[960,256]{1,0:T(8,128)(2,1)S(1)}, u32[]{:S(2)}, u32[]{:S(2)}) collective-permute-start(bf16[960,256]{1,0:T(8,128)(2,1)S(1)} %slice_bitcast_fusion.1), channel_id=1, source_target_pairs={{0,4},{4,8},{8,12},{12,0},{1,5},{5,9},{9,13},{13,1},{2,6},{6,10},{... | collective-permute-start | bytes 1474568 | tf_op jit(solution)/shard_map/ppermute | solution.py:35
  54.2 10.0 %collective-permute-start.7 = (bf16[960,256]{1,0:T(8,128)(2,1)S(1)}, bf16[960,256]{1,0:T(8,128)(2,1)S(1)}, u32[]{:S(2)}, u32[]{:S(2)}) collective-permute-start(bf16[960,256]{1,0:T(8,128)(2,1)S(1)} %slice_bitcast_fusion), channel_id=1, source_target_pairs={{0,12},{4,0},{8,4},{12,8},{1,13},{5,1},{9,5},{13,9},{2,14},{6,2},{... | collective-permute-start | bytes 1474568 | tf_op jit(solution)/shard_map/ppermute | solution.py:35
  55.7 10.1 %collective-permute-start.10 = (bf16[512,512]{1,0:T(8,128)(2,1)S(1)}, bf16[512,512]{1,0:T(8,128)(2,1)S(1)}, u32[]{:S(2)}, u32[]{:S(2)}) collective-permute-start(bf16[512,512]{1,0:T(8,128)(2,1)S(1)} %slice.39), channel_id=1, source_target_pairs={{0,64},{64,0},{1,65},{65,1},{2,66},{66,2},{3,67},{67,3},{4,68},{68... | collective-permute-start | bytes 1572872 | tf_op jit(solution)/shard_map/ppermute | solution.py:35
  64.3 13.2 %copy-start.12 = (bf16[2,960,256]{2,1,0:T(8,128)(2,1)}, bf16[2,960,256]{2,1,0:T(8,128)(2,1)S(1)}, u32[]{:S(2)}) copy-start(bf16[2,960,256]{2,1,0:T(8,128)(2,1)S(1)} %pad_maximum_fusion.3.refs_3_) | copy-start | bytes 2949124
  65.8 8.5 %copy-start.7 = (bf16[512,512]{1,0:T(8,128)(2,1)}, bf16[512,512]{1,0:T(8,128)(2,1)S(1)}, u32[]{:S(2)}) copy-start(bf16[512,512]{1,0:T(8,128)(2,1)S(1)} %collective-permute-done.10.refs_11_.refs_6_) | copy-start | bytes 1572868
  71.1 10.5 %collective-permute-start.11 = (bf16[6,960,256]{2,1,0:T(8,128)(2,1)S(1)}, bf16[6,960,256]{2,1,0:T(8,128)(2,1)}, u32[]{:S(2)}, u32[]{:S(2)}) collective-permute-start(bf16[6,960,256]{2,1,0:T(8,128)(2,1)S(1)} %pad_maximum_fusion), channel_id=1, source_target_pairs={{0,1},{1,0},{2,3},{3,2},{4,5},{5,4},{6,7},{7,6},{8,9},{9,8},{10,11... | collective-permute-start | bytes 8847368 | tf_op jit(solution)/shard_map/ppermute | solution.py:35
  74.3 24.9 %copy-start.5 = (bf16[512,1280]{1,0:T(8,128)(2,1)}, bf16[512,1280]{1,0:T(8,128)(2,1)S(1)}, u32[]{:S(2)}) copy-start(bf16[512,1280]{1,0:T(8,128)(2,1)S(1)} %pad_maximum_fusion.1.refs_0_.refs_2_) | copy-start | bytes 3932164
  74.4 30.6 %collective-permute-start.15 = (bf16[512,1280]{1,0:T(8,128)(2,1)S(1)}, bf16[512,1280]{1,0:T(8,128)(2,1)}, u32[]{:S(2)}, u32[]{:S(2)}) collective-permute-start(bf16[512,1280]{1,0:T(8,128)(2,1)S(1)} %pad_maximum_fusion.1.refs_0_.refs_2_), channel_id=1, source_target_pairs={{0,64},{64,0},{1,65},{65,1},{2,66},{66,2},{3,67},{67,3},{4,68},{68... | collective-permute-start | bytes 3932168 | tf_op jit(solution)/shard_map/ppermute | solution.py:35
  74.8 30.9 %collective-permute-start.14 = (bf16[512,1280]{1,0:T(8,128)(2,1)}, bf16[512,1280]{1,0:T(8,128)(2,1)}, u32[]{:S(2)}, u32[]{:S(2)}) collective-permute-start(bf16[512,1280]{1,0:T(8,128)(2,1)} %get-tuple-element.59.refs_10_.refs_5_), channel_id=1, source_target_pairs={{0,48},{16,0},{32,16},{48,32},{1,49},{17,1},{33,17},{49,33},{2,50}... | collective-permute-start | bytes 3932168 | tf_op jit(solution)/shard_map/ppermute | solution.py:35
  77.5 31.3 %collective-permute-start.13 = (bf16[512,1280]{1,0:T(8,128)(2,1)}, bf16[512,1280]{1,0:T(8,128)(2,1)}, u32[]{:S(2)}, u32[]{:S(2)}) collective-permute-start(bf16[512,1280]{1,0:T(8,128)(2,1)} %get-tuple-element.59.refs_10_.refs_5_), channel_id=1, source_target_pairs={{0,16},{16,32},{32,48},{48,0},{1,17},{17,33},{33,49},{49,1},{2,18}... | collective-permute-start | bytes 3932168 | tf_op jit(solution)/shard_map/ppermute | solution.py:35
  77.5 3.0 %collective-permute-start.12 = (bf16[2,960,256]{2,1,0:T(8,128)(2,1)S(1)}, bf16[2,960,256]{2,1,0:T(8,128)(2,1)S(1)}, u32[]{:S(2)}, u32[]{:S(2)}) collective-permute-start(bf16[2,960,256]{2,1,0:T(8,128)(2,1)S(1)} %pad_maximum_fusion.3.refs_3_), channel_id=1, source_target_pairs={{0,1},{1,0},{2,3},{3,2},{4,5},{5,4},{6,7},{7,6},{8,9},{9,8},{10,11... | collective-permute-start | bytes 2949128 | tf_op jit(solution)/shard_map/ppermute | solution.py:35
  78.2 30.6 %copy-start.6 = (bf16[512,512]{1,0:T(8,128)(2,1)}, bf16[512,512]{1,0:T(8,128)(2,1)S(1)}, u32[]{:S(2)}) copy-start(bf16[512,512]{1,0:T(8,128)(2,1)S(1)} %pad_maximum_fusion.4.refs_0_.refs_3_) | copy-start | bytes 1572868
  80.5 1.0 copy-start.13
  108.8 17.1 %collective-permute-start.18 = (bf16[512,512]{1,0:T(8,128)(2,1)S(1)}, bf16[512,512]{1,0:T(8,128)(2,1)S(1)}, u32[]{:S(2)}, u32[]{:S(2)}) collective-permute-start(bf16[512,512]{1,0:T(8,128)(2,1)S(1)} %pad_maximum_fusion.4.refs_0_.refs_3_), channel_id=1, source_target_pairs={{0,64},{64,0},{1,65},{65,1},{2,66},{66,2},{3,67},{67,3},{4,68},{68... | collective-permute-start | bytes 1572872 | tf_op jit(solution)/shard_map/ppermute | solution.py:35
  109.9 16.0 %collective-permute-start.17 = (bf16[512,512]{1,0:T(8,128)(2,1)}, bf16[512,512]{1,0:T(8,128)(2,1)S(1)}, u32[]{:S(2)}, u32[]{:S(2)}) collective-permute-start(bf16[512,512]{1,0:T(8,128)(2,1)} %copy-done.7), channel_id=1, source_target_pairs={{0,16},{16,32},{32,48},{48,0},{1,17},{17,33},{33,49},{49,1},{2,18}... | collective-permute-start | bytes 1572872 | tf_op jit(solution)/shard_map/ppermute | solution.py:35
  109.9 16.0 %collective-permute-start.16 = (bf16[512,512]{1,0:T(8,128)(2,1)}, bf16[512,512]{1,0:T(8,128)(2,1)}, u32[]{:S(2)}, u32[]{:S(2)}) collective-permute-start(bf16[512,512]{1,0:T(8,128)(2,1)} %copy-done.7), channel_id=1, source_target_pairs={{0,48},{16,0},{32,16},{48,32},{1,49},{17,1},{33,17},{49,33},{2,50}... | collective-permute-start | bytes 1572872 | tf_op jit(solution)/shard_map/ppermute | solution.py:35
  125.9 0.8 copy-start.8
  125.9 1.0 copy-start.9
  141.9 4.7 %collective-permute-start.19 = (bf16[2,960,256]{2,1,0:T(8,128)(2,1)}, bf16[2,960,256]{2,1,0:T(8,128)(2,1)S(1)}, u32[]{:S(2)}, u32[]{:S(2)}) collective-permute-start(bf16[2,960,256]{2,1,0:T(8,128)(2,1)} %get-tuple-element.67), channel_id=1, source_target_pairs={{0,1},{1,0},{2,3},{3,2},{4,5},{5,4},{6,7},{7,6},{8,9},{9,8},{10,11... | collective-permute-start | bytes 2949128 | tf_op jit(solution)/shard_map/ppermute | solution.py:35
  148.2 13.7 %collective-permute-start.21 = (bf16[2,480,256]{2,1,0:T(8,128)(2,1)S(1)}, bf16[2,480,256]{2,1,0:T(8,128)(2,1)S(1)}, u32[]{:S(2)}, u32[]{:S(2)}) collective-permute-start(bf16[2,480,256]{2,1,0:T(8,128)(2,1)S(1)} %get-tuple-element.68), channel_id=1, source_target_pairs={{0,4},{4,8},{8,12},{12,0},{1,5},{5,9},{9,13},{13,1},{2,6},{6,10},{... | collective-permute-start | bytes 1474568 | tf_op jit(solution)/shard_map/ppermute | solution.py:35
  148.9 13.0 %collective-permute-start.22 = (bf16[2,480,256]{2,1,0:T(8,128)(2,1)S(1)}, bf16[2,480,256]{2,1,0:T(8,128)(2,1)S(1)}, u32[]{:S(2)}, u32[]{:S(2)}) collective-permute-start(bf16[2,480,256]{2,1,0:T(8,128)(2,1)S(1)} %get-tuple-element.69), channel_id=1, source_target_pairs={{0,12},{4,0},{8,4},{12,8},{1,13},{5,1},{9,5},{13,9},{2,14},{6,2},{... | collective-permute-start | bytes 1474568 | tf_op jit(solution)/shard_map/ppermute | solution.py:35
  160.5 4.1 %copy-start.4 = (bf16[3,960,256]{2,1,0:T(8,128)(2,1)S(1)}, bf16[3,960,256]{2,1,0:T(8,128)(2,1)}, u32[]{:S(2)}) copy-start(bf16[3,960,256]{2,1,0:T(8,128)(2,1)} %get-tuple-element.71.mine_ref) | copy-start | bytes 4423684
  160.5 4.1 %collective-permute-start.20 = (bf16[3,960,256]{2,1,0:T(8,128)(2,1)}, bf16[3,960,256]{2,1,0:T(8,128)(2,1)S(1)}, u32[]{:S(2)}, u32[]{:S(2)}) collective-permute-start(bf16[3,960,256]{2,1,0:T(8,128)(2,1)} %get-tuple-element.72), channel_id=1, source_target_pairs={{0,1},{1,0},{2,3},{3,2},{4,5},{5,4},{6,7},{7,6},{8,9},{9,8},{10,11... | collective-permute-start | bytes 4423688 | tf_op jit(solution)/shard_map/ppermute | solution.py:35
  166.1 14.0 %collective-permute-start.23 = (bf16[960,256]{1,0:T(8,128)(2,1)}, bf16[960,256]{1,0:T(8,128)(2,1)}, u32[]{:S(2)}, u32[]{:S(2)}) collective-permute-start(bf16[960,256]{1,0:T(8,128)(2,1)} %get-tuple-element.75), channel_id=1, source_target_pairs={{0,4},{4,8},{8,12},{12,0},{1,5},{5,9},{9,13},{13,1},{2,6},{6,10},{... | collective-permute-start | bytes 1474568 | tf_op jit(solution)/shard_map/ppermute | solution.py:35
  166.1 14.0 %collective-permute-start.24 = (bf16[960,256]{1,0:T(8,128)(2,1)}, bf16[960,256]{1,0:T(8,128)(2,1)}, u32[]{:S(2)}, u32[]{:S(2)}) collective-permute-start(bf16[960,256]{1,0:T(8,128)(2,1)} %get-tuple-element.76), channel_id=1, source_target_pairs={{0,12},{4,0},{8,4},{12,8},{1,13},{5,1},{9,5},{13,9},{2,14},{6,2},{... | collective-permute-start | bytes 1474568 | tf_op jit(solution)/shard_map/ppermute | solution.py:35
  178.5 4.1 %collective-permute-start.25 = (bf16[3,960,256]{2,1,0:T(8,128)(2,1)}, bf16[3,960,256]{2,1,0:T(8,128)(2,1)S(1)}, u32[]{:S(2)}, u32[]{:S(2)}) collective-permute-start(bf16[3,960,256]{2,1,0:T(8,128)(2,1)} %get-tuple-element.82), channel_id=1, source_target_pairs={{0,1},{1,0},{2,3},{3,2},{4,5},{5,4},{6,7},{7,6},{8,9},{9,8},{10,11... | collective-permute-start | bytes 4423688 | tf_op jit(solution)/shard_map/ppermute | solution.py:35
  180.1 2.6 %copy-start.3 = (bf16[3,960,256]{2,1,0:T(8,128)(2,1)S(1)}, bf16[3,960,256]{2,1,0:T(8,128)(2,1)}, u32[]{:S(2)}) copy-start(bf16[3,960,256]{2,1,0:T(8,128)(2,1)} %get-tuple-element.81.mine_ref) | copy-start | bytes 4423684
  181.5 13.1 %collective-permute-start.28 = (bf16[960,256]{1,0:T(8,128)(2,1)S(1)}, bf16[960,256]{1,0:T(8,128)(2,1)S(1)}, u32[]{:S(2)}, u32[]{:S(2)}) collective-permute-start(bf16[960,256]{1,0:T(8,128)(2,1)S(1)} %add_convert_fusion.2), channel_id=1, source_target_pairs={{0,2},{2,0},{1,3},{3,1},{4,6},{6,4},{5,7},{7,5},{8,10},{10,8},{9,1... | collective-permute-start | bytes 1474568 | tf_op jit(solution)/shard_map/ppermute | solution.py:35
  183.4 12.8 %collective-permute-start.26 = (bf16[960,256]{1,0:T(8,128)(2,1)S(1)}, bf16[960,256]{1,0:T(8,128)(2,1)S(1)}, u32[]{:S(2)}, u32[]{:S(2)}) collective-permute-start(bf16[960,256]{1,0:T(8,128)(2,1)S(1)} %get-tuple-element.85), channel_id=1, source_target_pairs={{0,4},{4,8},{8,12},{12,0},{1,5},{5,9},{9,13},{13,1},{2,6},{6,10},{... | collective-permute-start | bytes 1474568 | tf_op jit(solution)/shard_map/ppermute | solution.py:35
  183.5 12.7 %collective-permute-start.27 = (bf16[960,256]{1,0:T(8,128)(2,1)S(1)}, bf16[960,256]{1,0:T(8,128)(2,1)S(1)}, u32[]{:S(2)}, u32[]{:S(2)}) collective-permute-start(bf16[960,256]{1,0:T(8,128)(2,1)S(1)} %get-tuple-element.86), channel_id=1, source_target_pairs={{0,12},{4,0},{8,4},{12,8},{1,13},{5,1},{9,5},{13,9},{2,14},{6,2},{... | collective-permute-start | bytes 1474568 | tf_op jit(solution)/shard_map/ppermute | solution.py:35

commit v4 on v3

--- a/solution.py
+++ b/solution.py
@@ -143,7 +143,14 @@
     )(*mine, *theirs, start, *pieces)
 
 
-def forward_late(late_x, total, cotangent, shards, offset, dest, name):
+def gelu(preact, cotangent):
+    normal_cdf = 0.5 * (1.0 + lax.erf(preact * inv_root_two))
+    normal_pdf = jnp.exp(-0.5 * preact * preact) * inv_root_tau
+    slope = cotangent.astype(F32) * (normal_cdf + preact * normal_pdf)
+    return (preact * normal_cdf).astype(BF16), slope.astype(BF16)
+
+
+def forward_late(late_x, total, cotangent, shards, name):
     tokens, width = total.shape
     rows, cols = shards[0].shape
     n = len(shards)
@@ -156,39 +163,45 @@
         for p in range(PARTS):
             at = pl.ds(p * t, t)
             preact = start_ref[at, :] + jnp.dot(x_ref[at, :], rhs, preferred_element_type=F32)
-            normal_cdf = 0.5 * (1.0 + lax.erf(preact * inv_root_two))
-            normal_pdf = jnp.exp(-0.5 * preact * preact) * inv_root_tau
-            act_ref[at, :] = (preact * normal_cdf).astype(BF16)
-            slope = cot_ref[at, :].astype(F32) * (normal_cdf + preact * normal_pdf)
-            slope_ref[at, :] = slope.astype(BF16)
-
-    first = offset // LANES
-    tile = pl.BlockSpec((tokens, LANES), lambda i: (0, i + first))
+            act_ref[at, :], slope_ref[at, :] = gelu(preact, cot_ref[at, :])
+
+    tile = pl.BlockSpec((tokens, LANES), lambda i: (0, i))
     return pl.pallas_call(
         kernel,
         grid=(cols // LANES,),
         in_specs=[pl.BlockSpec((tokens, depth), lambda i: (0, 0)), tile, tile]
-        + [pl.BlockSpec((rows, LANES), lambda i: (0, i))] * n
-        + [pl.BlockSpec(memory_space=pl.ANY)] * len(dest),
+        + [pl.BlockSpec((rows, LANES), lambda i: (0, i))] * n,
         out_specs=[tile, tile],
         out_shape=[jax.ShapeDtypeStruct((tokens, width), BF16)] * 2,
-        input_output_aliases={3 + n + k: k for k in range(len(dest))},
         compiler_params=pltpu.CompilerParams(vmem_limit_bytes=VMEM_LIMIT),
         cost_estimate=CHEAP,
         name=name,
-    )(late_x, total, cotangent, *shards, *dest)
-
-
-def gradient(places, slope, blocks, name):
+    )(late_x, total, cotangent, *shards)
+
+
+def gradient(places, slope, blocks, name, last=None):
     tokens, width = slope.shape
+    n_last = 0
+    if last is not None:
+        late_x, total, cotangent, shards, activated = last
+        cols = shards[0].shape[1]
+        edge = width - cols
+        depth = late_x.shape[1]
+        last_args = [late_x, total, cotangent, *shards, activated]
+        n_last = len(last_args)
     rows = 2 * LANES
     n = len(places)
     arrays = [a for shard in blocks for a in shard]
     t = tokens // CHUNKS
 
     def kernel(s_hbm, *refs):
+        last_refs, refs = refs[:n_last], refs[n_last:]
         a_refs, refs = refs[: len(arrays)], refs[len(arrays) :]
-        mine_hbm, theirs_hbm, s_buf, w_buf, out_buf, s_sem, w_sem, out_sem = refs
+        mine_hbm, theirs_hbm, *refs = refs
+        if last is not None:
+            s_out, act_out, *refs = refs
+            x_buf, total_buf, cot_buf, shard_buf, act_buf, *refs, l_sem, x_sem, act_sem = refs
+        s_buf, w_buf, out_buf, s_sem, w_sem, out_sem = refs
 
         def fetch(k):
             wanted = block_place(*places[k])
@@ -206,14 +219,58 @@
                         to += w
 
         chunks = [pl.ds(c * t, t) for c in range(CHUNKS)]
+        had = width if last is None else edge
         loads = [
-            pltpu.make_async_copy(s_hbm.at[at], s_buf.at[at], s_sem.at[c]) for c, at in enumerate(chunks)
-        ]
-        fetch(0)
-        for load in loads:
-            load.start()
+            pltpu.make_async_copy(
+                s_hbm.at[at, pl.ds(0, had)], s_buf.at[at, pl.ds(0, had)], s_sem.at[c]
+            )
+            for c, at in enumerate(chunks)
+        ]
+        stores = []
+        if last is None:
+            fetch(0)
+            for load in loads:
+                load.start()
+        else:
+            x_hbm, total_hbm, cot_hbm, *shard_hbm = last_refs[:-1]
+            tail = pl.ds(edge, cols)
+            first = [
+                pltpu.make_async_copy(ref, shard_buf.at[pl.ds(j * rows, rows)], l_sem.at[j])
+                for j, ref in enumerate(shard_hbm)
+            ]
+            by_chunk = [
+                [
+                    pltpu.make_async_copy(x_hbm.at[at], x_buf.at[at], x_sem.at[0, c]),
+                    pltpu.make_async_copy(total_hbm.at[at, tail], total_buf.at[at], x_sem.at[1, c]),
+                    pltpu.make_async_copy(cot_hbm.at[at, tail], cot_buf.at[at], x_sem.at[2, c]),
+                ]
+                for c, at in enumerate(chunks)
+            ]
+            for load in first + sum(by_chunk, []):
+                load.start()
+            for load in loads:
+                load.start()
+            fetch(0)
+            for load in first:
+                load.wait()
+            for c, at in enumerate(chunks):
+                for load in by_chunk[c]:
+                    load.wait()
+                for b in range(cols // LANES):
+                    here = pl.ds(b * LANES, LANES)
+                    preact = total_buf[at, here] + jnp.dot(
+                        x_buf[at, :], shard_buf[:, here], preferred_element_type=F32
+                    )
+                    act_buf[at, here], s_buf[at, pl.ds(edge + b * LANES, LANES)] = gelu(
+                        preact, cot_buf[at, here]
+                    )
+                stores.append(pltpu.make_async_copy(act_buf.at[at], act_out.at[at, tail], act_sem.at[0, c]))
+                stores.append(
+                    pltpu.make_async_copy(s_buf.at[at, tail], s_out.at[at, tail], act_sem.at[1, c])
+                )
+                stores[-2].start()
+                stores[-1].start()
         own = lax.axis_index("core")
-        stores = []
         for k in range(n):
             if k + 1 < n:
                 fetch(k + 1)
@@ -234,24 +291,43 @@
         for store in stores:
             store.wait()
 
+    last_scratch, last_sems, last_out, aliases = [], [], [], {}
+    if last is not None:
+        last_scratch = [
+            pltpu.VMEM((tokens, depth), BF16),
+            pltpu.VMEM((tokens, cols), F32),
+            pltpu.VMEM((tokens, cols), BF16),
+            pltpu.VMEM((depth, cols), BF16),
+            pltpu.VMEM((tokens, cols), BF16),
+        ]
+        last_sems = [
+            pltpu.SemaphoreType.DMA((len(shards),)),
+            pltpu.SemaphoreType.DMA((3, CHUNKS)),
+            pltpu.SemaphoreType.DMA((2, CHUNKS)),
+        ]
+        last_out = [jax.ShapeDtypeStruct((tokens, width), BF16)] * 2
+        aliases = {0: 2, n_last: 3}
     hbm = pl.BlockSpec(memory_space=pl.ANY)
     return pl.pallas_call(
         kernel,
-        in_specs=[hbm] * (1 + len(arrays)),
-        out_specs=[hbm] * 2,
-        scratch_shapes=[
+        in_specs=[hbm] * (1 + n_last + len(arrays)),
+        out_specs=[hbm] * (2 + len(last_out)),
+        scratch_shapes=last_scratch
+        + [
             pltpu.VMEM((tokens, width), BF16),
             pltpu.VMEM((n, rows, width), BF16),
             pltpu.VMEM((n, 2, tokens, LANES), BF16),
             pltpu.SemaphoreType.DMA((CHUNKS,)),
             pltpu.SemaphoreType.DMA((n,)),
             pltpu.SemaphoreType.DMA((n, 2, CHUNKS)),
-        ],
-        out_shape=[jax.ShapeDtypeStruct((n, tokens, LANES), BF16)] * 2,
+        ]
+        + last_sems,
+        out_shape=[jax.ShapeDtypeStruct((n, tokens, LANES), BF16)] * 2 + last_out,
+        input_output_aliases=aliases,
         compiler_params=pltpu.CompilerParams(vmem_limit_bytes=VMEM_LIMIT),
         cost_estimate=CHEAP,
         name=name,
-    )(slope, *arrays)
+    )(slope, *(last_args if last is not None else []), *arrays)
 
 
 def mark(cost, *arrays):
@@ -269,37 +345,44 @@
     )(*arrays)
 
 
-def add_up(mine, back, via_minus, via_plus, dyh, name):
+def add_up(mine, back, via_minus, via_plus, dyh, got, name):
     tokens, lanes = mine.shape[1:]
     steps = 2
     t = tokens // steps
 
-    def kernel(mine_ref, back_ref, minus_ref, plus_ref, up_ref, down_ref, own_ref):
+    def kernel(mine_ref, back_ref, minus_ref, plus_ref, *refs):
+        got_refs, (up_ref, down_ref, *own_ref) = refs[: len(got)], refs[len(got) :]
         first = pl.program_id(0) < steps // 2
         total = mine_ref[...].astype(F32) + back_ref[...].astype(F32)
         minus, plus = minus_ref[0].astype(F32), plus_ref[0].astype(F32)
         up_ref[...] = (total[0] + jnp.where(first, minus, 0.0)).astype(BF16)
         down_ref[...] = (total[1] + jnp.where(first, 0.0, plus)).astype(BF16)
-        own_ref[...] = total[2]
+        if got:
+            own = total[2]
+            for ref in got_refs:
+                own = own + ref[...].astype(F32)
+            own_ref[0][...] = own.astype(BF16)
 
     tile = pl.BlockSpec((t, lanes), lambda i: (i, 0))
-    three = pl.BlockSpec((3, t, lanes), lambda i: (0, i, 0))
+    stack = pl.BlockSpec((mine.shape[0], t, lanes), lambda i: (0, i, 0))
     last = steps // 2 - 1
+    n_out = 3 if got else 2
     return pl.pallas_call(
         kernel,
         grid=(steps,),
         in_specs=[
-            three,
-            three,
+            stack,
+            stack,
             pl.BlockSpec((1, t, lanes), lambda i: (dyh, jnp.minimum(i, last), 0)),
             pl.BlockSpec((1, t, lanes), lambda i: (dyh, jnp.maximum(i - last - 1, 0), 0)),
-        ],
-        out_specs=[tile] * 3,
-        out_shape=[jax.ShapeDtypeStruct((tokens, lanes), d) for d in (BF16, BF16, F32)],
+        ]
+        + [tile] * len(got),
+        out_specs=[tile] * n_out,
+        out_shape=[jax.ShapeDtypeStruct((tokens, lanes), BF16)] * n_out,
         compiler_params=pltpu.CompilerParams(vmem_limit_bytes=SMALL_LIMIT),
         cost_estimate=CHEAP,
         name=name,
-    )(mine, back, via_minus, via_plus)
+    )(mine, back, via_minus, via_plus, *got)
 
 
 def body(carried_sum, x_panels, w_panels, cotangent):
@@ -314,7 +397,8 @@
     pair = mark(flops(38 * 10**9), jnp.stack([x_panels, shift(x_panels, "y_hi", 1, 2)]))[0]
     x_minus = shift(pair, "x", 1, NX)
     x_plus = shift(pair, "x", -1, NX)
-    z_minus, z_plus, other_a = mark(DEAR, z_minus, z_plus, other_a)
+    z_minus, z_plus = mark(flops(80 * 10**9), z_minus, z_plus)
+    other_a = mark(DEAR, other_a)[0]
     up, down = z_minus[: rows // 2], z_plus[rows // 2 :]
     up, down, w_b, other_a, x_minus, x_plus = lax.optimization_barrier(
         (up, down, w_b, other_a, x_minus, x_plus)
@@ -336,8 +420,8 @@
     other_plus_a = shift(send_a, "z", -1, NZ)
     other_far_a = shift(far_a, "y_lo", 1, 2)
     total, late_x = forward_early(
-        ((0, 0), (0, 1), (0, 3), (1, 0)), ((0, 2), (1, 1), (1, 3), (1, 2)), mine, theirs, carried_sum,
-        [(w_panels,), (z_plus,), (z_minus,), (other_a, other_b)],
+        ((0, 0), (0, 1), (0, 3), (1, 0), (0, 2)), ((1, 1), (1, 3), (1, 2)), mine, theirs, carried_sum,
+        [(w_panels,), (z_plus,), (z_minus,), (other_a, other_b), (far_a, far_b)],
     )
     send_b, send_far_b = lax.optimization_barrier(
         (other_b, far_b, other_minus_a, other_plus_a, other_far_a, total)
@@ -345,37 +429,41 @@
     other_minus_b = shift(send_b, "z", 1, NZ)
     other_plus_b = shift(send_b, "z", -1, NZ)
     other_far_b = shift(send_far_b, "y_lo", 1, 2)
-    done = forward_late(
-        late_x, total, cotangent, [far_a, other_plus_a, other_minus_a, other_far_a], 0, [], "gelu_a"
+    activated, slope = forward_late(
+        late_x, total, cotangent, [other_plus_a, other_minus_a, other_far_a], "gelu_a"
     )
-    activated, slope = forward_late(
-        late_x, total, cotangent, [far_b, other_plus_b, other_minus_b, other_far_b], width_a, done, "gelu_b"
-    )
+    last = (late_x, total, cotangent, [other_plus_b, other_minus_b, other_far_b], activated)
     blocks = [(w_panels,), (z_plus,), (far_a, far_b), (z_minus,), (other_a, other_b)]
     blocks += [(other_plus_a, other_plus_b), (other_far_a, other_far_b), (other_minus_a, other_minus_b)]
 
     half = tokens // 2
-    m, t = gradient(((2, 0), (2, 1)), slope, blocks, "grad_far")
+    m, t, slope, activated = gradient(((2, 0), (2, 1)), slope, blocks, "grad_far", last)
     far_sum = (m.astype(F32) + shift(t, "core", 1, 2).astype(F32)).astype(BF16)
     up, down = lax.optimization_barrier((far_sum[:, :half], far_sum[:, half:]))
     via_minus = shift(up, "x", 1, NX)
     via_plus = shift(down, "x", -1, NX)
 
     slope = after(slope, up, down)
-    m, t = gradient(((1, 1), (3, 1), (0, 1)), slope, blocks, "grad_1")
+    m, t = gradient(((1, 1), (3, 1)), slope, blocks, "grad_1")
     via_minus, via_plus = mark(DEAR, via_minus, via_plus)
-    up, down, own_1 = add_up(m, shift(t, "core", 1, 2), via_minus, via_plus, 1, "add_1")
+    up, down = add_up(m, shift(t, "core", 1, 2), via_minus, via_plus, 1, [], "add_1")
     got_1 = shift(up, "x", 1, NX), shift(down, "x", -1, NX)
 
     slope = after(slope, up, down)
-    m, t = gradient(((1, 0), (3, 0), (0, 0)), slope, blocks, "grad_0")
+    m, t = gradient(((1, 0), (3, 0), (0, 1)), slope, blocks, "grad_0")
     got_1 = mark(DEAR, *got_1)
-    m, via_minus, *got_1 = lax.optimization_barrier((m, via_minus, *got_1))
-    up, down, own_0 = add_up(m, shift(t, "core", 1, 2), via_minus, via_plus, 0, "add_0")
+    up, down, to_other = add_up(m, shift(t, "core", 1, 2), via_minus, via_plus, 0, got_1, "add_0")
     got_0 = shift(up, "x", 1, NX), shift(down, "x", -1, NX)
-    to_other = own_1 + got_1[0].astype(F32) + got_1[1].astype(F32)
-    from_other = shift(to_other.astype(BF16), "y_hi", 1, 2)
-    input_grad = own_0 + got_0[0].astype(F32) + got_0[1].astype(F32) + from_other.astype(F32)
+    from_other = shift(to_other, "y_hi", 1, 2)
+
+    slope = after(slope, up, down, to_other)
+    m, t = gradient(((0, 0),), slope, blocks, "grad_own")
+    got_0 = mark(DEAR, *got_0)
+    from_other = mark(flops(60 * 10**9), from_other)[0]
+    input_grad = m[0].astype(F32) + shift(t, "core", 1, 2)[0].astype(F32)
+    for part in (*got_0, from_other):
+        input_grad = input_grad + part.astype(F32)
+    input_grad = input_grad.astype(BF16)
     return activated, input_grad.astype(BF16)
 
 

time: 199 us -> 192 us (0.965)
  waiting for transfers between devices: 78.9 us -> 70.6 us
    pallas_call x2 -> x1, Pallas kernels: 20.7 us -> 12.1 us  [forward_late(): pl.pallas_call(kernel, grid=(cols // LANES,), in_specs=[pl.BlockSpec((tok...]
    ppermute x29 -> x30, waiting for transfers between devices: 78.9 us -> 70.6 us  [shift(): return lax.ppermute(value, axis, pairs)]
    pallas_call x5 -> x6, Pallas kernels: 29.1 us -> 36.8 us  [the longest x4 33.8 us: gradient(): pl.pallas_call(kernel, in_specs=[hbm] * (1 + n_last + len(arrays)), out_s...]
    ppermute x29 -> x30, starting transfers between devices: 40.4 us -> 41.9 us  [shift(): return lax.ppermute(value, axis, pairs)]
  transfers between devices with their start and end apart: 29 -> 30, of which waited for: 18 -> 14; matrix products, arithmetic and copies ran while one was open for 2% -> 3% of each run, Pallas kernels for 26% -> 27%
where the time goes in v4:
time: 192 us
  waiting for transfers between devices  70.6 us (37%)
  Pallas kernels  67.6 us (35%)
  starting transfers between devices  41.9 us (22%)
  local copies, waits for them, and re-layouts  6.67 us (3%)
  other arithmetic  4.01 us (2%)
    ppermute x30, waiting for transfers between devices, shift(): return lax.ppermute(value, axis, pairs)  70.6 us
    ppermute x30, starting transfers between devices, shift(): return lax.ppermute(value, axis, pairs)  41.9 us
    pallas_call x4, Pallas kernels, gradient(): pl.pallas_call(kernel, in_specs=[hbm] * (1 + n_last + len(arrays)), out_s...  33.8 us
    pallas_call x1, Pallas kernels, forward_early(): pl.pallas_call(kernel, grid=(width // LANES,), in_specs=[hbm] * n_p + [ti...  18.7 us
    pallas_call x1, Pallas kernels, forward_late(): pl.pallas_call(kernel, grid=(cols // LANES,), in_specs=[pl.BlockSpec((tok...  12.1 us
  transfers between devices with their start and end apart: 30, of which 14 were waited for; matrix products, arithmetic and copies ran while one was open for 3% of the time, Pallas kernels for 27%

profile of v4, /device:TPU:1, one launch (start us, length us, event | category | flops | bytes accessed | tf_op | source)
XLA Modules:
  0.0 191.7 jit_solution(5985051158542605093)
XLA Ops:
  0.6 3.8 %collective-permute-start = (bf16[960,256]{1,0:T(8,128)(2,1)}, bf16[960,256]{1,0:T(8,128)(2,1)S(1)}, u32[]{:S(2)}, u32[]{:S(2)}) collective-permute-start(bf16[960,256]{1,0:T(8,128)(2,1)} %param.5), channel_id=1, source_target_pairs={{0,2},{2,0},{1,3},{3,1},{4,6},{6,4},{5,7},{7,5},{8,10},{10,8},{9,1... | collective-permute-start | bytes 1474568 | tf_op jit(solution)/shard_map/ppermute | solution.py:35
  4.5 3.8 %collective-permute-start.2 = (bf16[512,1792]{1,0:T(8,128)(2,1)}, bf16[512,1792]{1,0:T(8,128)(2,1)S(1)}, u32[]{:S(2)}, u32[]{:S(2)}) collective-permute-start(bf16[512,1792]{1,0:T(8,128)(2,1)} %refs_0_.5), channel_id=1, source_target_pairs={{0,48},{16,0},{32,16},{48,32},{1,49},{17,1},{33,17},{49,33},{2,50}... | collective-permute-start | bytes 5505032 | tf_op jit(solution)/shard_map/ppermute | solution.py:35
  8.2 1.5 slice.39
  10.2 1.9 slice.38
  12.0 3.3 %collective-permute-done = bf16[960,256]{1,0:T(8,128)(2,1)S(1)} collective-permute-done((bf16[960,256]{1,0:T(8,128)(2,1)}, bf16[960,256]{1,0:T(8,128)(2,1)S(1)}, u32[]{:S(2)}, u32[]{:S(2)}) %collective-permute-start) | collective-permute-done | bytes 491552 | tf_op jit(solution)/shard_map/ppermute | solution.py:35
  15.5 2.6 %collective-permute-start.5 = (bf16[2,960,256]{2,1,0:T(8,128)(2,1)S(1)}, bf16[2,960,256]{2,1,0:T(8,128)(2,1)S(1)}, u32[]{:S(2)}, u32[]{:S(2)}) collective-permute-start(bf16[2,960,256]{2,1,0:T(8,128)(2,1)S(1)} %mark.7.refs_0_), channel_id=1, source_target_pairs={{0,12},{4,0},{8,4},{12,8},{1,13},{5,1},{9,5},{13,9},{2,14},{6,2},{... | collective-permute-start | bytes 2949128 | tf_op jit(solution)/shard_map/ppermute | solution.py:35
  18.0 25.9 %collective-permute-done.3.refs_0_ = bf16[512,1280]{1,0:T(8,128)(2,1)} collective-permute-done((bf16[512,1280]{1,0:T(8,128)(2,1)S(1)}, bf16[512,1280]{1,0:T(8,128)(2,1)}, u32[]{:S(2)}, u32[]{:S(2)}) %collective-permute-start.3) | collective-permute-done | bytes 1310752 | tf_op jit(solution)/shard_map/ppermute | solution.py:35
  43.9 3.0 %collective-permute-done.2.refs_1_ = bf16[512,1792]{1,0:T(8,128)(2,1)S(1)} collective-permute-done((bf16[512,1792]{1,0:T(8,128)(2,1)}, bf16[512,1792]{1,0:T(8,128)(2,1)S(1)}, u32[]{:S(2)}, u32[]{:S(2)}) %collective-permute-start.2) | collective-permute-done | bytes 1835040 | tf_op jit(solution)/shard_map/ppermute | solution.py:35
  46.9 3.0 %collective-permute-done.1.refs_0_ = bf16[512,1792]{1,0:T(8,128)(2,1)S(1)} collective-permute-done((bf16[512,1792]{1,0:T(8,128)(2,1)}, bf16[512,1792]{1,0:T(8,128)(2,1)S(1)}, u32[]{:S(2)}, u32[]{:S(2)}) %collective-permute-start.1) | collective-permute-done | bytes 1835040 | tf_op jit(solution)/shard_map/ppermute | solution.py:35
  50.2 2.7 %collective-permute-start.9 = (bf16[256,1792]{1,0:T(8,128)(2,1)S(1)}, bf16[256,1792]{1,0:T(8,128)(2,1)S(1)}, u32[]{:S(2)}, u32[]{:S(2)}) collective-permute-start(bf16[256,1792]{1,0:T(8,128)(2,1)S(1)} %slice.37), channel_id=1, source_target_pairs={{0,48},{16,0},{32,16},{48,32},{1,49},{17,1},{33,17},{49,33},{2,50}... | collective-permute-start | bytes 2752520 | tf_op jit(solution)/shard_map/ppermute | solution.py:35
  52.9 1.3 collective-permute-start.6
  54.2 1.5 collective-permute-start.7
  56.4 7.8 %collective-permute-done.6 = bf16[960,256]{1,0:T(8,128)(2,1)S(1)} collective-permute-done((bf16[960,256]{1,0:T(8,128)(2,1)S(1)}, bf16[960,256]{1,0:T(8,128)(2,1)S(1)}, u32[]{:S(2)}, u32[]{:S(2)}) %collective-permute-start.6) | collective-permute-done | bytes 491552 | tf_op jit(solution)/shard_map/ppermute | solution.py:35
  64.3 1.5 collective-permute-done.10.refs_11_.refs_13_.refs_6_
  65.8 5.2 %collective-permute-done.8 = bf16[256,1792]{1,0:T(8,128)(2,1)S(1)} collective-permute-done((bf16[256,1792]{1,0:T(8,128)(2,1)S(1)}, bf16[256,1792]{1,0:T(8,128)(2,1)S(1)}, u32[]{:S(2)}, u32[]{:S(2)}) %collective-permute-start.8) | collective-permute-done | bytes 917536 | tf_op jit(solution)/shard_map/ppermute | solution.py:35
  71.1 3.1 %collective-permute-start.11 = (bf16[6,960,256]{2,1,0:T(8,128)(2,1)S(1)}, bf16[6,960,256]{2,1,0:T(8,128)(2,1)}, u32[]{:S(2)}, u32[]{:S(2)}) collective-permute-start(bf16[6,960,256]{2,1,0:T(8,128)(2,1)S(1)} %pad_maximum_fusion), channel_id=1, source_target_pairs={{0,1},{1,0},{2,3},{3,2},{4,5},{5,4},{6,7},{7,6},{8,9},{9,8},{10,11... | collective-permute-start | bytes 8847368 | tf_op jit(solution)/shard_map/ppermute | solution.py:35
  74.8 2.7 %collective-permute-start.13 = (bf16[512,1280]{1,0:T(8,128)(2,1)}, bf16[512,1280]{1,0:T(8,128)(2,1)}, u32[]{:S(2)}, u32[]{:S(2)}) collective-permute-start(bf16[512,1280]{1,0:T(8,128)(2,1)} %mark.9.refs_10_.refs_12_.refs_5_), channel_id=1, source_target_pairs={{0,48},{16,0},{32,16},{48,32},{1,49},{17,1},{33,17},{49,33},{2,50}... | collective-permute-start | bytes 3932168 | tf_op jit(solution)/shard_map/ppermute | solution.py:35
  79.2 1.3 collective-permute-done.12.refs_5_
  80.6 1.0 copy-done.13
  81.5 18.7 %early.1 = (f32[960,1792]{1,0:T(8,128)}, bf16[960,1536]{1,0:T(8,128)(2,1)}) custom-call(bf16[2,960,256]{2,1,0:T(8,128)(2,1)} %copy-done.2, bf16[2,960,256]{2,1,0:T(8,128)(2,1)} %copy-done.10, bf16[2,960,256]{2,1,0:T(8,128)(2,1)} %copy-done.11, bf16[2,960,256]{2,1,0:T(8,128)(2,1)} %copy-done.12, bf16[6,960,256]{2,1,0:T(8,128)(2,1)} %collective-permute-done.11.refs_4_, ...), custom_call_target="tpu_custom_call" | custom-call | flops 1000 | bytes 1000 | tf_op jit(solution)/shard_map/early/pallas_call | solution.py:129
  100.2 4.7 %collective-permute-done.15.refs_2_.refs_16_.refs_9_ = bf16[512,1280]{1,0:T(8,128)(2,1)} collective-permute-done((bf16[512,1280]{1,0:T(8,128)(2,1)S(1)}, bf16[512,1280]{1,0:T(8,128)(2,1)}, u32[]{:S(2)}, u32[]{:S(2)}) %collective-permute-start.15) | collective-permute-done | bytes 1310752 | tf_op jit(solution)/shard_map/ppermute | solution.py:35
  105.0 1.5 collective-permute-done.14.refs_1_.refs_18_.refs_11_
  106.5 1.1 collective-permute-start.18
  107.5 0.9 collective-permute-start.17
  108.4 1.8 collective-permute-start.16
  110.2 12.1 %gelu_a.1 = (bf16[960,1792]{1,0:T(8,128)(2,1)}, bf16[960,1792]{1,0:T(8,128)(2,1)}) custom-call(bf16[960,1536]{1,0:T(8,128)(2,1)} %get-tuple-element.55.x_ref.refs_0_, f32[960,1792]{1,0:T(8,128)} %get-tuple-element.56.start_ref.refs_1_, bf16[960,1792]{1,0:T(8,128)(2,1)} %refs_2_.1, bf16[512,1280]{1,0:T(8,128)(2,1)} %collective-permute-done.13.refs_0_.refs_14_.refs_7_, ...), custom_call_target="tpu_custom_call" | custom-call | flops 1000 | bytes 1000 | tf_op jit(solution)/shard_map/gelu_a/pallas_call | solution.py:169
  123.3 11.9 %grad_far.1 = (bf16[2,960,256]{2,1,0:T(8,128)(2,1)}, bf16[2,960,256]{2,1,0:T(8,128)(2,1)}, bf16[960,1792]{1,0:T(8,128)(2,1)}, bf16[960,1792]{1,0:T(8,128)(2,1)}) custom-call(bf16[960,1792]{1,0:T(8,128)(2,1)} %get-tuple-element.58.s_hbm, bf16[960,1536]{1,0:T(8,128)(2,1)} %get-tuple-element.55.x_ref.refs_0_, ...), custom_call_target="tpu_custom_call", output_to_operand_aliasing={{2}: (0, {}), {3}: (7, {})} | custom-call | flops 1000 | bytes 1000 | tf_op jit(solution)/shard_map/grad_far/pallas_call | solution.py:311
  135.1 2.0 %collective-permute-start.19 = (bf16[2,960,256]{2,1,0:T(8,128)(2,1)}, bf16[2,960,256]{2,1,0:T(8,128)(2,1)S(1)}, u32[]{:S(2)}, u32[]{:S(2)}) collective-permute-start(bf16[2,960,256]{2,1,0:T(8,128)(2,1)} %get-tuple-element.65), channel_id=1, source_target_pairs={{0,1},{1,0},{2,3},{3,2},{4,5},{5,4},{6,7},{7,6},{8,9},{9,8},{10,11... | collective-permute-start | bytes 2949128 | tf_op jit(solution)/shard_map/ppermute | solution.py:35
  137.2 2.4 %collective-permute-done.19 = bf16[2,960,256]{2,1,0:T(8,128)(2,1)S(1)} collective-permute-done((bf16[2,960,256]{2,1,0:T(8,128)(2,1)}, bf16[2,960,256]{2,1,0:T(8,128)(2,1)S(1)}, u32[]{:S(2)}, u32[]{:S(2)}) %collective-permute-start.19) | collective-permute-done | bytes 983072 | tf_op jit(solution)/shard_map/ppermute | solution.py:35
  139.6 1.5 add_convert_fusion
  141.1 1.5 collective-permute-start.21
  142.6 1.2 collective-permute-start.22
  143.9 7.1 %grad_1.1 = (bf16[2,960,256]{2,1,0:T(8,128)(2,1)}, bf16[2,960,256]{2,1,0:T(8,128)(2,1)}) custom-call(bf16[960,1792]{1,0:T(8,128)(2,1)} %get-tuple-element.83.s_hbm, bf16[512,1792]{1,0:T(8,128)(2,1)} %refs_0_.5, bf16[512,1792]{1,0:T(8,128)(2,1)} %copy-done, bf16[512,1280]{1,0:T(8,128)(2,1)} %copy-done.5, ...), custom_call_target="tpu_custom_call" | custom-call | flops 1000 | bytes 1000 | tf_op jit(solution)/shard_map/grad_1/pallas_call | solution.py:311
  151.0 1.0 collective-permute-start.20
  152.0 2.8 %collective-permute-done.21.refs_0_ = bf16[2,480,256]{2,1,0:T(8,128)(2,1)S(1)} collective-permute-done((bf16[2,480,256]{2,1,0:T(8,128)(2,1)S(1)}, bf16[2,480,256]{2,1,0:T(8,128)(2,1)S(1)}, u32[]{:S(2)}, u32[]{:S(2)}) %collective-permute-start.21) | collective-permute-done | bytes 491552 | tf_op jit(solution)/shard_map/ppermute | solution.py:35
  154.8 1.3 add_1.1
  156.2 0.9 collective-permute-start.24
  157.0 1.8 collective-permute-start.25
  158.8 9.7 %grad_0.1 = (bf16[3,960,256]{2,1,0:T(8,128)(2,1)}, bf16[3,960,256]{2,1,0:T(8,128)(2,1)}) custom-call(bf16[960,1792]{1,0:T(8,128)(2,1)} %get-tuple-element.83.s_hbm, bf16[512,1792]{1,0:T(8,128)(2,1)} %refs_0_.5, bf16[512,1792]{1,0:T(8,128)(2,1)} %copy-done, bf16[512,1280]{1,0:T(8,128)(2,1)} %copy-done.5, ...), custom_call_target="tpu_custom_call" | custom-call | flops 1000 | bytes 1000 | tf_op jit(solution)/shard_map/grad_0/pallas_call | solution.py:311
  168.6 2.1 %collective-permute-start.23 = (bf16[3,960,256]{2,1,0:T(8,128)(2,1)}, bf16[3,960,256]{2,1,0:T(8,128)(2,1)S(1)}, u32[]{:S(2)}, u32[]{:S(2)}) collective-permute-start(bf16[3,960,256]{2,1,0:T(8,128)(2,1)} %get-tuple-element.77), channel_id=1, source_target_pairs={{0,1},{1,0},{2,3},{3,2},{4,5},{5,4},{6,7},{7,6},{8,9},{9,8},{10,11... | collective-permute-start | bytes 4423688 | tf_op jit(solution)/shard_map/ppermute | solution.py:35
  170.6 3.1 %collective-permute-done.23.back_ref = bf16[3,960,256]{2,1,0:T(8,128)(2,1)S(1)} collective-permute-done((bf16[3,960,256]{2,1,0:T(8,128)(2,1)}, bf16[3,960,256]{2,1,0:T(8,128)(2,1)S(1)}, u32[]{:S(2)}, u32[]{:S(2)}) %collective-permute-start.23) | collective-permute-done | bytes 1474592 | tf_op jit(solution)/shard_map/ppermute | solution.py:35
  173.8 1.7 add_0.1
  175.8 2.4 %collective-permute-start.28 = (bf16[960,256]{1,0:T(8,128)(2,1)}, bf16[960,256]{1,0:T(8,128)(2,1)S(1)}, u32[]{:S(2)}, u32[]{:S(2)}) collective-permute-start(bf16[960,256]{1,0:T(8,128)(2,1)} %get-tuple-element.81), channel_id=1, source_target_pairs={{0,12},{4,0},{8,4},{12,8},{1,13},{5,1},{9,5},{13,9},{2,14},{6,2},{... | collective-permute-start | bytes 1474568 | tf_op jit(solution)/shard_map/ppermute | solution.py:35
  178.1 5.1 %grad_own.1 = (bf16[1,960,256]{2,1,0:T(8,128)(2,1)}, bf16[1,960,256]{2,1,0:T(8,128)(2,1)}) custom-call(bf16[960,1792]{1,0:T(8,128)(2,1)} %get-tuple-element.83.s_hbm, bf16[512,1792]{1,0:T(8,128)(2,1)} %refs_0_.5, bf16[512,1792]{1,0:T(8,128)(2,1)} %copy-done, bf16[512,1280]{1,0:T(8,128)(2,1)} %copy-done.5, ...), custom_call_target="tpu_custom_call" | custom-call | flops 1000 | bytes 1000 | tf_op jit(solution)/shard_map/grad_own/pallas_call | solution.py:311
  183.2 1.3 collective-permute-start.26
  184.5 5.0 %collective-permute-done.29.refs_0_ = bf16[960,256]{1,0:T(8,128)(2,1)S(1)} collective-permute-done((bf16[960,256]{1,0:T(8,128)(2,1)}, bf16[960,256]{1,0:T(8,128)(2,1)S(1)}, u32[]{:S(2)}, u32[]{:S(2)}) %collective-permute-start.29) | collective-permute-done | bytes 491552 | tf_op jit(solution)/shard_map/ppermute | solution.py:35
  189.6 1.0 copy-done.15
  190.6 1.1 fusion.2
  (79 shorter events, 5.4 us)
Async XLA Ops:
  0.6 14.7 %copy-start.16 = (bf16[960,256]{1,0:T(8,128)(2,1)S(1)}, bf16[960,256]{1,0:T(8,128)(2,1)}, u32[]{:S(2)}) copy-start(bf16[960,256]{1,0:T(8,128)(2,1)} %param.5) | copy-start | bytes 1474564
  0.6 14.7 %collective-permute-start = (bf16[960,256]{1,0:T(8,128)(2,1)}, bf16[960,256]{1,0:T(8,128)(2,1)S(1)}, u32[]{:S(2)}, u32[]{:S(2)}) collective-permute-start(bf16[960,256]{1,0:T(8,128)(2,1)} %param.5), channel_id=1, source_target_pairs={{0,2},{2,0},{1,3},{3,1},{4,6},{6,4},{5,7},{7,5},{8,10},{10,8},{9,1... | collective-permute-start | bytes 1474568 | tf_op jit(solution)/shard_map/ppermute | solution.py:35
  4.5 42.4 %collective-permute-start.2 = (bf16[512,1792]{1,0:T(8,128)(2,1)}, bf16[512,1792]{1,0:T(8,128)(2,1)S(1)}, u32[]{:S(2)}, u32[]{:S(2)}) collective-permute-start(bf16[512,1792]{1,0:T(8,128)(2,1)} %refs_0_.5), channel_id=1, source_target_pairs={{0,48},{16,0},{32,16},{48,32},{1,49},{17,1},{33,17},{49,33},{2,50}... | collective-permute-start | bytes 5505032 | tf_op jit(solution)/shard_map/ppermute | solution.py:35
  8.2 41.7 %collective-permute-start.1 = (bf16[512,1792]{1,0:T(8,128)(2,1)}, bf16[512,1792]{1,0:T(8,128)(2,1)S(1)}, u32[]{:S(2)}, u32[]{:S(2)}) collective-permute-start(bf16[512,1792]{1,0:T(8,128)(2,1)} %refs_0_.5), channel_id=1, source_target_pairs={{0,16},{16,32},{32,48},{48,0},{1,17},{17,33},{33,49},{49,1},{2,18}... | collective-permute-start | bytes 5505032 | tf_op jit(solution)/shard_map/ppermute | solution.py:35
  9.7 34.2 %collective-permute-start.3 = (bf16[512,1280]{1,0:T(8,128)(2,1)S(1)}, bf16[512,1280]{1,0:T(8,128)(2,1)}, u32[]{:S(2)}, u32[]{:S(2)}) collective-permute-start(bf16[512,1280]{1,0:T(8,128)(2,1)S(1)} %slice.39), channel_id=1, source_target_pairs={{0,64},{64,0},{1,65},{65,1},{2,66},{66,2},{3,67},{67,3},{4,68},{68... | collective-permute-start | bytes 3932168 | tf_op jit(solution)/shard_map/ppermute | solution.py:35
  15.4 40.6 %copy-start.2 = (bf16[2,960,256]{2,1,0:T(8,128)(2,1)}, bf16[2,960,256]{2,1,0:T(8,128)(2,1)S(1)}, u32[]{:S(2)}) copy-start(bf16[2,960,256]{2,1,0:T(8,128)(2,1)S(1)} %mark.7.refs_0_) | copy-start | bytes 2949124
  15.5 34.6 %collective-permute-start.5 = (bf16[2,960,256]{2,1,0:T(8,128)(2,1)S(1)}, bf16[2,960,256]{2,1,0:T(8,128)(2,1)S(1)}, u32[]{:S(2)}, u32[]{:S(2)}) collective-permute-start(bf16[2,960,256]{2,1,0:T(8,128)(2,1)S(1)} %mark.7.refs_0_), channel_id=1, source_target_pairs={{0,12},{4,0},{8,4},{12,8},{1,13},{5,1},{9,5},{13,9},{2,14},{6,2},{... | collective-permute-start | bytes 2949128 | tf_op jit(solution)/shard_map/ppermute | solution.py:35
  18.0 32.1 %collective-permute-start.4 = (bf16[2,960,256]{2,1,0:T(8,128)(2,1)S(1)}, bf16[2,960,256]{2,1,0:T(8,128)(2,1)S(1)}, u32[]{:S(2)}, u32[]{:S(2)}) collective-permute-start(bf16[2,960,256]{2,1,0:T(8,128)(2,1)S(1)} %mark.7.refs_0_), channel_id=1, source_target_pairs={{0,4},{4,8},{8,12},{12,0},{1,5},{5,9},{9,13},{13,1},{2,6},{6,10},{... | collective-permute-start | bytes 2949128 | tf_op jit(solution)/shard_map/ppermute | solution.py:35
  49.9 3.0 %copy-start = (bf16[512,1792]{1,0:T(8,128)(2,1)}, bf16[512,1792]{1,0:T(8,128)(2,1)S(1)}, u32[]{:S(2)}) copy-start(bf16[512,1792]{1,0:T(8,128)(2,1)S(1)} %get-tuple-element.46.refs_8_.refs_1_) | copy-start | bytes 5505028
  49.9 3.0 %copy-start.1 = (bf16[512,1792]{1,0:T(8,128)(2,1)}, bf16[512,1792]{1,0:T(8,128)(2,1)S(1)}, u32[]{:S(2)}) copy-start(bf16[512,1792]{1,0:T(8,128)(2,1)S(1)} %get-tuple-element.45.refs_9_.refs_11_.refs_4_) | copy-start | bytes 5505028
  50.0 5.7 %copy-start.14 = (bf16[512,512]{1,0:T(8,128)(2,1)S(1)}, bf16[512,512]{1,0:T(8,128)(2,1)}, u32[]{:S(2)}) copy-start(bf16[512,512]{1,0:T(8,128)(2,1)} %slice.38) | copy-start | bytes 1572868
  50.1 6.3 %copy-start.10 = (bf16[2,960,256]{2,1,0:T(8,128)(2,1)}, bf16[2,960,256]{2,1,0:T(8,128)(2,1)S(1)}, u32[]{:S(2)}) copy-start(bf16[2,960,256]{2,1,0:T(8,128)(2,1)S(1)} %collective-permute-done.5.refs_1_) | copy-start | bytes 2949124
  50.1 6.3 %copy-start.11 = (bf16[2,960,256]{2,1,0:T(8,128)(2,1)}, bf16[2,960,256]{2,1,0:T(8,128)(2,1)S(1)}, u32[]{:S(2)}) copy-start(bf16[2,960,256]{2,1,0:T(8,128)(2,1)S(1)} %collective-permute-done.4.refs_2_) | copy-start | bytes 2949124
  50.1 21.0 %collective-permute-start.8 = (bf16[256,1792]{1,0:T(8,128)(2,1)S(1)}, bf16[256,1792]{1,0:T(8,128)(2,1)S(1)}, u32[]{:S(2)}, u32[]{:S(2)}) collective-permute-start(bf16[256,1792]{1,0:T(8,128)(2,1)S(1)} %slice.36), channel_id=1, source_target_pairs={{0,16},{16,32},{32,48},{48,0},{1,17},{17,33},{33,49},{49,1},{2,18}... | collective-permute-start | bytes 2752520 | tf_op jit(solution)/shard_map/ppermute | solution.py:35
  50.2 20.9 %collective-permute-start.9 = (bf16[256,1792]{1,0:T(8,128)(2,1)S(1)}, bf16[256,1792]{1,0:T(8,128)(2,1)S(1)}, u32[]{:S(2)}, u32[]{:S(2)}) collective-permute-start(bf16[256,1792]{1,0:T(8,128)(2,1)S(1)} %slice.37), channel_id=1, source_target_pairs={{0,48},{16,0},{32,16},{48,32},{1,49},{17,1},{33,17},{49,33},{2,50}... | collective-permute-start | bytes 2752520 | tf_op jit(solution)/shard_map/ppermute | solution.py:35
  52.9 11.3 %collective-permute-start.6 = (bf16[960,256]{1,0:T(8,128)(2,1)S(1)}, bf16[960,256]{1,0:T(8,128)(2,1)S(1)}, u32[]{:S(2)}, u32[]{:S(2)}) collective-permute-start(bf16[960,256]{1,0:T(8,128)(2,1)S(1)} %slice_bitcast_fusion.1), channel_id=1, source_target_pairs={{0,4},{4,8},{8,12},{12,0},{1,5},{5,9},{9,13},{13,1},{2,6},{6,10},{... | collective-permute-start | bytes 1474568 | tf_op jit(solution)/shard_map/ppermute | solution.py:35
  54.2 10.0 %collective-permute-start.7 = (bf16[960,256]{1,0:T(8,128)(2,1)S(1)}, bf16[960,256]{1,0:T(8,128)(2,1)S(1)}, u32[]{:S(2)}, u32[]{:S(2)}) collective-permute-start(bf16[960,256]{1,0:T(8,128)(2,1)S(1)} %slice_bitcast_fusion), channel_id=1, source_target_pairs={{0,12},{4,0},{8,4},{12,8},{1,13},{5,1},{9,5},{13,9},{2,14},{6,2},{... | collective-permute-start | bytes 1474568 | tf_op jit(solution)/shard_map/ppermute | solution.py:35
  55.7 10.1 %collective-permute-start.10 = (bf16[512,512]{1,0:T(8,128)(2,1)S(1)}, bf16[512,512]{1,0:T(8,128)(2,1)S(1)}, u32[]{:S(2)}, u32[]{:S(2)}) collective-permute-start(bf16[512,512]{1,0:T(8,128)(2,1)S(1)} %copy-done.14), channel_id=1, source_target_pairs={{0,64},{64,0},{1,65},{65,1},{2,66},{66,2},{3,67},{67,3},{4,68},{68... | collective-permute-start | bytes 1572872 | tf_op jit(solution)/shard_map/ppermute | solution.py:35
  64.3 13.2 %copy-start.12 = (bf16[2,960,256]{2,1,0:T(8,128)(2,1)}, bf16[2,960,256]{2,1,0:T(8,128)(2,1)S(1)}, u32[]{:S(2)}) copy-start(bf16[2,960,256]{2,1,0:T(8,128)(2,1)S(1)} %pad_maximum_fusion.3.refs_3_) | copy-start | bytes 2949124
  65.8 8.5 %copy-start.7 = (bf16[512,512]{1,0:T(8,128)(2,1)}, bf16[512,512]{1,0:T(8,128)(2,1)S(1)}, u32[]{:S(2)}) copy-start(bf16[512,512]{1,0:T(8,128)(2,1)S(1)} %collective-permute-done.10.refs_11_.refs_13_.refs_6_) | copy-start | bytes 1572868
  71.1 10.5 %collective-permute-start.11 = (bf16[6,960,256]{2,1,0:T(8,128)(2,1)S(1)}, bf16[6,960,256]{2,1,0:T(8,128)(2,1)}, u32[]{:S(2)}, u32[]{:S(2)}) collective-permute-start(bf16[6,960,256]{2,1,0:T(8,128)(2,1)S(1)} %pad_maximum_fusion), channel_id=1, source_target_pairs={{0,1},{1,0},{2,3},{3,2},{4,5},{5,4},{6,7},{7,6},{8,9},{9,8},{10,11... | collective-permute-start | bytes 8847368 | tf_op jit(solution)/shard_map/ppermute | solution.py:35
  74.4 7.2 %copy-start.5 = (bf16[512,1280]{1,0:T(8,128)(2,1)}, bf16[512,1280]{1,0:T(8,128)(2,1)S(1)}, u32[]{:S(2)}) copy-start(bf16[512,1280]{1,0:T(8,128)(2,1)S(1)} %pad_maximum_fusion.1.refs_12_.refs_9_.refs_2_) | copy-start | bytes 3932164
  74.4 30.6 %collective-permute-start.15 = (bf16[512,1280]{1,0:T(8,128)(2,1)S(1)}, bf16[512,1280]{1,0:T(8,128)(2,1)}, u32[]{:S(2)}, u32[]{:S(2)}) collective-permute-start(bf16[512,1280]{1,0:T(8,128)(2,1)S(1)} %pad_maximum_fusion.1.refs_12_.refs_9_.refs_2_), channel_id=1, source_target_pairs={{0,64},{64,0},{1,65},{65,1},{2,66},{66,2},{3,67},{67,3},{4,68},{68... | collective-permute-start | bytes 3932168 | tf_op jit(solution)/shard_map/ppermute | solution.py:35
  74.8 31.6 %collective-permute-start.14 = (bf16[512,1280]{1,0:T(8,128)(2,1)}, bf16[512,1280]{1,0:T(8,128)(2,1)}, u32[]{:S(2)}, u32[]{:S(2)}) collective-permute-start(bf16[512,1280]{1,0:T(8,128)(2,1)} %mark.9.refs_10_.refs_12_.refs_5_), channel_id=1, source_target_pairs={{0,16},{16,32},{32,48},{48,0},{1,17},{17,33},{33,49},{49,1},{2,18}... | collective-permute-start | bytes 3932168 | tf_op jit(solution)/shard_map/ppermute | solution.py:35
  74.8 31.6 %collective-permute-start.13 = (bf16[512,1280]{1,0:T(8,128)(2,1)}, bf16[512,1280]{1,0:T(8,128)(2,1)}, u32[]{:S(2)}, u32[]{:S(2)}) collective-permute-start(bf16[512,1280]{1,0:T(8,128)(2,1)} %mark.9.refs_10_.refs_12_.refs_5_), channel_id=1, source_target_pairs={{0,48},{16,0},{32,16},{48,32},{1,49},{17,1},{33,17},{49,33},{2,50}... | collective-permute-start | bytes 3932168 | tf_op jit(solution)/shard_map/ppermute | solution.py:35
  77.5 3.0 %collective-permute-start.12 = (bf16[2,960,256]{2,1,0:T(8,128)(2,1)S(1)}, bf16[2,960,256]{2,1,0:T(8,128)(2,1)S(1)}, u32[]{:S(2)}, u32[]{:S(2)}) collective-permute-start(bf16[2,960,256]{2,1,0:T(8,128)(2,1)S(1)} %pad_maximum_fusion.3.refs_3_), channel_id=1, source_target_pairs={{0,1},{1,0},{2,3},{3,2},{4,5},{5,4},{6,7},{7,6},{8,9},{9,8},{10,11... | collective-permute-start | bytes 2949128 | tf_op jit(solution)/shard_map/ppermute | solution.py:35
  79.2 27.2 %copy-start.6 = (bf16[512,512]{1,0:T(8,128)(2,1)S(1)}, bf16[512,512]{1,0:T(8,128)(2,1)}, u32[]{:S(2)}) copy-start(bf16[512,512]{1,0:T(8,128)(2,1)} %pad_maximum_fusion.4.refs_13_.refs_10_.refs_3_) | copy-start | bytes 1572868
  80.6 1.0 copy-start.13
  106.5 15.8 %collective-permute-start.18 = (bf16[512,512]{1,0:T(8,128)(2,1)S(1)}, bf16[512,512]{1,0:T(8,128)(2,1)S(1)}, u32[]{:S(2)}, u32[]{:S(2)}) collective-permute-start(bf16[512,512]{1,0:T(8,128)(2,1)S(1)} %copy-done.6), channel_id=1, source_target_pairs={{0,64},{64,0},{1,65},{65,1},{2,66},{66,2},{3,67},{67,3},{4,68},{68... | collective-permute-start | bytes 1572872 | tf_op jit(solution)/shard_map/ppermute | solution.py:35
  107.5 14.8 %collective-permute-start.17 = (bf16[512,512]{1,0:T(8,128)(2,1)}, bf16[512,512]{1,0:T(8,128)(2,1)S(1)}, u32[]{:S(2)}, u32[]{:S(2)}) collective-permute-start(bf16[512,512]{1,0:T(8,128)(2,1)} %copy-done.7), channel_id=1, source_target_pairs={{0,16},{16,32},{32,48},{48,0},{1,17},{17,33},{33,49},{49,1},{2,18}... | collective-permute-start | bytes 1572872 | tf_op jit(solution)/shard_map/ppermute | solution.py:35
  108.4 13.9 %collective-permute-start.16 = (bf16[512,512]{1,0:T(8,128)(2,1)}, bf16[512,512]{1,0:T(8,128)(2,1)}, u32[]{:S(2)}, u32[]{:S(2)}) collective-permute-start(bf16[512,512]{1,0:T(8,128)(2,1)} %copy-done.7), channel_id=1, source_target_pairs={{0,48},{16,0},{32,16},{48,32},{1,49},{17,1},{33,17},{49,33},{2,50}... | collective-permute-start | bytes 1572872 | tf_op jit(solution)/shard_map/ppermute | solution.py:35
  122.3 0.8 copy-start.8
  122.3 1.0 copy-start.9
  135.1 4.4 %collective-permute-start.19 = (bf16[2,960,256]{2,1,0:T(8,128)(2,1)}, bf16[2,960,256]{2,1,0:T(8,128)(2,1)S(1)}, u32[]{:S(2)}, u32[]{:S(2)}) collective-permute-start(bf16[2,960,256]{2,1,0:T(8,128)(2,1)} %get-tuple-element.65), channel_id=1, source_target_pairs={{0,1},{1,0},{2,3},{3,2},{4,5},{5,4},{6,7},{7,6},{8,9},{9,8},{10,11... | collective-permute-start | bytes 2949128 | tf_op jit(solution)/shard_map/ppermute | solution.py:35
  141.1 13.7 %collective-permute-start.21 = (bf16[2,480,256]{2,1,0:T(8,128)(2,1)S(1)}, bf16[2,480,256]{2,1,0:T(8,128)(2,1)S(1)}, u32[]{:S(2)}, u32[]{:S(2)}) collective-permute-start(bf16[2,480,256]{2,1,0:T(8,128)(2,1)S(1)} %get-tuple-element.66), channel_id=1, source_target_pairs={{0,4},{4,8},{8,12},{12,0},{1,5},{5,9},{9,13},{13,1},{2,6},{6,10},{... | collective-permute-start | bytes 1474568 | tf_op jit(solution)/shard_map/ppermute | solution.py:35
  142.6 12.2 %collective-permute-start.22 = (bf16[2,480,256]{2,1,0:T(8,128)(2,1)S(1)}, bf16[2,480,256]{2,1,0:T(8,128)(2,1)S(1)}, u32[]{:S(2)}, u32[]{:S(2)}) collective-permute-start(bf16[2,480,256]{2,1,0:T(8,128)(2,1)S(1)} %get-tuple-element.67), channel_id=1, source_target_pairs={{0,12},{4,0},{8,4},{12,8},{1,13},{5,1},{9,5},{13,9},{2,14},{6,2},{... | collective-permute-start | bytes 1474568 | tf_op jit(solution)/shard_map/ppermute | solution.py:35
  151.0 3.8 %copy-start.4 = (bf16[2,960,256]{2,1,0:T(8,128)(2,1)S(1)}, bf16[2,960,256]{2,1,0:T(8,128)(2,1)}, u32[]{:S(2)}) copy-start(bf16[2,960,256]{2,1,0:T(8,128)(2,1)} %get-tuple-element.69.mine_ref) | copy-start | bytes 2949124
  151.0 3.8 %collective-permute-start.20 = (bf16[2,960,256]{2,1,0:T(8,128)(2,1)}, bf16[2,960,256]{2,1,0:T(8,128)(2,1)S(1)}, u32[]{:S(2)}, u32[]{:S(2)}) collective-permute-start(bf16[2,960,256]{2,1,0:T(8,128)(2,1)} %get-tuple-element.70), channel_id=1, source_target_pairs={{0,1},{1,0},{2,3},{3,2},{4,5},{5,4},{6,7},{7,6},{8,9},{9,8},{10,11... | collective-permute-start | bytes 2949128 | tf_op jit(solution)/shard_map/ppermute | solution.py:35
  156.2 14.5 %collective-permute-start.24 = (bf16[960,256]{1,0:T(8,128)(2,1)}, bf16[960,256]{1,0:T(8,128)(2,1)S(1)}, u32[]{:S(2)}, u32[]{:S(2)}) collective-permute-start(bf16[960,256]{1,0:T(8,128)(2,1)} %get-tuple-element.73), channel_id=1, source_target_pairs={{0,4},{4,8},{8,12},{12,0},{1,5},{5,9},{9,13},{13,1},{2,6},{6,10},{... | collective-permute-start | bytes 1474568 | tf_op jit(solution)/shard_map/ppermute | solution.py:35
  157.0 13.6 %collective-permute-start.25 = (bf16[960,256]{1,0:T(8,128)(2,1)}, bf16[960,256]{1,0:T(8,128)(2,1)S(1)}, u32[]{:S(2)}, u32[]{:S(2)}) collective-permute-start(bf16[960,256]{1,0:T(8,128)(2,1)} %get-tuple-element.74), channel_id=1, source_target_pairs={{0,12},{4,0},{8,4},{12,8},{1,13},{5,1},{9,5},{13,9},{2,14},{6,2},{... | collective-permute-start | bytes 1474568 | tf_op jit(solution)/shard_map/ppermute | solution.py:35
  168.5 5.2 %copy-start.3 = (bf16[3,960,256]{2,1,0:T(8,128)(2,1)S(1)}, bf16[3,960,256]{2,1,0:T(8,128)(2,1)}, u32[]{:S(2)}) copy-start(bf16[3,960,256]{2,1,0:T(8,128)(2,1)} %get-tuple-element.76.mine_ref) | copy-start | bytes 4423684
  168.6 5.2 %collective-permute-start.23 = (bf16[3,960,256]{2,1,0:T(8,128)(2,1)}, bf16[3,960,256]{2,1,0:T(8,128)(2,1)S(1)}, u32[]{:S(2)}, u32[]{:S(2)}) collective-permute-start(bf16[3,960,256]{2,1,0:T(8,128)(2,1)} %get-tuple-element.77), channel_id=1, source_target_pairs={{0,1},{1,0},{2,3},{3,2},{4,5},{5,4},{6,7},{7,6},{8,9},{9,8},{10,11... | collective-permute-start | bytes 4423688 | tf_op jit(solution)/shard_map/ppermute | solution.py:35
  175.4 14.2 %collective-permute-start.29 = (bf16[960,256]{1,0:T(8,128)(2,1)}, bf16[960,256]{1,0:T(8,128)(2,1)S(1)}, u32[]{:S(2)}, u32[]{:S(2)}) collective-permute-start(bf16[960,256]{1,0:T(8,128)(2,1)} %get-tuple-element.82), channel_id=1, source_target_pairs={{0,2},{2,0},{1,3},{3,1},{4,6},{6,4},{5,7},{7,5},{8,10},{10,8},{9,1... | collective-permute-start | bytes 1474568 | tf_op jit(solution)/shard_map/ppermute | solution.py:35
  175.5 14.1 %collective-permute-start.27 = (bf16[960,256]{1,0:T(8,128)(2,1)}, bf16[960,256]{1,0:T(8,128)(2,1)S(1)}, u32[]{:S(2)}, u32[]{:S(2)}) collective-permute-start(bf16[960,256]{1,0:T(8,128)(2,1)} %get-tuple-element.80), channel_id=1, source_target_pairs={{0,4},{4,8},{8,12},{12,0},{1,5},{5,9},{9,13},{13,1},{2,6},{6,10},{... | collective-permute-start | bytes 1474568 | tf_op jit(solution)/shard_map/ppermute | solution.py:35
  175.8 13.8 %collective-permute-start.28 = (bf16[960,256]{1,0:T(8,128)(2,1)}, bf16[960,256]{1,0:T(8,128)(2,1)S(1)}, u32[]{:S(2)}, u32[]{:S(2)}) collective-permute-start(bf16[960,256]{1,0:T(8,128)(2,1)} %get-tuple-element.81), channel_id=1, source_target_pairs={{0,12},{4,0},{8,4},{12,8},{1,13},{5,1},{9,5},{13,9},{2,14},{6,2},{... | collective-permute-start | bytes 1474568 | tf_op jit(solution)/shard_map/ppermute | solution.py:35
  183.2 6.4 %collective-permute-start.26 = (bf16[1,960,256]{2,1,0:T(8,128)(2,1)}, bf16[1,960,256]{2,1,0:T(8,128)(2,1)S(1)}, u32[]{:S(2)}, u32[]{:S(2)}) collective-permute-start(bf16[1,960,256]{2,1,0:T(8,128)(2,1)} %get-tuple-element.85), channel_id=1, source_target_pairs={{0,1},{1,0},{2,3},{3,2},{4,5},{5,4},{6,7},{7,6},{8,9},{9,8},{10,11... | collective-permute-start | bytes 1474568 | tf_op jit(solution)/shard_map/ppermute | solution.py:35
  189.6 1.0 copy-start.15

commit v5 on v4

--- a/solution.py
+++ b/solution.py
@@ -28,6 +28,7 @@
 
 
 DEAR = flops(4 * 10**10)
+SOME = flops(2 * 10**10)
 
 
 def shift(value, axis, by, size):
@@ -330,7 +331,7 @@
     )(slope, *(last_args if last is not None else []), *arrays)
 
 
-def mark(cost, *arrays):
+def mark(cost, *arrays, limit=SMALL_LIMIT):
     n = len(arrays)
     any_space = [pl.BlockSpec(memory_space=pl.ANY)] * n
     return pl.pallas_call(
@@ -339,7 +340,7 @@
         out_specs=any_space,
         out_shape=[jax.ShapeDtypeStruct(a.shape, a.dtype) for a in arrays],
         input_output_aliases={i: i for i in range(n)},
-        compiler_params=pltpu.CompilerParams(vmem_limit_bytes=SMALL_LIMIT),
+        compiler_params=pltpu.CompilerParams(vmem_limit_bytes=limit),
         cost_estimate=cost,
         name="mark",
     )(*arrays)
@@ -423,9 +424,9 @@
         ((0, 0), (0, 1), (0, 3), (1, 0), (0, 2)), ((1, 1), (1, 3), (1, 2)), mine, theirs, carried_sum,
         [(w_panels,), (z_plus,), (z_minus,), (other_a, other_b), (far_a, far_b)],
     )
-    send_b, send_far_b = lax.optimization_barrier(
-        (other_b, far_b, other_minus_a, other_plus_a, other_far_a, total)
-    )[:2]
+    other_minus_a, other_plus_a = mark(SOME, other_minus_a, other_plus_a, limit=VMEM_LIMIT)
+    send_b = after(other_b, total)
+    send_far_b = after(far_b, other_far_a, total)
     other_minus_b = shift(send_b, "z", 1, NZ)
     other_plus_b = shift(send_b, "z", -1, NZ)
     other_far_b = shift(send_far_b, "y_lo", 1, 2)

time: 192 us -> 191 us (level)
  transfers between devices with their start and end apart: 30 -> 30, of which waited for: 14 -> 16; matrix products, arithmetic and copies ran while one was open for 3% -> 3% of each run, Pallas kernels for 27% -> 28%
where the time goes in v5:
time: 191 us
  waiting for transfers between devices  69.4 us (36%)
  Pallas kernels  67.6 us (35%)
  starting transfers between devices  42.5 us (22%)
  local copies, waits for them, and re-layouts  6.19 us (3%)
  other arithmetic  4.01 us (2%)
    ppermute x30, waiting for transfers between devices, shift(): return lax.ppermute(value, axis, pairs)  69.4 us
    ppermute x30, starting transfers between devices, shift(): return lax.ppermute(value, axis, pairs)  42.5 us
    pallas_call x4, Pallas kernels, gradient(): pl.pallas_call(kernel, in_specs=[hbm] * (1 + n_last + len(arrays)), out_s...  33.8 us
    pallas_call x1, Pallas kernels, forward_early(): pl.pallas_call(kernel, grid=(width // LANES,), in_specs=[hbm] * n_p + [ti...  18.7 us
    pallas_call x1, Pallas kernels, forward_late(): pl.pallas_call(kernel, grid=(cols // LANES,), in_specs=[pl.BlockSpec((tok...  12.1 us
  transfers between devices with their start and end apart: 30, of which 16 were waited for; matrix products, arithmetic and copies ran while one was open for 3% of the time, Pallas kernels for 28%

profile of v5, /device:TPU:1, one launch (start us, length us, event | category | flops | bytes accessed | tf_op | source)
XLA Modules:
  0.0 190.7 jit_solution(17788834454547961186)
XLA Ops:
  0.6 3.8 %collective-permute-start = (bf16[960,256]{1,0:T(8,128)(2,1)}, bf16[960,256]{1,0:T(8,128)(2,1)S(1)}, u32[]{:S(2)}, u32[]{:S(2)}) collective-permute-start(bf16[960,256]{1,0:T(8,128)(2,1)} %param.5), channel_id=1, source_target_pairs={{0,2},{2,0},{1,3},{3,1},{4,6},{6,4},{5,7},{7,5},{8,10},{10,8},{9,1... | collective-permute-start | bytes 1474568 | tf_op jit(solution)/shard_map/ppermute | solution.py:36
  4.5 3.8 %collective-permute-start.2 = (bf16[512,1792]{1,0:T(8,128)(2,1)}, bf16[512,1792]{1,0:T(8,128)(2,1)S(1)}, u32[]{:S(2)}, u32[]{:S(2)}) collective-permute-start(bf16[512,1792]{1,0:T(8,128)(2,1)} %refs_0_.5), channel_id=1, source_target_pairs={{0,48},{16,0},{32,16},{48,32},{1,49},{17,1},{33,17},{49,33},{2,50}... | collective-permute-start | bytes 5505032 | tf_op jit(solution)/shard_map/ppermute | solution.py:36
  8.2 1.5 slice.39
  10.2 1.9 slice.38
  12.0 3.3 %collective-permute-done = bf16[960,256]{1,0:T(8,128)(2,1)S(1)} collective-permute-done((bf16[960,256]{1,0:T(8,128)(2,1)}, bf16[960,256]{1,0:T(8,128)(2,1)S(1)}, u32[]{:S(2)}, u32[]{:S(2)}) %collective-permute-start) | collective-permute-done | bytes 491552 | tf_op jit(solution)/shard_map/ppermute | solution.py:36
  15.5 2.6 %collective-permute-start.5 = (bf16[2,960,256]{2,1,0:T(8,128)(2,1)S(1)}, bf16[2,960,256]{2,1,0:T(8,128)(2,1)S(1)}, u32[]{:S(2)}, u32[]{:S(2)}) collective-permute-start(bf16[2,960,256]{2,1,0:T(8,128)(2,1)S(1)} %mark.8.refs_0_), channel_id=1, source_target_pairs={{0,12},{4,0},{8,4},{12,8},{1,13},{5,1},{9,5},{13,9},{2,14},{6,2},{... | collective-permute-start | bytes 2949128 | tf_op jit(solution)/shard_map/ppermute | solution.py:36
  18.0 25.9 %collective-permute-done.3.refs_0_ = bf16[512,1280]{1,0:T(8,128)(2,1)} collective-permute-done((bf16[512,1280]{1,0:T(8,128)(2,1)S(1)}, bf16[512,1280]{1,0:T(8,128)(2,1)}, u32[]{:S(2)}, u32[]{:S(2)}) %collective-permute-start.3) | collective-permute-done | bytes 1310752 | tf_op jit(solution)/shard_map/ppermute | solution.py:36
  43.9 3.0 %collective-permute-done.2.refs_1_ = bf16[512,1792]{1,0:T(8,128)(2,1)S(1)} collective-permute-done((bf16[512,1792]{1,0:T(8,128)(2,1)}, bf16[512,1792]{1,0:T(8,128)(2,1)S(1)}, u32[]{:S(2)}, u32[]{:S(2)}) %collective-permute-start.2) | collective-permute-done | bytes 1835040 | tf_op jit(solution)/shard_map/ppermute | solution.py:36
  46.9 3.0 %collective-permute-done.1.refs_0_ = bf16[512,1792]{1,0:T(8,128)(2,1)S(1)} collective-permute-done((bf16[512,1792]{1,0:T(8,128)(2,1)}, bf16[512,1792]{1,0:T(8,128)(2,1)S(1)}, u32[]{:S(2)}, u32[]{:S(2)}) %collective-permute-start.1) | collective-permute-done | bytes 1835040 | tf_op jit(solution)/shard_map/ppermute | solution.py:36
  50.2 2.7 %collective-permute-start.9 = (bf16[256,1792]{1,0:T(8,128)(2,1)S(1)}, bf16[256,1792]{1,0:T(8,128)(2,1)S(1)}, u32[]{:S(2)}, u32[]{:S(2)}) collective-permute-start(bf16[256,1792]{1,0:T(8,128)(2,1)S(1)} %slice.37), channel_id=1, source_target_pairs={{0,48},{16,0},{32,16},{48,32},{1,49},{17,1},{33,17},{49,33},{2,50}... | collective-permute-start | bytes 2752520 | tf_op jit(solution)/shard_map/ppermute | solution.py:36
  52.9 1.3 collective-permute-start.6
  54.2 1.5 collective-permute-start.7
  56.4 7.8 %collective-permute-done.6 = bf16[960,256]{1,0:T(8,128)(2,1)S(1)} collective-permute-done((bf16[960,256]{1,0:T(8,128)(2,1)S(1)}, bf16[960,256]{1,0:T(8,128)(2,1)S(1)}, u32[]{:S(2)}, u32[]{:S(2)}) %collective-permute-start.6) | collective-permute-done | bytes 491552 | tf_op jit(solution)/shard_map/ppermute | solution.py:36
  64.3 1.5 collective-permute-done.10.refs_11_.refs_13_.refs_6_
  65.8 5.2 %collective-permute-done.8 = bf16[256,1792]{1,0:T(8,128)(2,1)S(1)} collective-permute-done((bf16[256,1792]{1,0:T(8,128)(2,1)S(1)}, bf16[256,1792]{1,0:T(8,128)(2,1)S(1)}, u32[]{:S(2)}, u32[]{:S(2)}) %collective-permute-start.8) | collective-permute-done | bytes 917536 | tf_op jit(solution)/shard_map/ppermute | solution.py:36
  71.1 3.1 %collective-permute-start.11 = (bf16[6,960,256]{2,1,0:T(8,128)(2,1)S(1)}, bf16[6,960,256]{2,1,0:T(8,128)(2,1)}, u32[]{:S(2)}, u32[]{:S(2)}) collective-permute-start(bf16[6,960,256]{2,1,0:T(8,128)(2,1)S(1)} %pad_maximum_fusion), channel_id=1, source_target_pairs={{0,1},{1,0},{2,3},{3,2},{4,5},{5,4},{6,7},{7,6},{8,9},{9,8},{10,11... | collective-permute-start | bytes 8847368 | tf_op jit(solution)/shard_map/ppermute | solution.py:36
  74.8 2.7 %collective-permute-start.14 = (bf16[512,1280]{1,0:T(8,128)(2,1)}, bf16[512,1280]{1,0:T(8,128)(2,1)}, u32[]{:S(2)}, u32[]{:S(2)}) collective-permute-start(bf16[512,1280]{1,0:T(8,128)(2,1)} %mark.10.refs_10_.refs_12_.refs_5_), channel_id=1, source_target_pairs={{0,48},{16,0},{32,16},{48,32},{1,49},{17,1},{33,17},{49,33},{2,50}... | collective-permute-start | bytes 3932168 | tf_op jit(solution)/shard_map/ppermute | solution.py:36
  78.1 0.8 pad_maximum_fusion.4.refs_13_.refs_10_.refs_3_
  79.0 1.6 collective-permute-done.12.refs_5_
  80.6 1.0 copy-done.12
  81.5 18.7 %early.1 = (f32[960,1792]{1,0:T(8,128)}, bf16[960,1536]{1,0:T(8,128)(2,1)}) custom-call(bf16[2,960,256]{2,1,0:T(8,128)(2,1)} %copy-done.2, bf16[2,960,256]{2,1,0:T(8,128)(2,1)} %copy-done.9, bf16[2,960,256]{2,1,0:T(8,128)(2,1)} %copy-done.10, bf16[2,960,256]{2,1,0:T(8,128)(2,1)} %copy-done.11, bf16[6,960,256]{2,1,0:T(8,128)(2,1)} %collective-permute-done.11.refs_4_, ...), custom_call_target="tpu_custom_call" | custom-call | flops 1000 | bytes 1000 | tf_op jit(solution)/shard_map/early/pallas_call | solution.py:130
  100.3 2.7 %collective-permute-start.16 = (bf16[512,512]{1,0:T(8,128)(2,1)}, bf16[512,512]{1,0:T(8,128)(2,1)}, u32[]{:S(2)}, u32[]{:S(2)}) collective-permute-start(bf16[512,512]{1,0:T(8,128)(2,1)} %copy-done.7), channel_id=1, source_target_pairs={{0,48},{16,0},{32,16},{48,32},{1,49},{17,1},{33,17},{49,33},{2,50}... | collective-permute-start | bytes 1572872 | tf_op jit(solution)/shard_map/ppermute | solution.py:36
  103.1 1.9 collective-permute-done.15.refs_2_.refs_16_.refs_9_
  105.7 3.1 %collective-permute-done.13.refs_0_ = bf16[512,1280]{1,0:T(8,128)(2,1)} collective-permute-done((bf16[512,1280]{1,0:T(8,128)(2,1)}, bf16[512,1280]{1,0:T(8,128)(2,1)}, u32[]{:S(2)}, u32[]{:S(2)}) %collective-permute-start.13) | collective-permute-done | bytes 1310752 | tf_op jit(solution)/shard_map/ppermute | solution.py:36
  108.8 12.1 %gelu_a.1 = (bf16[960,1792]{1,0:T(8,128)(2,1)}, bf16[960,1792]{1,0:T(8,128)(2,1)}) custom-call(bf16[960,1536]{1,0:T(8,128)(2,1)} %get-tuple-element.57.x_ref.refs_0_, f32[960,1792]{1,0:T(8,128)} %get-tuple-element.58.start_ref.refs_1_, bf16[960,1792]{1,0:T(8,128)(2,1)} %refs_2_.1, bf16[512,1280]{1,0:T(8,128)(2,1)} %get-tuple-element.60.refs_0_.refs_14_.refs_7_, ...), custom_call_target="tpu_custom_call" | custom-call | flops 1000 | bytes 1000 | tf_op jit(solution)/shard_map/gelu_a/pallas_call | solution.py:170
  120.9 0.8 copy-done.8
  121.7 11.8 %grad_far.1 = (bf16[2,960,256]{2,1,0:T(8,128)(2,1)}, bf16[2,960,256]{2,1,0:T(8,128)(2,1)}, bf16[960,1792]{1,0:T(8,128)(2,1)}, bf16[960,1792]{1,0:T(8,128)(2,1)}) custom-call(bf16[960,1792]{1,0:T(8,128)(2,1)} %get-tuple-element.62.s_hbm, bf16[960,1536]{1,0:T(8,128)(2,1)} %get-tuple-element.57.x_ref.refs_0_, ...), custom_call_target="tpu_custom_call", output_to_operand_aliasing={{2}: (0, {}), {3}: (7, {})} | custom-call | flops 1000 | bytes 1000 | tf_op jit(solution)/shard_map/grad_far/pallas_call | solution.py:312
  133.6 2.5 %collective-permute-start.19 = (bf16[2,960,256]{2,1,0:T(8,128)(2,1)}, bf16[2,960,256]{2,1,0:T(8,128)(2,1)S(1)}, u32[]{:S(2)}, u32[]{:S(2)}) collective-permute-start(bf16[2,960,256]{2,1,0:T(8,128)(2,1)} %get-tuple-element.69), channel_id=1, source_target_pairs={{0,1},{1,0},{2,3},{3,2},{4,5},{5,4},{6,7},{7,6},{8,9},{9,8},{10,11... | collective-permute-start | bytes 2949128 | tf_op jit(solution)/shard_map/ppermute | solution.py:36
  136.1 2.4 %collective-permute-done.19 = bf16[2,960,256]{2,1,0:T(8,128)(2,1)S(1)} collective-permute-done((bf16[2,960,256]{2,1,0:T(8,128)(2,1)}, bf16[2,960,256]{2,1,0:T(8,128)(2,1)S(1)}, u32[]{:S(2)}, u32[]{:S(2)}) %collective-permute-start.19) | collective-permute-done | bytes 983072 | tf_op jit(solution)/shard_map/ppermute | solution.py:36
  138.5 1.5 add_convert_fusion
  140.1 1.5 collective-permute-start.21
  141.6 1.2 collective-permute-start.22
  142.8 7.1 %grad_1.1 = (bf16[2,960,256]{2,1,0:T(8,128)(2,1)}, bf16[2,960,256]{2,1,0:T(8,128)(2,1)}) custom-call(bf16[960,1792]{1,0:T(8,128)(2,1)} %get-tuple-element.87.s_hbm, bf16[512,1792]{1,0:T(8,128)(2,1)} %refs_0_.5, bf16[512,1792]{1,0:T(8,128)(2,1)} %copy-done, bf16[512,1280]{1,0:T(8,128)(2,1)} %copy-done.5, ...), custom_call_target="tpu_custom_call" | custom-call | flops 1000 | bytes 1000 | tf_op jit(solution)/shard_map/grad_1/pallas_call | solution.py:312
  150.0 1.0 collective-permute-start.20
  151.0 2.8 %collective-permute-done.21.refs_0_ = bf16[2,480,256]{2,1,0:T(8,128)(2,1)S(1)} collective-permute-done((bf16[2,480,256]{2,1,0:T(8,128)(2,1)S(1)}, bf16[2,480,256]{2,1,0:T(8,128)(2,1)S(1)}, u32[]{:S(2)}, u32[]{:S(2)}) %collective-permute-start.21) | collective-permute-done | bytes 491552 | tf_op jit(solution)/shard_map/ppermute | solution.py:36
  153.8 1.3 add_1.1
  155.1 0.9 collective-permute-start.24
  156.0 1.8 collective-permute-start.25
  157.8 9.7 %grad_0.1 = (bf16[3,960,256]{2,1,0:T(8,128)(2,1)}, bf16[3,960,256]{2,1,0:T(8,128)(2,1)}) custom-call(bf16[960,1792]{1,0:T(8,128)(2,1)} %get-tuple-element.87.s_hbm, bf16[512,1792]{1,0:T(8,128)(2,1)} %refs_0_.5, bf16[512,1792]{1,0:T(8,128)(2,1)} %copy-done, bf16[512,1280]{1,0:T(8,128)(2,1)} %copy-done.5, ...), custom_call_target="tpu_custom_call" | custom-call | flops 1000 | bytes 1000 | tf_op jit(solution)/shard_map/grad_0/pallas_call | solution.py:312
  167.5 2.1 %collective-permute-start.23 = (bf16[3,960,256]{2,1,0:T(8,128)(2,1)}, bf16[3,960,256]{2,1,0:T(8,128)(2,1)S(1)}, u32[]{:S(2)}, u32[]{:S(2)}) collective-permute-start(bf16[3,960,256]{2,1,0:T(8,128)(2,1)} %get-tuple-element.81), channel_id=1, source_target_pairs={{0,1},{1,0},{2,3},{3,2},{4,5},{5,4},{6,7},{7,6},{8,9},{9,8},{10,11... | collective-permute-start | bytes 4423688 | tf_op jit(solution)/shard_map/ppermute | solution.py:36
  169.6 3.1 %collective-permute-done.23.back_ref = bf16[3,960,256]{2,1,0:T(8,128)(2,1)S(1)} collective-permute-done((bf16[3,960,256]{2,1,0:T(8,128)(2,1)}, bf16[3,960,256]{2,1,0:T(8,128)(2,1)S(1)}, u32[]{:S(2)}, u32[]{:S(2)}) %collective-permute-start.23) | collective-permute-done | bytes 1474592 | tf_op jit(solution)/shard_map/ppermute | solution.py:36
  172.7 1.7 add_0.1
  174.4 1.0 collective-permute-start.29
  175.7 2.3 %collective-permute-start.28 = (bf16[960,256]{1,0:T(8,128)(2,1)}, bf16[960,256]{1,0:T(8,128)(2,1)S(1)}, u32[]{:S(2)}, u32[]{:S(2)}) collective-permute-start(bf16[960,256]{1,0:T(8,128)(2,1)} %get-tuple-element.85), channel_id=1, source_target_pairs={{0,12},{4,0},{8,4},{12,8},{1,13},{5,1},{9,5},{13,9},{2,14},{6,2},{... | collective-permute-start | bytes 1474568 | tf_op jit(solution)/shard_map/ppermute | solution.py:36
  178.0 5.1 %grad_own.1 = (bf16[1,960,256]{2,1,0:T(8,128)(2,1)}, bf16[1,960,256]{2,1,0:T(8,128)(2,1)}) custom-call(bf16[960,1792]{1,0:T(8,128)(2,1)} %get-tuple-element.87.s_hbm, bf16[512,1792]{1,0:T(8,128)(2,1)} %refs_0_.5, bf16[512,1792]{1,0:T(8,128)(2,1)} %copy-done, bf16[512,1280]{1,0:T(8,128)(2,1)} %copy-done.5, ...), custom_call_target="tpu_custom_call" | custom-call | flops 1000 | bytes 1000 | tf_op jit(solution)/shard_map/grad_own/pallas_call | solution.py:312
  183.1 1.3 collective-permute-start.26
  184.4 4.1 %collective-permute-done.29.refs_0_ = bf16[960,256]{1,0:T(8,128)(2,1)S(1)} collective-permute-done((bf16[960,256]{1,0:T(8,128)(2,1)}, bf16[960,256]{1,0:T(8,128)(2,1)S(1)}, u32[]{:S(2)}, u32[]{:S(2)}) %collective-permute-start.29) | collective-permute-done | bytes 491552 | tf_op jit(solution)/shard_map/ppermute | solution.py:36
  189.6 1.1 fusion.2
  (78 shorter events, 5.3 us)
Async XLA Ops:
  0.6 14.7 %copy-start.15 = (bf16[960,256]{1,0:T(8,128)(2,1)S(1)}, bf16[960,256]{1,0:T(8,128)(2,1)}, u32[]{:S(2)}) copy-start(bf16[960,256]{1,0:T(8,128)(2,1)} %param.5) | copy-start | bytes 1474564
  0.6 14.7 %collective-permute-start = (bf16[960,256]{1,0:T(8,128)(2,1)}, bf16[960,256]{1,0:T(8,128)(2,1)S(1)}, u32[]{:S(2)}, u32[]{:S(2)}) collective-permute-start(bf16[960,256]{1,0:T(8,128)(2,1)} %param.5), channel_id=1, source_target_pairs={{0,2},{2,0},{1,3},{3,1},{4,6},{6,4},{5,7},{7,5},{8,10},{10,8},{9,1... | collective-permute-start | bytes 1474568 | tf_op jit(solution)/shard_map/ppermute | solution.py:36
  4.5 42.4 %collective-permute-start.2 = (bf16[512,1792]{1,0:T(8,128)(2,1)}, bf16[512,1792]{1,0:T(8,128)(2,1)S(1)}, u32[]{:S(2)}, u32[]{:S(2)}) collective-permute-start(bf16[512,1792]{1,0:T(8,128)(2,1)} %refs_0_.5), channel_id=1, source_target_pairs={{0,48},{16,0},{32,16},{48,32},{1,49},{17,1},{33,17},{49,33},{2,50}... | collective-permute-start | bytes 5505032 | tf_op jit(solution)/shard_map/ppermute | solution.py:36
  8.2 41.7 %collective-permute-start.1 = (bf16[512,1792]{1,0:T(8,128)(2,1)}, bf16[512,1792]{1,0:T(8,128)(2,1)S(1)}, u32[]{:S(2)}, u32[]{:S(2)}) collective-permute-start(bf16[512,1792]{1,0:T(8,128)(2,1)} %refs_0_.5), channel_id=1, source_target_pairs={{0,16},{16,32},{32,48},{48,0},{1,17},{17,33},{33,49},{49,1},{2,18}... | collective-permute-start | bytes 5505032 | tf_op jit(solution)/shard_map/ppermute | solution.py:36
  9.7 34.2 %collective-permute-start.3 = (bf16[512,1280]{1,0:T(8,128)(2,1)S(1)}, bf16[512,1280]{1,0:T(8,128)(2,1)}, u32[]{:S(2)}, u32[]{:S(2)}) collective-permute-start(bf16[512,1280]{1,0:T(8,128)(2,1)S(1)} %slice.39), channel_id=1, source_target_pairs={{0,64},{64,0},{1,65},{65,1},{2,66},{66,2},{3,67},{67,3},{4,68},{68... | collective-permute-start | bytes 3932168 | tf_op jit(solution)/shard_map/ppermute | solution.py:36
  15.4 40.6 %copy-start.2 = (bf16[2,960,256]{2,1,0:T(8,128)(2,1)}, bf16[2,960,256]{2,1,0:T(8,128)(2,1)S(1)}, u32[]{:S(2)}) copy-start(bf16[2,960,256]{2,1,0:T(8,128)(2,1)S(1)} %mark.8.refs_0_) | copy-start | bytes 2949124
  15.5 34.6 %collective-permute-start.5 = (bf16[2,960,256]{2,1,0:T(8,128)(2,1)S(1)}, bf16[2,960,256]{2,1,0:T(8,128)(2,1)S(1)}, u32[]{:S(2)}, u32[]{:S(2)}) collective-permute-start(bf16[2,960,256]{2,1,0:T(8,128)(2,1)S(1)} %mark.8.refs_0_), channel_id=1, source_target_pairs={{0,12},{4,0},{8,4},{12,8},{1,13},{5,1},{9,5},{13,9},{2,14},{6,2},{... | collective-permute-start | bytes 2949128 | tf_op jit(solution)/shard_map/ppermute | solution.py:36
  18.0 32.1 %collective-permute-start.4 = (bf16[2,960,256]{2,1,0:T(8,128)(2,1)S(1)}, bf16[2,960,256]{2,1,0:T(8,128)(2,1)S(1)}, u32[]{:S(2)}, u32[]{:S(2)}) collective-permute-start(bf16[2,960,256]{2,1,0:T(8,128)(2,1)S(1)} %mark.8.refs_0_), channel_id=1, source_target_pairs={{0,4},{4,8},{8,12},{12,0},{1,5},{5,9},{9,13},{13,1},{2,6},{6,10},{... | collective-permute-start | bytes 2949128 | tf_op jit(solution)/shard_map/ppermute | solution.py:36
  49.9 3.0 %copy-start = (bf16[512,1792]{1,0:T(8,128)(2,1)}, bf16[512,1792]{1,0:T(8,128)(2,1)S(1)}, u32[]{:S(2)}) copy-start(bf16[512,1792]{1,0:T(8,128)(2,1)S(1)} %get-tuple-element.48.refs_8_.refs_1_) | copy-start | bytes 5505028
  49.9 3.0 %copy-start.1 = (bf16[512,1792]{1,0:T(8,128)(2,1)}, bf16[512,1792]{1,0:T(8,128)(2,1)S(1)}, u32[]{:S(2)}) copy-start(bf16[512,1792]{1,0:T(8,128)(2,1)S(1)} %get-tuple-element.47.refs_9_.refs_11_.refs_4_) | copy-start | bytes 5505028
  50.0 5.7 %copy-start.13 = (bf16[512,512]{1,0:T(8,128)(2,1)S(1)}, bf16[512,512]{1,0:T(8,128)(2,1)}, u32[]{:S(2)}) copy-start(bf16[512,512]{1,0:T(8,128)(2,1)} %slice.38) | copy-start | bytes 1572868
  50.1 6.3 %copy-start.9 = (bf16[2,960,256]{2,1,0:T(8,128)(2,1)}, bf16[2,960,256]{2,1,0:T(8,128)(2,1)S(1)}, u32[]{:S(2)}) copy-start(bf16[2,960,256]{2,1,0:T(8,128)(2,1)S(1)} %collective-permute-done.5.refs_1_) | copy-start | bytes 2949124
  50.1 6.3 %copy-start.10 = (bf16[2,960,256]{2,1,0:T(8,128)(2,1)}, bf16[2,960,256]{2,1,0:T(8,128)(2,1)S(1)}, u32[]{:S(2)}) copy-start(bf16[2,960,256]{2,1,0:T(8,128)(2,1)S(1)} %collective-permute-done.4.refs_2_) | copy-start | bytes 2949124
  50.1 21.0 %collective-permute-start.8 = (bf16[256,1792]{1,0:T(8,128)(2,1)S(1)}, bf16[256,1792]{1,0:T(8,128)(2,1)S(1)}, u32[]{:S(2)}, u32[]{:S(2)}) collective-permute-start(bf16[256,1792]{1,0:T(8,128)(2,1)S(1)} %slice.36), channel_id=1, source_target_pairs={{0,16},{16,32},{32,48},{48,0},{1,17},{17,33},{33,49},{49,1},{2,18}... | collective-permute-start | bytes 2752520 | tf_op jit(solution)/shard_map/ppermute | solution.py:36
  50.2 20.9 %collective-permute-start.9 = (bf16[256,1792]{1,0:T(8,128)(2,1)S(1)}, bf16[256,1792]{1,0:T(8,128)(2,1)S(1)}, u32[]{:S(2)}, u32[]{:S(2)}) collective-permute-start(bf16[256,1792]{1,0:T(8,128)(2,1)S(1)} %slice.37), channel_id=1, source_target_pairs={{0,48},{16,0},{32,16},{48,32},{1,49},{17,1},{33,17},{49,33},{2,50}... | collective-permute-start | bytes 2752520 | tf_op jit(solution)/shard_map/ppermute | solution.py:36
  52.9 11.3 %collective-permute-start.6 = (bf16[960,256]{1,0:T(8,128)(2,1)S(1)}, bf16[960,256]{1,0:T(8,128)(2,1)S(1)}, u32[]{:S(2)}, u32[]{:S(2)}) collective-permute-start(bf16[960,256]{1,0:T(8,128)(2,1)S(1)} %slice_bitcast_fusion.1), channel_id=1, source_target_pairs={{0,4},{4,8},{8,12},{12,0},{1,5},{5,9},{9,13},{13,1},{2,6},{6,10},{... | collective-permute-start | bytes 1474568 | tf_op jit(solution)/shard_map/ppermute | solution.py:36
  54.2 10.0 %collective-permute-start.7 = (bf16[960,256]{1,0:T(8,128)(2,1)S(1)}, bf16[960,256]{1,0:T(8,128)(2,1)S(1)}, u32[]{:S(2)}, u32[]{:S(2)}) collective-permute-start(bf16[960,256]{1,0:T(8,128)(2,1)S(1)} %slice_bitcast_fusion), channel_id=1, source_target_pairs={{0,12},{4,0},{8,4},{12,8},{1,13},{5,1},{9,5},{13,9},{2,14},{6,2},{... | collective-permute-start | bytes 1474568 | tf_op jit(solution)/shard_map/ppermute | solution.py:36
  55.7 10.1 %collective-permute-start.10 = (bf16[512,512]{1,0:T(8,128)(2,1)S(1)}, bf16[512,512]{1,0:T(8,128)(2,1)S(1)}, u32[]{:S(2)}, u32[]{:S(2)}) collective-permute-start(bf16[512,512]{1,0:T(8,128)(2,1)S(1)} %copy-done.13), channel_id=1, source_target_pairs={{0,64},{64,0},{1,65},{65,1},{2,66},{66,2},{3,67},{67,3},{4,68},{68... | collective-permute-start | bytes 1572872 | tf_op jit(solution)/shard_map/ppermute | solution.py:36
  64.3 13.2 %copy-start.11 = (bf16[2,960,256]{2,1,0:T(8,128)(2,1)}, bf16[2,960,256]{2,1,0:T(8,128)(2,1)S(1)}, u32[]{:S(2)}) copy-start(bf16[2,960,256]{2,1,0:T(8,128)(2,1)S(1)} %pad_maximum_fusion.3.refs_3_) | copy-start | bytes 2949124
  65.8 8.5 %copy-start.7 = (bf16[512,512]{1,0:T(8,128)(2,1)}, bf16[512,512]{1,0:T(8,128)(2,1)S(1)}, u32[]{:S(2)}) copy-start(bf16[512,512]{1,0:T(8,128)(2,1)S(1)} %collective-permute-done.10.refs_11_.refs_13_.refs_6_) | copy-start | bytes 1572868
  71.1 10.5 %collective-permute-start.11 = (bf16[6,960,256]{2,1,0:T(8,128)(2,1)S(1)}, bf16[6,960,256]{2,1,0:T(8,128)(2,1)}, u32[]{:S(2)}, u32[]{:S(2)}) collective-permute-start(bf16[6,960,256]{2,1,0:T(8,128)(2,1)S(1)} %pad_maximum_fusion), channel_id=1, source_target_pairs={{0,1},{1,0},{2,3},{3,2},{4,5},{5,4},{6,7},{7,6},{8,9},{9,8},{10,11... | collective-permute-start | bytes 8847368 | tf_op jit(solution)/shard_map/ppermute | solution.py:36
  74.4 7.2 %copy-start.5 = (bf16[512,1280]{1,0:T(8,128)(2,1)}, bf16[512,1280]{1,0:T(8,128)(2,1)S(1)}, u32[]{:S(2)}) copy-start(bf16[512,1280]{1,0:T(8,128)(2,1)S(1)} %pad_maximum_fusion.1.refs_12_.refs_9_.refs_2_) | copy-start | bytes 3932164
  74.4 30.6 %collective-permute-start.15 = (bf16[512,1280]{1,0:T(8,128)(2,1)S(1)}, bf16[512,1280]{1,0:T(8,128)(2,1)}, u32[]{:S(2)}, u32[]{:S(2)}) collective-permute-start(bf16[512,1280]{1,0:T(8,128)(2,1)S(1)} %pad_maximum_fusion.1.refs_12_.refs_9_.refs_2_), channel_id=1, source_target_pairs={{0,64},{64,0},{1,65},{65,1},{2,66},{66,2},{3,67},{67,3},{4,68},{68... | collective-permute-start | bytes 3932168 | tf_op jit(solution)/shard_map/ppermute | solution.py:36
  74.8 30.9 %collective-permute-start.14 = (bf16[512,1280]{1,0:T(8,128)(2,1)}, bf16[512,1280]{1,0:T(8,128)(2,1)}, u32[]{:S(2)}, u32[]{:S(2)}) collective-permute-start(bf16[512,1280]{1,0:T(8,128)(2,1)} %mark.10.refs_10_.refs_12_.refs_5_), channel_id=1, source_target_pairs={{0,48},{16,0},{32,16},{48,32},{1,49},{17,1},{33,17},{49,33},{2,50}... | collective-permute-start | bytes 3932168 | tf_op jit(solution)/shard_map/ppermute | solution.py:36
  77.5 31.3 %collective-permute-start.13 = (bf16[512,1280]{1,0:T(8,128)(2,1)}, bf16[512,1280]{1,0:T(8,128)(2,1)}, u32[]{:S(2)}, u32[]{:S(2)}) collective-permute-start(bf16[512,1280]{1,0:T(8,128)(2,1)} %mark.10.refs_10_.refs_12_.refs_5_), channel_id=1, source_target_pairs={{0,16},{16,32},{32,48},{48,0},{1,17},{17,33},{33,49},{49,1},{2,18}... | collective-permute-start | bytes 3932168 | tf_op jit(solution)/shard_map/ppermute | solution.py:36
  77.5 3.0 %collective-permute-start.12 = (bf16[2,960,256]{2,1,0:T(8,128)(2,1)S(1)}, bf16[2,960,256]{2,1,0:T(8,128)(2,1)S(1)}, u32[]{:S(2)}, u32[]{:S(2)}) collective-permute-start(bf16[2,960,256]{2,1,0:T(8,128)(2,1)S(1)} %pad_maximum_fusion.3.refs_3_), channel_id=1, source_target_pairs={{0,1},{1,0},{2,3},{3,2},{4,5},{5,4},{6,7},{7,6},{8,9},{9,8},{10,11... | collective-permute-start | bytes 2949128 | tf_op jit(solution)/shard_map/ppermute | solution.py:36
  79.0 26.0 %copy-start.6 = (bf16[512,512]{1,0:T(8,128)(2,1)S(1)}, bf16[512,512]{1,0:T(8,128)(2,1)}, u32[]{:S(2)}) copy-start(bf16[512,512]{1,0:T(8,128)(2,1)} %pad_maximum_fusion.4.refs_13_.refs_10_.refs_3_) | copy-start | bytes 1572868
  80.6 1.0 copy-start.12
  100.2 20.7 %collective-permute-start.17 = (bf16[512,512]{1,0:T(8,128)(2,1)}, bf16[512,512]{1,0:T(8,128)(2,1)}, u32[]{:S(2)}, u32[]{:S(2)}) collective-permute-start(bf16[512,512]{1,0:T(8,128)(2,1)} %copy-done.7), channel_id=1, source_target_pairs={{0,16},{16,32},{32,48},{48,0},{1,17},{17,33},{33,49},{49,1},{2,18}... | collective-permute-start | bytes 1572872 | tf_op jit(solution)/shard_map/ppermute | solution.py:36
  100.3 20.6 %collective-permute-start.16 = (bf16[512,512]{1,0:T(8,128)(2,1)}, bf16[512,512]{1,0:T(8,128)(2,1)}, u32[]{:S(2)}, u32[]{:S(2)}) collective-permute-start(bf16[512,512]{1,0:T(8,128)(2,1)} %copy-done.7), channel_id=1, source_target_pairs={{0,48},{16,0},{32,16},{48,32},{1,49},{17,1},{33,17},{49,33},{2,50}... | collective-permute-start | bytes 1572872 | tf_op jit(solution)/shard_map/ppermute | solution.py:36
  105.0 16.0 %collective-permute-start.18 = (bf16[512,512]{1,0:T(8,128)(2,1)S(1)}, bf16[512,512]{1,0:T(8,128)(2,1)S(1)}, u32[]{:S(2)}, u32[]{:S(2)}) collective-permute-start(bf16[512,512]{1,0:T(8,128)(2,1)S(1)} %copy-done.6), channel_id=1, source_target_pairs={{0,64},{64,0},{1,65},{65,1},{2,66},{66,2},{3,67},{67,3},{4,68},{68... | collective-permute-start | bytes 1572872 | tf_op jit(solution)/shard_map/ppermute | solution.py:36
  120.9 0.8 copy-start.8
  133.6 4.9 %collective-permute-start.19 = (bf16[2,960,256]{2,1,0:T(8,128)(2,1)}, bf16[2,960,256]{2,1,0:T(8,128)(2,1)S(1)}, u32[]{:S(2)}, u32[]{:S(2)}) collective-permute-start(bf16[2,960,256]{2,1,0:T(8,128)(2,1)} %get-tuple-element.69), channel_id=1, source_target_pairs={{0,1},{1,0},{2,3},{3,2},{4,5},{5,4},{6,7},{7,6},{8,9},{9,8},{10,11... | collective-permute-start | bytes 2949128 | tf_op jit(solution)/shard_map/ppermute | solution.py:36
  140.1 13.7 %collective-permute-start.21 = (bf16[2,480,256]{2,1,0:T(8,128)(2,1)S(1)}, bf16[2,480,256]{2,1,0:T(8,128)(2,1)S(1)}, u32[]{:S(2)}, u32[]{:S(2)}) collective-permute-start(bf16[2,480,256]{2,1,0:T(8,128)(2,1)S(1)} %get-tuple-element.70), channel_id=1, source_target_pairs={{0,4},{4,8},{8,12},{12,0},{1,5},{5,9},{9,13},{13,1},{2,6},{6,10},{... | collective-permute-start | bytes 1474568 | tf_op jit(solution)/shard_map/ppermute | solution.py:36
  141.6 12.2 %collective-permute-start.22 = (bf16[2,480,256]{2,1,0:T(8,128)(2,1)S(1)}, bf16[2,480,256]{2,1,0:T(8,128)(2,1)S(1)}, u32[]{:S(2)}, u32[]{:S(2)}) collective-permute-start(bf16[2,480,256]{2,1,0:T(8,128)(2,1)S(1)} %get-tuple-element.71), channel_id=1, source_target_pairs={{0,12},{4,0},{8,4},{12,8},{1,13},{5,1},{9,5},{13,9},{2,14},{6,2},{... | collective-permute-start | bytes 1474568 | tf_op jit(solution)/shard_map/ppermute | solution.py:36
  149.9 3.8 %copy-start.4 = (bf16[2,960,256]{2,1,0:T(8,128)(2,1)S(1)}, bf16[2,960,256]{2,1,0:T(8,128)(2,1)}, u32[]{:S(2)}) copy-start(bf16[2,960,256]{2,1,0:T(8,128)(2,1)} %get-tuple-element.73.mine_ref) | copy-start | bytes 2949124
  150.0 3.8 %collective-permute-start.20 = (bf16[2,960,256]{2,1,0:T(8,128)(2,1)}, bf16[2,960,256]{2,1,0:T(8,128)(2,1)S(1)}, u32[]{:S(2)}, u32[]{:S(2)}) collective-permute-start(bf16[2,960,256]{2,1,0:T(8,128)(2,1)} %get-tuple-element.74), channel_id=1, source_target_pairs={{0,1},{1,0},{2,3},{3,2},{4,5},{5,4},{6,7},{7,6},{8,9},{9,8},{10,11... | collective-permute-start | bytes 2949128 | tf_op jit(solution)/shard_map/ppermute | solution.py:36
  155.1 14.5 %collective-permute-start.24 = (bf16[960,256]{1,0:T(8,128)(2,1)}, bf16[960,256]{1,0:T(8,128)(2,1)S(1)}, u32[]{:S(2)}, u32[]{:S(2)}) collective-permute-start(bf16[960,256]{1,0:T(8,128)(2,1)} %get-tuple-element.77), channel_id=1, source_target_pairs={{0,4},{4,8},{8,12},{12,0},{1,5},{5,9},{9,13},{13,1},{2,6},{6,10},{... | collective-permute-start | bytes 1474568 | tf_op jit(solution)/shard_map/ppermute | solution.py:36
  156.0 13.6 %collective-permute-start.25 = (bf16[960,256]{1,0:T(8,128)(2,1)}, bf16[960,256]{1,0:T(8,128)(2,1)S(1)}, u32[]{:S(2)}, u32[]{:S(2)}) collective-permute-start(bf16[960,256]{1,0:T(8,128)(2,1)} %get-tuple-element.78), channel_id=1, source_target_pairs={{0,12},{4,0},{8,4},{12,8},{1,13},{5,1},{9,5},{13,9},{2,14},{6,2},{... | collective-permute-start | bytes 1474568 | tf_op jit(solution)/shard_map/ppermute | solution.py:36
  167.5 5.2 %copy-start.3 = (bf16[3,960,256]{2,1,0:T(8,128)(2,1)S(1)}, bf16[3,960,256]{2,1,0:T(8,128)(2,1)}, u32[]{:S(2)}) copy-start(bf16[3,960,256]{2,1,0:T(8,128)(2,1)} %get-tuple-element.80.mine_ref) | copy-start | bytes 4423684
  167.5 5.2 %collective-permute-start.23 = (bf16[3,960,256]{2,1,0:T(8,128)(2,1)}, bf16[3,960,256]{2,1,0:T(8,128)(2,1)S(1)}, u32[]{:S(2)}, u32[]{:S(2)}) collective-permute-start(bf16[3,960,256]{2,1,0:T(8,128)(2,1)} %get-tuple-element.81), channel_id=1, source_target_pairs={{0,1},{1,0},{2,3},{3,2},{4,5},{5,4},{6,7},{7,6},{8,9},{9,8},{10,11... | collective-permute-start | bytes 4423688 | tf_op jit(solution)/shard_map/ppermute | solution.py:36
  174.4 14.2 %collective-permute-start.29 = (bf16[960,256]{1,0:T(8,128)(2,1)}, bf16[960,256]{1,0:T(8,128)(2,1)S(1)}, u32[]{:S(2)}, u32[]{:S(2)}) collective-permute-start(bf16[960,256]{1,0:T(8,128)(2,1)} %get-tuple-element.86), channel_id=1, source_target_pairs={{0,2},{2,0},{1,3},{3,1},{4,6},{6,4},{5,7},{7,5},{8,10},{10,8},{9,1... | collective-permute-start | bytes 1474568 | tf_op jit(solution)/shard_map/ppermute | solution.py:36
  175.4 13.5 %collective-permute-start.27 = (bf16[960,256]{1,0:T(8,128)(2,1)}, bf16[960,256]{1,0:T(8,128)(2,1)S(1)}, u32[]{:S(2)}, u32[]{:S(2)}) collective-permute-start(bf16[960,256]{1,0:T(8,128)(2,1)} %get-tuple-element.84), channel_id=1, source_target_pairs={{0,4},{4,8},{8,12},{12,0},{1,5},{5,9},{9,13},{13,1},{2,6},{6,10},{... | collective-permute-start | bytes 1474568 | tf_op jit(solution)/shard_map/ppermute | solution.py:36
  175.7 13.2 %collective-permute-start.28 = (bf16[960,256]{1,0:T(8,128)(2,1)}, bf16[960,256]{1,0:T(8,128)(2,1)S(1)}, u32[]{:S(2)}, u32[]{:S(2)}) collective-permute-start(bf16[960,256]{1,0:T(8,128)(2,1)} %get-tuple-element.85), channel_id=1, source_target_pairs={{0,12},{4,0},{8,4},{12,8},{1,13},{5,1},{9,5},{13,9},{2,14},{6,2},{... | collective-permute-start | bytes 1474568 | tf_op jit(solution)/shard_map/ppermute | solution.py:36
  183.1 5.8 %collective-permute-start.26 = (bf16[1,960,256]{2,1,0:T(8,128)(2,1)}, bf16[1,960,256]{2,1,0:T(8,128)(2,1)S(1)}, u32[]{:S(2)}, u32[]{:S(2)}) collective-permute-start(bf16[1,960,256]{2,1,0:T(8,128)(2,1)} %get-tuple-element.89), channel_id=1, source_target_pairs={{0,1},{1,0},{2,3},{3,2},{4,5},{5,4},{6,7},{7,6},{8,9},{9,8},{10,11... | collective-permute-start | bytes 1474568 | tf_op jit(solution)/shard_map/ppermute | solution.py:36
  188.5 1.0 copy-start.14

commit v6 on v5

--- a/solution.py
+++ b/solution.py
@@ -16,7 +16,7 @@
 F32, BF16 = jnp.float32, jnp.bfloat16
 VMEM_LIMIT = 62 * 2**20
 SMALL_LIMIT = 16 * 2**20
-PARTS = 2
+PARTS = 1
 CHUNKS = 2
 
 
@@ -28,7 +28,7 @@
 
 
 DEAR = flops(4 * 10**10)
-SOME = flops(2 * 10**10)
+SOME = flops(4 * 10**10)
 
 
 def shift(value, axis, by, size):

time: 191 us -> 191 us (level)
  no operation moved by 1% of the time
where the time goes in v6:
time: 191 us; the launch traced here: 190 us
  waiting for transfers between devices  69.4 us (36%)
  Pallas kernels  67.3 us (35%)
  starting transfers between devices  42.5 us (22%)
  local copies, waits for them, and re-layouts  6.19 us (3%)
  other arithmetic  4.01 us (2%)
    ppermute x30, waiting for transfers between devices, shift(): return lax.ppermute(value, axis, pairs)  69.4 us
    ppermute x30, starting transfers between devices, shift(): return lax.ppermute(value, axis, pairs)  42.5 us
    pallas_call x4, Pallas kernels, gradient(): pl.pallas_call(kernel, in_specs=[hbm] * (1 + n_last + len(arrays)), out_s...  33.8 us
    pallas_call x1, Pallas kernels, forward_early(): pl.pallas_call(kernel, grid=(width // LANES,), in_specs=[hbm] * n_p + [ti...  18.7 us
    pallas_call x1, Pallas kernels, forward_late(): pl.pallas_call(kernel, grid=(cols // LANES,), in_specs=[pl.BlockSpec((tok...  11.8 us
  transfers between devices with their start and end apart: 30, of which 16 were waited for; matrix products, arithmetic and copies ran while one was open for 3% of the time, Pallas kernels for 28%

profile of v6, /device:TPU:1, one launch (start us, length us, event | category | flops | bytes accessed | tf_op | source)
XLA Modules:
  0.0 190.4 jit_solution(5841768350463179690)
XLA Ops:
  0.6 3.8 %collective-permute-start = (bf16[960,256]{1,0:T(8,128)(2,1)}, bf16[960,256]{1,0:T(8,128)(2,1)S(1)}, u32[]{:S(2)}, u32[]{:S(2)}) collective-permute-start(bf16[960,256]{1,0:T(8,128)(2,1)} %param.5), channel_id=1, source_target_pairs={{0,2},{2,0},{1,3},{3,1},{4,6},{6,4},{5,7},{7,5},{8,10},{10,8},{9,1... | collective-permute-start | bytes 1474568 | tf_op jit(solution)/shard_map/ppermute | solution.py:36
  4.5 3.8 %collective-permute-start.2 = (bf16[512,1792]{1,0:T(8,128)(2,1)}, bf16[512,1792]{1,0:T(8,128)(2,1)S(1)}, u32[]{:S(2)}, u32[]{:S(2)}) collective-permute-start(bf16[512,1792]{1,0:T(8,128)(2,1)} %refs_0_.5), channel_id=1, source_target_pairs={{0,48},{16,0},{32,16},{48,32},{1,49},{17,1},{33,17},{49,33},{2,50}... | collective-permute-start | bytes 5505032 | tf_op jit(solution)/shard_map/ppermute | solution.py:36
  8.2 1.5 slice.39
  10.2 1.9 slice.38
  12.0 3.3 %collective-permute-done = bf16[960,256]{1,0:T(8,128)(2,1)S(1)} collective-permute-done((bf16[960,256]{1,0:T(8,128)(2,1)}, bf16[960,256]{1,0:T(8,128)(2,1)S(1)}, u32[]{:S(2)}, u32[]{:S(2)}) %collective-permute-start) | collective-permute-done | bytes 491552 | tf_op jit(solution)/shard_map/ppermute | solution.py:36
  15.5 2.6 %collective-permute-start.5 = (bf16[2,960,256]{2,1,0:T(8,128)(2,1)S(1)}, bf16[2,960,256]{2,1,0:T(8,128)(2,1)S(1)}, u32[]{:S(2)}, u32[]{:S(2)}) collective-permute-start(bf16[2,960,256]{2,1,0:T(8,128)(2,1)S(1)} %mark.8.refs_0_), channel_id=1, source_target_pairs={{0,12},{4,0},{8,4},{12,8},{1,13},{5,1},{9,5},{13,9},{2,14},{6,2},{... | collective-permute-start | bytes 2949128 | tf_op jit(solution)/shard_map/ppermute | solution.py:36
  18.0 25.9 %collective-permute-done.3.refs_0_ = bf16[512,1280]{1,0:T(8,128)(2,1)} collective-permute-done((bf16[512,1280]{1,0:T(8,128)(2,1)S(1)}, bf16[512,1280]{1,0:T(8,128)(2,1)}, u32[]{:S(2)}, u32[]{:S(2)}) %collective-permute-start.3) | collective-permute-done | bytes 1310752 | tf_op jit(solution)/shard_map/ppermute | solution.py:36
  43.9 3.0 %collective-permute-done.2.refs_1_ = bf16[512,1792]{1,0:T(8,128)(2,1)S(1)} collective-permute-done((bf16[512,1792]{1,0:T(8,128)(2,1)}, bf16[512,1792]{1,0:T(8,128)(2,1)S(1)}, u32[]{:S(2)}, u32[]{:S(2)}) %collective-permute-start.2) | collective-permute-done | bytes 1835040 | tf_op jit(solution)/shard_map/ppermute | solution.py:36
  46.9 3.0 %collective-permute-done.1.refs_0_ = bf16[512,1792]{1,0:T(8,128)(2,1)S(1)} collective-permute-done((bf16[512,1792]{1,0:T(8,128)(2,1)}, bf16[512,1792]{1,0:T(8,128)(2,1)S(1)}, u32[]{:S(2)}, u32[]{:S(2)}) %collective-permute-start.1) | collective-permute-done | bytes 1835040 | tf_op jit(solution)/shard_map/ppermute | solution.py:36
  50.2 2.7 %collective-permute-start.9 = (bf16[256,1792]{1,0:T(8,128)(2,1)S(1)}, bf16[256,1792]{1,0:T(8,128)(2,1)S(1)}, u32[]{:S(2)}, u32[]{:S(2)}) collective-permute-start(bf16[256,1792]{1,0:T(8,128)(2,1)S(1)} %slice.37), channel_id=1, source_target_pairs={{0,48},{16,0},{32,16},{48,32},{1,49},{17,1},{33,17},{49,33},{2,50}... | collective-permute-start | bytes 2752520 | tf_op jit(solution)/shard_map/ppermute | solution.py:36
  52.9 1.3 collective-permute-start.6
  54.2 1.5 collective-permute-start.7
  56.4 7.8 %collective-permute-done.6 = bf16[960,256]{1,0:T(8,128)(2,1)S(1)} collective-permute-done((bf16[960,256]{1,0:T(8,128)(2,1)S(1)}, bf16[960,256]{1,0:T(8,128)(2,1)S(1)}, u32[]{:S(2)}, u32[]{:S(2)}) %collective-permute-start.6) | collective-permute-done | bytes 491552 | tf_op jit(solution)/shard_map/ppermute | solution.py:36
  64.3 1.5 collective-permute-done.10.refs_11_.refs_13_.refs_6_
  65.8 5.2 %collective-permute-done.8 = bf16[256,1792]{1,0:T(8,128)(2,1)S(1)} collective-permute-done((bf16[256,1792]{1,0:T(8,128)(2,1)S(1)}, bf16[256,1792]{1,0:T(8,128)(2,1)S(1)}, u32[]{:S(2)}, u32[]{:S(2)}) %collective-permute-start.8) | collective-permute-done | bytes 917536 | tf_op jit(solution)/shard_map/ppermute | solution.py:36
  71.1 3.1 %collective-permute-start.11 = (bf16[6,960,256]{2,1,0:T(8,128)(2,1)S(1)}, bf16[6,960,256]{2,1,0:T(8,128)(2,1)}, u32[]{:S(2)}, u32[]{:S(2)}) collective-permute-start(bf16[6,960,256]{2,1,0:T(8,128)(2,1)S(1)} %pad_maximum_fusion), channel_id=1, source_target_pairs={{0,1},{1,0},{2,3},{3,2},{4,5},{5,4},{6,7},{7,6},{8,9},{9,8},{10,11... | collective-permute-start | bytes 8847368 | tf_op jit(solution)/shard_map/ppermute | solution.py:36
  74.8 2.7 %collective-permute-start.14 = (bf16[512,1280]{1,0:T(8,128)(2,1)}, bf16[512,1280]{1,0:T(8,128)(2,1)}, u32[]{:S(2)}, u32[]{:S(2)}) collective-permute-start(bf16[512,1280]{1,0:T(8,128)(2,1)} %mark.10.refs_10_.refs_12_.refs_5_), channel_id=1, source_target_pairs={{0,48},{16,0},{32,16},{48,32},{1,49},{17,1},{33,17},{49,33},{2,50}... | collective-permute-start | bytes 3932168 | tf_op jit(solution)/shard_map/ppermute | solution.py:36
  78.1 0.8 pad_maximum_fusion.4.refs_13_.refs_10_.refs_3_
  79.0 1.6 collective-permute-done.12.refs_5_
  80.6 1.0 copy-done.12
  81.5 18.7 %early.1 = (f32[960,1792]{1,0:T(8,128)}, bf16[960,1536]{1,0:T(8,128)(2,1)}) custom-call(bf16[2,960,256]{2,1,0:T(8,128)(2,1)} %copy-done.2, bf16[2,960,256]{2,1,0:T(8,128)(2,1)} %copy-done.9, bf16[2,960,256]{2,1,0:T(8,128)(2,1)} %copy-done.10, bf16[2,960,256]{2,1,0:T(8,128)(2,1)} %copy-done.11, bf16[6,960,256]{2,1,0:T(8,128)(2,1)} %collective-permute-done.11.refs_4_, ...), custom_call_target="tpu_custom_call" | custom-call | flops 1000 | bytes 1000 | tf_op jit(solution)/shard_map/early/pallas_call | solution.py:130
  100.3 2.7 %collective-permute-start.16 = (bf16[512,512]{1,0:T(8,128)(2,1)}, bf16[512,512]{1,0:T(8,128)(2,1)}, u32[]{:S(2)}, u32[]{:S(2)}) collective-permute-start(bf16[512,512]{1,0:T(8,128)(2,1)} %copy-done.7), channel_id=1, source_target_pairs={{0,48},{16,0},{32,16},{48,32},{1,49},{17,1},{33,17},{49,33},{2,50}... | collective-permute-start | bytes 1572872 | tf_op jit(solution)/shard_map/ppermute | solution.py:36
  103.1 1.9 collective-permute-done.15.refs_2_.refs_16_.refs_9_
  105.7 3.1 %collective-permute-done.13.refs_0_ = bf16[512,1280]{1,0:T(8,128)(2,1)} collective-permute-done((bf16[512,1280]{1,0:T(8,128)(2,1)}, bf16[512,1280]{1,0:T(8,128)(2,1)}, u32[]{:S(2)}, u32[]{:S(2)}) %collective-permute-start.13) | collective-permute-done | bytes 1310752 | tf_op jit(solution)/shard_map/ppermute | solution.py:36
  108.8 11.8 %gelu_a.1 = (bf16[960,1792]{1,0:T(8,128)(2,1)}, bf16[960,1792]{1,0:T(8,128)(2,1)}) custom-call(bf16[960,1536]{1,0:T(8,128)(2,1)} %get-tuple-element.57.x_ref.refs_0_, f32[960,1792]{1,0:T(8,128)} %get-tuple-element.58.start_ref.refs_1_, bf16[960,1792]{1,0:T(8,128)(2,1)} %refs_2_.1, bf16[512,1280]{1,0:T(8,128)(2,1)} %get-tuple-element.60.refs_0_.refs_14_.refs_7_, ...), custom_call_target="tpu_custom_call" | custom-call | flops 1000 | bytes 1000 | tf_op jit(solution)/shard_map/gelu_a/pallas_call | solution.py:170
  120.7 0.8 copy-done.8
  121.5 11.8 %grad_far.1 = (bf16[2,960,256]{2,1,0:T(8,128)(2,1)}, bf16[2,960,256]{2,1,0:T(8,128)(2,1)}, bf16[960,1792]{1,0:T(8,128)(2,1)}, bf16[960,1792]{1,0:T(8,128)(2,1)}) custom-call(bf16[960,1792]{1,0:T(8,128)(2,1)} %get-tuple-element.62.s_hbm, bf16[960,1536]{1,0:T(8,128)(2,1)} %get-tuple-element.57.x_ref.refs_0_, ...), custom_call_target="tpu_custom_call", output_to_operand_aliasing={{2}: (0, {}), {3}: (7, {})} | custom-call | flops 1000 | bytes 1000 | tf_op jit(solution)/shard_map/grad_far/pallas_call | solution.py:312
  133.3 2.5 %collective-permute-start.19 = (bf16[2,960,256]{2,1,0:T(8,128)(2,1)}, bf16[2,960,256]{2,1,0:T(8,128)(2,1)S(1)}, u32[]{:S(2)}, u32[]{:S(2)}) collective-permute-start(bf16[2,960,256]{2,1,0:T(8,128)(2,1)} %get-tuple-element.69), channel_id=1, source_target_pairs={{0,1},{1,0},{2,3},{3,2},{4,5},{5,4},{6,7},{7,6},{8,9},{9,8},{10,11... | collective-permute-start | bytes 2949128 | tf_op jit(solution)/shard_map/ppermute | solution.py:36
  135.9 2.4 %collective-permute-done.19 = bf16[2,960,256]{2,1,0:T(8,128)(2,1)S(1)} collective-permute-done((bf16[2,960,256]{2,1,0:T(8,128)(2,1)}, bf16[2,960,256]{2,1,0:T(8,128)(2,1)S(1)}, u32[]{:S(2)}, u32[]{:S(2)}) %collective-permute-start.19) | collective-permute-done | bytes 983072 | tf_op jit(solution)/shard_map/ppermute | solution.py:36
  138.3 1.5 add_convert_fusion
  139.8 1.5 collective-permute-start.21
  141.3 1.2 collective-permute-start.22
  142.5 7.1 %grad_1.1 = (bf16[2,960,256]{2,1,0:T(8,128)(2,1)}, bf16[2,960,256]{2,1,0:T(8,128)(2,1)}) custom-call(bf16[960,1792]{1,0:T(8,128)(2,1)} %get-tuple-element.87.s_hbm, bf16[512,1792]{1,0:T(8,128)(2,1)} %refs_0_.5, bf16[512,1792]{1,0:T(8,128)(2,1)} %copy-done, bf16[512,1280]{1,0:T(8,128)(2,1)} %copy-done.5, ...), custom_call_target="tpu_custom_call" | custom-call | flops 1000 | bytes 1000 | tf_op jit(solution)/shard_map/grad_1/pallas_call | solution.py:312
  149.7 1.0 collective-permute-start.20
  150.7 2.8 %collective-permute-done.21.refs_0_ = bf16[2,480,256]{2,1,0:T(8,128)(2,1)S(1)} collective-permute-done((bf16[2,480,256]{2,1,0:T(8,128)(2,1)S(1)}, bf16[2,480,256]{2,1,0:T(8,128)(2,1)S(1)}, u32[]{:S(2)}, u32[]{:S(2)}) %collective-permute-start.21) | collective-permute-done | bytes 491552 | tf_op jit(solution)/shard_map/ppermute | solution.py:36
  153.5 1.3 add_1.1
  154.8 0.9 collective-permute-start.24
  155.7 1.8 collective-permute-start.25
  157.5 9.7 %grad_0.1 = (bf16[3,960,256]{2,1,0:T(8,128)(2,1)}, bf16[3,960,256]{2,1,0:T(8,128)(2,1)}) custom-call(bf16[960,1792]{1,0:T(8,128)(2,1)} %get-tuple-element.87.s_hbm, bf16[512,1792]{1,0:T(8,128)(2,1)} %refs_0_.5, bf16[512,1792]{1,0:T(8,128)(2,1)} %copy-done, bf16[512,1280]{1,0:T(8,128)(2,1)} %copy-done.5, ...), custom_call_target="tpu_custom_call" | custom-call | flops 1000 | bytes 1000 | tf_op jit(solution)/shard_map/grad_0/pallas_call | solution.py:312
  167.3 2.1 %collective-permute-start.23 = (bf16[3,960,256]{2,1,0:T(8,128)(2,1)}, bf16[3,960,256]{2,1,0:T(8,128)(2,1)S(1)}, u32[]{:S(2)}, u32[]{:S(2)}) collective-permute-start(bf16[3,960,256]{2,1,0:T(8,128)(2,1)} %get-tuple-element.81), channel_id=1, source_target_pairs={{0,1},{1,0},{2,3},{3,2},{4,5},{5,4},{6,7},{7,6},{8,9},{9,8},{10,11... | collective-permute-start | bytes 4423688 | tf_op jit(solution)/shard_map/ppermute | solution.py:36
  169.3 3.1 %collective-permute-done.23.back_ref = bf16[3,960,256]{2,1,0:T(8,128)(2,1)S(1)} collective-permute-done((bf16[3,960,256]{2,1,0:T(8,128)(2,1)}, bf16[3,960,256]{2,1,0:T(8,128)(2,1)S(1)}, u32[]{:S(2)}, u32[]{:S(2)}) %collective-permute-start.23) | collective-permute-done | bytes 1474592 | tf_op jit(solution)/shard_map/ppermute | solution.py:36
  172.4 1.7 add_0.1
  174.1 1.0 collective-permute-start.29
  175.4 2.3 %collective-permute-start.28 = (bf16[960,256]{1,0:T(8,128)(2,1)}, bf16[960,256]{1,0:T(8,128)(2,1)S(1)}, u32[]{:S(2)}, u32[]{:S(2)}) collective-permute-start(bf16[960,256]{1,0:T(8,128)(2,1)} %get-tuple-element.85), channel_id=1, source_target_pairs={{0,12},{4,0},{8,4},{12,8},{1,13},{5,1},{9,5},{13,9},{2,14},{6,2},{... | collective-permute-start | bytes 1474568 | tf_op jit(solution)/shard_map/ppermute | solution.py:36
  177.8 5.1 %grad_own.1 = (bf16[1,960,256]{2,1,0:T(8,128)(2,1)}, bf16[1,960,256]{2,1,0:T(8,128)(2,1)}) custom-call(bf16[960,1792]{1,0:T(8,128)(2,1)} %get-tuple-element.87.s_hbm, bf16[512,1792]{1,0:T(8,128)(2,1)} %refs_0_.5, bf16[512,1792]{1,0:T(8,128)(2,1)} %copy-done, bf16[512,1280]{1,0:T(8,128)(2,1)} %copy-done.5, ...), custom_call_target="tpu_custom_call" | custom-call | flops 1000 | bytes 1000 | tf_op jit(solution)/shard_map/grad_own/pallas_call | solution.py:312
  182.9 1.3 collective-permute-start.26
  184.2 4.1 %collective-permute-done.29.refs_0_ = bf16[960,256]{1,0:T(8,128)(2,1)S(1)} collective-permute-done((bf16[960,256]{1,0:T(8,128)(2,1)}, bf16[960,256]{1,0:T(8,128)(2,1)S(1)}, u32[]{:S(2)}, u32[]{:S(2)}) %collective-permute-start.29) | collective-permute-done | bytes 491552 | tf_op jit(solution)/shard_map/ppermute | solution.py:36
  189.3 1.1 fusion.2
  (78 shorter events, 5.3 us)
Async XLA Ops:
  0.6 14.7 %copy-start.15 = (bf16[960,256]{1,0:T(8,128)(2,1)S(1)}, bf16[960,256]{1,0:T(8,128)(2,1)}, u32[]{:S(2)}) copy-start(bf16[960,256]{1,0:T(8,128)(2,1)} %param.5) | copy-start | bytes 1474564
  0.6 14.7 %collective-permute-start = (bf16[960,256]{1,0:T(8,128)(2,1)}, bf16[960,256]{1,0:T(8,128)(2,1)S(1)}, u32[]{:S(2)}, u32[]{:S(2)}) collective-permute-start(bf16[960,256]{1,0:T(8,128)(2,1)} %param.5), channel_id=1, source_target_pairs={{0,2},{2,0},{1,3},{3,1},{4,6},{6,4},{5,7},{7,5},{8,10},{10,8},{9,1... | collective-permute-start | bytes 1474568 | tf_op jit(solution)/shard_map/ppermute | solution.py:36
  4.5 42.4 %collective-permute-start.2 = (bf16[512,1792]{1,0:T(8,128)(2,1)}, bf16[512,1792]{1,0:T(8,128)(2,1)S(1)}, u32[]{:S(2)}, u32[]{:S(2)}) collective-permute-start(bf16[512,1792]{1,0:T(8,128)(2,1)} %refs_0_.5), channel_id=1, source_target_pairs={{0,48},{16,0},{32,16},{48,32},{1,49},{17,1},{33,17},{49,33},{2,50}... | collective-permute-start | bytes 5505032 | tf_op jit(solution)/shard_map/ppermute | solution.py:36
  8.2 41.7 %collective-permute-start.1 = (bf16[512,1792]{1,0:T(8,128)(2,1)}, bf16[512,1792]{1,0:T(8,128)(2,1)S(1)}, u32[]{:S(2)}, u32[]{:S(2)}) collective-permute-start(bf16[512,1792]{1,0:T(8,128)(2,1)} %refs_0_.5), channel_id=1, source_target_pairs={{0,16},{16,32},{32,48},{48,0},{1,17},{17,33},{33,49},{49,1},{2,18}... | collective-permute-start | bytes 5505032 | tf_op jit(solution)/shard_map/ppermute | solution.py:36
  9.7 34.2 %collective-permute-start.3 = (bf16[512,1280]{1,0:T(8,128)(2,1)S(1)}, bf16[512,1280]{1,0:T(8,128)(2,1)}, u32[]{:S(2)}, u32[]{:S(2)}) collective-permute-start(bf16[512,1280]{1,0:T(8,128)(2,1)S(1)} %slice.39), channel_id=1, source_target_pairs={{0,64},{64,0},{1,65},{65,1},{2,66},{66,2},{3,67},{67,3},{4,68},{68... | collective-permute-start | bytes 3932168 | tf_op jit(solution)/shard_map/ppermute | solution.py:36
  15.4 40.6 %copy-start.2 = (bf16[2,960,256]{2,1,0:T(8,128)(2,1)}, bf16[2,960,256]{2,1,0:T(8,128)(2,1)S(1)}, u32[]{:S(2)}) copy-start(bf16[2,960,256]{2,1,0:T(8,128)(2,1)S(1)} %mark.8.refs_0_) | copy-start | bytes 2949124
  15.5 34.6 %collective-permute-start.5 = (bf16[2,960,256]{2,1,0:T(8,128)(2,1)S(1)}, bf16[2,960,256]{2,1,0:T(8,128)(2,1)S(1)}, u32[]{:S(2)}, u32[]{:S(2)}) collective-permute-start(bf16[2,960,256]{2,1,0:T(8,128)(2,1)S(1)} %mark.8.refs_0_), channel_id=1, source_target_pairs={{0,12},{4,0},{8,4},{12,8},{1,13},{5,1},{9,5},{13,9},{2,14},{6,2},{... | collective-permute-start | bytes 2949128 | tf_op jit(solution)/shard_map/ppermute | solution.py:36
  18.0 32.1 %collective-permute-start.4 = (bf16[2,960,256]{2,1,0:T(8,128)(2,1)S(1)}, bf16[2,960,256]{2,1,0:T(8,128)(2,1)S(1)}, u32[]{:S(2)}, u32[]{:S(2)}) collective-permute-start(bf16[2,960,256]{2,1,0:T(8,128)(2,1)S(1)} %mark.8.refs_0_), channel_id=1, source_target_pairs={{0,4},{4,8},{8,12},{12,0},{1,5},{5,9},{9,13},{13,1},{2,6},{6,10},{... | collective-permute-start | bytes 2949128 | tf_op jit(solution)/shard_map/ppermute | solution.py:36
  49.9 3.0 %copy-start = (bf16[512,1792]{1,0:T(8,128)(2,1)}, bf16[512,1792]{1,0:T(8,128)(2,1)S(1)}, u32[]{:S(2)}) copy-start(bf16[512,1792]{1,0:T(8,128)(2,1)S(1)} %get-tuple-element.48.refs_8_.refs_1_) | copy-start | bytes 5505028
  49.9 3.0 %copy-start.1 = (bf16[512,1792]{1,0:T(8,128)(2,1)}, bf16[512,1792]{1,0:T(8,128)(2,1)S(1)}, u32[]{:S(2)}) copy-start(bf16[512,1792]{1,0:T(8,128)(2,1)S(1)} %get-tuple-element.47.refs_9_.refs_11_.refs_4_) | copy-start | bytes 5505028
  50.0 5.7 %copy-start.13 = (bf16[512,512]{1,0:T(8,128)(2,1)S(1)}, bf16[512,512]{1,0:T(8,128)(2,1)}, u32[]{:S(2)}) copy-start(bf16[512,512]{1,0:T(8,128)(2,1)} %slice.38) | copy-start | bytes 1572868
  50.1 6.3 %copy-start.9 = (bf16[2,960,256]{2,1,0:T(8,128)(2,1)}, bf16[2,960,256]{2,1,0:T(8,128)(2,1)S(1)}, u32[]{:S(2)}) copy-start(bf16[2,960,256]{2,1,0:T(8,128)(2,1)S(1)} %collective-permute-done.5.refs_1_) | copy-start | bytes 2949124
  50.1 6.3 %copy-start.10 = (bf16[2,960,256]{2,1,0:T(8,128)(2,1)}, bf16[2,960,256]{2,1,0:T(8,128)(2,1)S(1)}, u32[]{:S(2)}) copy-start(bf16[2,960,256]{2,1,0:T(8,128)(2,1)S(1)} %collective-permute-done.4.refs_2_) | copy-start | bytes 2949124
  50.1 21.0 %collective-permute-start.8 = (bf16[256,1792]{1,0:T(8,128)(2,1)S(1)}, bf16[256,1792]{1,0:T(8,128)(2,1)S(1)}, u32[]{:S(2)}, u32[]{:S(2)}) collective-permute-start(bf16[256,1792]{1,0:T(8,128)(2,1)S(1)} %slice.36), channel_id=1, source_target_pairs={{0,16},{16,32},{32,48},{48,0},{1,17},{17,33},{33,49},{49,1},{2,18}... | collective-permute-start | bytes 2752520 | tf_op jit(solution)/shard_map/ppermute | solution.py:36
  50.2 20.9 %collective-permute-start.9 = (bf16[256,1792]{1,0:T(8,128)(2,1)S(1)}, bf16[256,1792]{1,0:T(8,128)(2,1)S(1)}, u32[]{:S(2)}, u32[]{:S(2)}) collective-permute-start(bf16[256,1792]{1,0:T(8,128)(2,1)S(1)} %slice.37), channel_id=1, source_target_pairs={{0,48},{16,0},{32,16},{48,32},{1,49},{17,1},{33,17},{49,33},{2,50}... | collective-permute-start | bytes 2752520 | tf_op jit(solution)/shard_map/ppermute | solution.py:36
  52.9 11.3 %collective-permute-start.6 = (bf16[960,256]{1,0:T(8,128)(2,1)S(1)}, bf16[960,256]{1,0:T(8,128)(2,1)S(1)}, u32[]{:S(2)}, u32[]{:S(2)}) collective-permute-start(bf16[960,256]{1,0:T(8,128)(2,1)S(1)} %slice_bitcast_fusion.1), channel_id=1, source_target_pairs={{0,4},{4,8},{8,12},{12,0},{1,5},{5,9},{9,13},{13,1},{2,6},{6,10},{... | collective-permute-start | bytes 1474568 | tf_op jit(solution)/shard_map/ppermute | solution.py:36
  54.2 10.0 %collective-permute-start.7 = (bf16[960,256]{1,0:T(8,128)(2,1)S(1)}, bf16[960,256]{1,0:T(8,128)(2,1)S(1)}, u32[]{:S(2)}, u32[]{:S(2)}) collective-permute-start(bf16[960,256]{1,0:T(8,128)(2,1)S(1)} %slice_bitcast_fusion), channel_id=1, source_target_pairs={{0,12},{4,0},{8,4},{12,8},{1,13},{5,1},{9,5},{13,9},{2,14},{6,2},{... | collective-permute-start | bytes 1474568 | tf_op jit(solution)/shard_map/ppermute | solution.py:36
  55.7 10.1 %collective-permute-start.10 = (bf16[512,512]{1,0:T(8,128)(2,1)S(1)}, bf16[512,512]{1,0:T(8,128)(2,1)S(1)}, u32[]{:S(2)}, u32[]{:S(2)}) collective-permute-start(bf16[512,512]{1,0:T(8,128)(2,1)S(1)} %copy-done.13), channel_id=1, source_target_pairs={{0,64},{64,0},{1,65},{65,1},{2,66},{66,2},{3,67},{67,3},{4,68},{68... | collective-permute-start | bytes 1572872 | tf_op jit(solution)/shard_map/ppermute | solution.py:36
  64.3 13.2 %copy-start.11 = (bf16[2,960,256]{2,1,0:T(8,128)(2,1)}, bf16[2,960,256]{2,1,0:T(8,128)(2,1)S(1)}, u32[]{:S(2)}) copy-start(bf16[2,960,256]{2,1,0:T(8,128)(2,1)S(1)} %pad_maximum_fusion.3.refs_3_) | copy-start | bytes 2949124
  65.8 8.5 %copy-start.7 = (bf16[512,512]{1,0:T(8,128)(2,1)}, bf16[512,512]{1,0:T(8,128)(2,1)S(1)}, u32[]{:S(2)}) copy-start(bf16[512,512]{1,0:T(8,128)(2,1)S(1)} %collective-permute-done.10.refs_11_.refs_13_.refs_6_) | copy-start | bytes 1572868
  71.1 10.5 %collective-permute-start.11 = (bf16[6,960,256]{2,1,0:T(8,128)(2,1)S(1)}, bf16[6,960,256]{2,1,0:T(8,128)(2,1)}, u32[]{:S(2)}, u32[]{:S(2)}) collective-permute-start(bf16[6,960,256]{2,1,0:T(8,128)(2,1)S(1)} %pad_maximum_fusion), channel_id=1, source_target_pairs={{0,1},{1,0},{2,3},{3,2},{4,5},{5,4},{6,7},{7,6},{8,9},{9,8},{10,11... | collective-permute-start | bytes 8847368 | tf_op jit(solution)/shard_map/ppermute | solution.py:36
  74.4 7.2 %copy-start.5 = (bf16[512,1280]{1,0:T(8,128)(2,1)}, bf16[512,1280]{1,0:T(8,128)(2,1)S(1)}, u32[]{:S(2)}) copy-start(bf16[512,1280]{1,0:T(8,128)(2,1)S(1)} %pad_maximum_fusion.1.refs_12_.refs_9_.refs_2_) | copy-start | bytes 3932164
  74.4 30.6 %collective-permute-start.15 = (bf16[512,1280]{1,0:T(8,128)(2,1)S(1)}, bf16[512,1280]{1,0:T(8,128)(2,1)}, u32[]{:S(2)}, u32[]{:S(2)}) collective-permute-start(bf16[512,1280]{1,0:T(8,128)(2,1)S(1)} %pad_maximum_fusion.1.refs_12_.refs_9_.refs_2_), channel_id=1, source_target_pairs={{0,64},{64,0},{1,65},{65,1},{2,66},{66,2},{3,67},{67,3},{4,68},{68... | collective-permute-start | bytes 3932168 | tf_op jit(solution)/shard_map/ppermute | solution.py:36
  74.8 30.9 %collective-permute-start.14 = (bf16[512,1280]{1,0:T(8,128)(2,1)}, bf16[512,1280]{1,0:T(8,128)(2,1)}, u32[]{:S(2)}, u32[]{:S(2)}) collective-permute-start(bf16[512,1280]{1,0:T(8,128)(2,1)} %mark.10.refs_10_.refs_12_.refs_5_), channel_id=1, source_target_pairs={{0,48},{16,0},{32,16},{48,32},{1,49},{17,1},{33,17},{49,33},{2,50}... | collective-permute-start | bytes 3932168 | tf_op jit(solution)/shard_map/ppermute | solution.py:36
  77.5 31.3 %collective-permute-start.13 = (bf16[512,1280]{1,0:T(8,128)(2,1)}, bf16[512,1280]{1,0:T(8,128)(2,1)}, u32[]{:S(2)}, u32[]{:S(2)}) collective-permute-start(bf16[512,1280]{1,0:T(8,128)(2,1)} %mark.10.refs_10_.refs_12_.refs_5_), channel_id=1, source_target_pairs={{0,16},{16,32},{32,48},{48,0},{1,17},{17,33},{33,49},{49,1},{2,18}... | collective-permute-start | bytes 3932168 | tf_op jit(solution)/shard_map/ppermute | solution.py:36
  77.5 3.0 %collective-permute-start.12 = (bf16[2,960,256]{2,1,0:T(8,128)(2,1)S(1)}, bf16[2,960,256]{2,1,0:T(8,128)(2,1)S(1)}, u32[]{:S(2)}, u32[]{:S(2)}) collective-permute-start(bf16[2,960,256]{2,1,0:T(8,128)(2,1)S(1)} %pad_maximum_fusion.3.refs_3_), channel_id=1, source_target_pairs={{0,1},{1,0},{2,3},{3,2},{4,5},{5,4},{6,7},{7,6},{8,9},{9,8},{10,11... | collective-permute-start | bytes 2949128 | tf_op jit(solution)/shard_map/ppermute | solution.py:36
  79.0 26.0 %copy-start.6 = (bf16[512,512]{1,0:T(8,128)(2,1)S(1)}, bf16[512,512]{1,0:T(8,128)(2,1)}, u32[]{:S(2)}) copy-start(bf16[512,512]{1,0:T(8,128)(2,1)} %pad_maximum_fusion.4.refs_13_.refs_10_.refs_3_) | copy-start | bytes 1572868
  80.6 1.0 copy-start.12
  100.2 20.4 %collective-permute-start.17 = (bf16[512,512]{1,0:T(8,128)(2,1)}, bf16[512,512]{1,0:T(8,128)(2,1)}, u32[]{:S(2)}, u32[]{:S(2)}) collective-permute-start(bf16[512,512]{1,0:T(8,128)(2,1)} %copy-done.7), channel_id=1, source_target_pairs={{0,16},{16,32},{32,48},{48,0},{1,17},{17,33},{33,49},{49,1},{2,18}... | collective-permute-start | bytes 1572872 | tf_op jit(solution)/shard_map/ppermute | solution.py:36
  100.3 20.3 %collective-permute-start.16 = (bf16[512,512]{1,0:T(8,128)(2,1)}, bf16[512,512]{1,0:T(8,128)(2,1)}, u32[]{:S(2)}, u32[]{:S(2)}) collective-permute-start(bf16[512,512]{1,0:T(8,128)(2,1)} %copy-done.7), channel_id=1, source_target_pairs={{0,48},{16,0},{32,16},{48,32},{1,49},{17,1},{33,17},{49,33},{2,50}... | collective-permute-start | bytes 1572872 | tf_op jit(solution)/shard_map/ppermute | solution.py:36
  105.0 15.7 %collective-permute-start.18 = (bf16[512,512]{1,0:T(8,128)(2,1)S(1)}, bf16[512,512]{1,0:T(8,128)(2,1)S(1)}, u32[]{:S(2)}, u32[]{:S(2)}) collective-permute-start(bf16[512,512]{1,0:T(8,128)(2,1)S(1)} %copy-done.6), channel_id=1, source_target_pairs={{0,64},{64,0},{1,65},{65,1},{2,66},{66,2},{3,67},{67,3},{4,68},{68... | collective-permute-start | bytes 1572872 | tf_op jit(solution)/shard_map/ppermute | solution.py:36
  120.7 0.8 copy-start.8
  133.3 4.9 %collective-permute-start.19 = (bf16[2,960,256]{2,1,0:T(8,128)(2,1)}, bf16[2,960,256]{2,1,0:T(8,128)(2,1)S(1)}, u32[]{:S(2)}, u32[]{:S(2)}) collective-permute-start(bf16[2,960,256]{2,1,0:T(8,128)(2,1)} %get-tuple-element.69), channel_id=1, source_target_pairs={{0,1},{1,0},{2,3},{3,2},{4,5},{5,4},{6,7},{7,6},{8,9},{9,8},{10,11... | collective-permute-start | bytes 2949128 | tf_op jit(solution)/shard_map/ppermute | solution.py:36
  139.8 13.7 %collective-permute-start.21 = (bf16[2,480,256]{2,1,0:T(8,128)(2,1)S(1)}, bf16[2,480,256]{2,1,0:T(8,128)(2,1)S(1)}, u32[]{:S(2)}, u32[]{:S(2)}) collective-permute-start(bf16[2,480,256]{2,1,0:T(8,128)(2,1)S(1)} %get-tuple-element.70), channel_id=1, source_target_pairs={{0,4},{4,8},{8,12},{12,0},{1,5},{5,9},{9,13},{13,1},{2,6},{6,10},{... | collective-permute-start | bytes 1474568 | tf_op jit(solution)/shard_map/ppermute | solution.py:36
  141.3 12.2 %collective-permute-start.22 = (bf16[2,480,256]{2,1,0:T(8,128)(2,1)S(1)}, bf16[2,480,256]{2,1,0:T(8,128)(2,1)S(1)}, u32[]{:S(2)}, u32[]{:S(2)}) collective-permute-start(bf16[2,480,256]{2,1,0:T(8,128)(2,1)S(1)} %get-tuple-element.71), channel_id=1, source_target_pairs={{0,12},{4,0},{8,4},{12,8},{1,13},{5,1},{9,5},{13,9},{2,14},{6,2},{... | collective-permute-start | bytes 1474568 | tf_op jit(solution)/shard_map/ppermute | solution.py:36
  149.7 3.8 %copy-start.4 = (bf16[2,960,256]{2,1,0:T(8,128)(2,1)S(1)}, bf16[2,960,256]{2,1,0:T(8,128)(2,1)}, u32[]{:S(2)}) copy-start(bf16[2,960,256]{2,1,0:T(8,128)(2,1)} %get-tuple-element.73.mine_ref) | copy-start | bytes 2949124
  149.7 3.8 %collective-permute-start.20 = (bf16[2,960,256]{2,1,0:T(8,128)(2,1)}, bf16[2,960,256]{2,1,0:T(8,128)(2,1)S(1)}, u32[]{:S(2)}, u32[]{:S(2)}) collective-permute-start(bf16[2,960,256]{2,1,0:T(8,128)(2,1)} %get-tuple-element.74), channel_id=1, source_target_pairs={{0,1},{1,0},{2,3},{3,2},{4,5},{5,4},{6,7},{7,6},{8,9},{9,8},{10,11... | collective-permute-start | bytes 2949128 | tf_op jit(solution)/shard_map/ppermute | solution.py:36
  154.8 14.5 %collective-permute-start.24 = (bf16[960,256]{1,0:T(8,128)(2,1)}, bf16[960,256]{1,0:T(8,128)(2,1)S(1)}, u32[]{:S(2)}, u32[]{:S(2)}) collective-permute-start(bf16[960,256]{1,0:T(8,128)(2,1)} %get-tuple-element.77), channel_id=1, source_target_pairs={{0,4},{4,8},{8,12},{12,0},{1,5},{5,9},{9,13},{13,1},{2,6},{6,10},{... | collective-permute-start | bytes 1474568 | tf_op jit(solution)/shard_map/ppermute | solution.py:36
  155.7 13.6 %collective-permute-start.25 = (bf16[960,256]{1,0:T(8,128)(2,1)}, bf16[960,256]{1,0:T(8,128)(2,1)S(1)}, u32[]{:S(2)}, u32[]{:S(2)}) collective-permute-start(bf16[960,256]{1,0:T(8,128)(2,1)} %get-tuple-element.78), channel_id=1, source_target_pairs={{0,12},{4,0},{8,4},{12,8},{1,13},{5,1},{9,5},{13,9},{2,14},{6,2},{... | collective-permute-start | bytes 1474568 | tf_op jit(solution)/shard_map/ppermute | solution.py:36
  167.2 5.2 %copy-start.3 = (bf16[3,960,256]{2,1,0:T(8,128)(2,1)S(1)}, bf16[3,960,256]{2,1,0:T(8,128)(2,1)}, u32[]{:S(2)}) copy-start(bf16[3,960,256]{2,1,0:T(8,128)(2,1)} %get-tuple-element.80.mine_ref) | copy-start | bytes 4423684
  167.3 5.2 %collective-permute-start.23 = (bf16[3,960,256]{2,1,0:T(8,128)(2,1)}, bf16[3,960,256]{2,1,0:T(8,128)(2,1)S(1)}, u32[]{:S(2)}, u32[]{:S(2)}) collective-permute-start(bf16[3,960,256]{2,1,0:T(8,128)(2,1)} %get-tuple-element.81), channel_id=1, source_target_pairs={{0,1},{1,0},{2,3},{3,2},{4,5},{5,4},{6,7},{7,6},{8,9},{9,8},{10,11... | collective-permute-start | bytes 4423688 | tf_op jit(solution)/shard_map/ppermute | solution.py:36
  174.1 14.2 %collective-permute-start.29 = (bf16[960,256]{1,0:T(8,128)(2,1)}, bf16[960,256]{1,0:T(8,128)(2,1)S(1)}, u32[]{:S(2)}, u32[]{:S(2)}) collective-permute-start(bf16[960,256]{1,0:T(8,128)(2,1)} %get-tuple-element.86), channel_id=1, source_target_pairs={{0,2},{2,0},{1,3},{3,1},{4,6},{6,4},{5,7},{7,5},{8,10},{10,8},{9,1... | collective-permute-start | bytes 1474568 | tf_op jit(solution)/shard_map/ppermute | solution.py:36
  175.1 13.5 %collective-permute-start.27 = (bf16[960,256]{1,0:T(8,128)(2,1)}, bf16[960,256]{1,0:T(8,128)(2,1)S(1)}, u32[]{:S(2)}, u32[]{:S(2)}) collective-permute-start(bf16[960,256]{1,0:T(8,128)(2,1)} %get-tuple-element.84), channel_id=1, source_target_pairs={{0,4},{4,8},{8,12},{12,0},{1,5},{5,9},{9,13},{13,1},{2,6},{6,10},{... | collective-permute-start | bytes 1474568 | tf_op jit(solution)/shard_map/ppermute | solution.py:36
  175.4 13.2 %collective-permute-start.28 = (bf16[960,256]{1,0:T(8,128)(2,1)}, bf16[960,256]{1,0:T(8,128)(2,1)S(1)}, u32[]{:S(2)}, u32[]{:S(2)}) collective-permute-start(bf16[960,256]{1,0:T(8,128)(2,1)} %get-tuple-element.85), channel_id=1, source_target_pairs={{0,12},{4,0},{8,4},{12,8},{1,13},{5,1},{9,5},{13,9},{2,14},{6,2},{... | collective-permute-start | bytes 1474568 | tf_op jit(solution)/shard_map/ppermute | solution.py:36
  182.9 5.8 %collective-permute-start.26 = (bf16[1,960,256]{2,1,0:T(8,128)(2,1)}, bf16[1,960,256]{2,1,0:T(8,128)(2,1)S(1)}, u32[]{:S(2)}, u32[]{:S(2)}) collective-permute-start(bf16[1,960,256]{2,1,0:T(8,128)(2,1)} %get-tuple-element.89), channel_id=1, source_target_pairs={{0,1},{1,0},{2,3},{3,2},{4,5},{5,4},{6,7},{7,6},{8,9},{9,8},{10,11... | collective-permute-start | bytes 1474568 | tf_op jit(solution)/shard_map/ppermute | solution.py:36
  188.3 1.0 copy-start.14
